TPU v7x, 32 devices: a whole 2x2x4 slice. The times are simulated.
32 devices in a mesh: fsdp: 4 (over z), ctx: 4 (over x, core), tp: 2 (over y).
Axes of the slice: x: 2, y: 2, z: 4, core: 2. Of those that a mesh axis runs over, the one named last changes fastest.
Arguments:
- hidden_in: bfloat16 [8, 1024, 1024], P('fsdp', 'ctx'), may hold values from -6 to 6
- encoder_states: bfloat16 [8, 512, 1024], P('fsdp', 'ctx'), may hold values from -6 to 6
- dec_segments: int32 [8, 1024], P('fsdp'), may hold values from 0 to 7, as said below
- enc_segments: int32 [8, 512], P('fsdp'), may hold values from 0 to 7, as said below
- bucket_table: int32 [1024], replicated, may hold values from 0 to 31, as said below
- out_cotangent: bfloat16 [8, 1024, 1024], P('fsdp', 'ctx'), may hold values from -6 to 6
- self_gain: bfloat16 [1024], P('fsdp'), may hold values from 0.25 to 1.75
- self_query: bfloat16 [1024, 1024], P('fsdp', 'tp'), may hold values from -0.0234375 to 0.0234375
- self_key: bfloat16 [1024, 1024], P('fsdp', 'tp'), may hold values from -0.1875 to 0.1875
- self_value: bfloat16 [1024, 1024], P('fsdp', 'tp'), may hold values from -0.1875 to 0.1875
- self_output: bfloat16 [1024, 1024], P('tp', 'fsdp'), may hold values from -1 to 1
- position_bias: bfloat16 [32, 16], P('fsdp', 'tp'), may hold values from -4 to 4
- cross_gain: bfloat16 [1024], P('fsdp'), may hold values from 0.25 to 1.75
- cross_query: bfloat16 [1024, 1024], P('fsdp', 'tp'), may hold values from -0.0234375 to 0.0234375
- cross_key: bfloat16 [1024, 1024], P('fsdp', 'tp'), may hold values from -0.1875 to 0.1875
- cross_value: bfloat16 [1024, 1024], P('fsdp', 'tp'), may hold values from -0.1875 to 0.1875
- cross_output: bfloat16 [1024, 1024], P('tp', 'fsdp'), may hold values from -1 to 1
- ffn_gain: bfloat16 [1024], P('fsdp'), may hold values from 0.25 to 1.75
- ffn_gate: bfloat16 [1024, 2816], P('fsdp', 'tp'), may hold values from -0.1875 to 0.1875
- ffn_up: bfloat16 [1024, 2816], P('fsdp', 'tp'), may hold values from -0.1875 to 0.1875
- ffn_down: bfloat16 [2816, 1024], P('tp', 'fsdp'), may hold values from -0.15625 to 0.15625
Outputs:
- layer_output: bfloat16 [8, 1024, 1024], P('fsdp', 'ctx')
- grad_hidden: bfloat16 [8, 1024, 1024], P('fsdp', 'ctx')
- grad_encoder: bfloat16 [8, 512, 1024], P('fsdp', 'ctx')
- grad_self_gain: float32 [1024], P('fsdp')
- grad_self_query: float32 [1024, 1024], P('fsdp', 'tp')
- grad_self_key: float32 [1024, 1024], P('fsdp', 'tp')
- grad_self_value: float32 [1024, 1024], P('fsdp', 'tp')
- grad_self_output: float32 [1024, 1024], P('tp', 'fsdp')
- grad_position_bias: float32 [32, 16], P('fsdp', 'tp')
- grad_cross_gain: float32 [1024], P('fsdp')
- grad_cross_query: float32 [1024, 1024], P('fsdp', 'tp')
- grad_cross_key: float32 [1024, 1024], P('fsdp', 'tp')
- grad_cross_value: float32 [1024, 1024], P('fsdp', 'tp')
- grad_cross_output: float32 [1024, 1024], P('tp', 'fsdp')
- grad_ffn_gain: float32 [1024], P('fsdp')
- grad_ffn_gate: float32 [1024, 2816], P('fsdp', 'tp')
- grad_ffn_up: float32 [1024, 2816], P('fsdp', 'tp')
- grad_ffn_down: float32 [2816, 1024], P('tp', 'fsdp')
Inputs may be any that keep to these rules, and one draw needn't show every extreme that they name: `dec_segments`: each row gives the document of every decoder position of a sequence: 0 at the first position, never falling, rising by at most one from a position to the next. In each aligned block of 2 rows, one row's last document begins before position 128. `enc_segments`: each row gives the document of every encoder position of the same sequence: 0 at the first position, never falling, rising by at most one at a time, and with the same last number as the decoder row, so that every decoder document has encoder positions. `bucket_table`: entry d is the bucket of a key d positions before its query; 0 at d = 0, never falling.
All inputs are finite; a program needn't handle non-finite values.
Results may differ from a plain program's by a relative error of at most 0.033.
Values may be sent and summed in bfloat16 or wider, within the bound.
No kernel may reach another device: no remote copies, remote signals or barrier semaphores. Data moves between devices by JAX's collectives and lax.ppermute only.
A program may use at most 192 MiB of HBM per device.

v0:
```python
import jax
import jax.numpy as jnp
from jax import lax
from jax.sharding import PartitionSpec as P

EPSILON = 1e-06
NEGATIVE = -1e30


def project(input_rows, weight_matrix):
    return jnp.einsum("myv,vc->myc", input_rows, weight_matrix, preferred_element_type=jnp.float32)


def project_back(gradient_list, weight_matrix):
    return jnp.einsum(
        "fyb,cb->fyc", gradient_list, weight_matrix, preferred_element_type=jnp.float32
    )


def weight_grad(input_rows, gradient_list):
    return jnp.einsum("yzl,yzc->lc", input_rows, gradient_list, preferred_element_type=jnp.float32)


def gelu_tanh(values):
    return jax.nn.gelu(values, approximate=True)


def split_heads(tensor, head_count):
    return tensor.reshape(tensor.shape[0], tensor.shape[1], head_count, -1)


def combine_heads(tensor):
    return tensor.reshape(tensor.shape[0], tensor.shape[1], -1)


def rms_forward(values, gain_row):
    inverse_rms = lax.rsqrt(jnp.mean(values * values, axis=-1, keepdims=True) + EPSILON)
    unit_rows = values * inverse_rms
    return (unit_rows, inverse_rms, unit_rows * gain_row)


def rms_backward(grad_normed, unit_rows, inverse_rms, gain_row):
    grad_unit = grad_normed * gain_row
    grad_gain = jnp.sum(grad_normed * unit_rows, axis=(0, 1))
    inner_sum = jnp.mean(grad_unit * unit_rows, axis=-1, keepdims=True)
    return (inverse_rms * (grad_unit - unit_rows * inner_sum), grad_gain)


def toeplitz_rows(lookup, offset, row_count):
    head_count, length = lookup.shape
    extent = row_count + length
    backward = jnp.flip(lookup, axis=1)
    padding = jnp.zeros((head_count, extent), lookup.dtype)
    padded = jnp.concatenate([padding, backward, padding], axis=1)
    edge_row = lax.dynamic_slice_in_dim(padded, 2 * length - 1 - offset, extent, 1)
    shifted = jnp.roll(edge_row, -row_count, axis=1)
    repeated = jnp.broadcast_to(shifted[:, None, :], (head_count, row_count, extent)).reshape(
        head_count, row_count * extent
    )
    skewed = repeated[:, : row_count * (extent - 1)].reshape(head_count, row_count, extent - 1)
    return skewed[:, :, :length]


def diagonal_sums(grid_vals, offset):
    head_count, row_count, length = grid_vals.shape
    extent = row_count + length
    widened = jnp.concatenate(
        [grid_vals, jnp.zeros((head_count, row_count, row_count - 1), grid_vals.dtype)], axis=2
    )
    flattened = widened.reshape(head_count, row_count * (extent - 1))
    flattened = jnp.concatenate(
        [flattened, jnp.zeros((head_count, row_count), grid_vals.dtype)], axis=1
    )
    columns = jnp.sum(flattened.reshape(head_count, row_count, extent), axis=1)
    centred = jnp.roll(columns, row_count, axis=1)
    backward = jnp.flip(centred, axis=1)
    padded = jnp.concatenate([backward, jnp.zeros((head_count, length), grid_vals.dtype)], axis=1)
    return lax.dynamic_slice_in_dim(padded, length - 1 - offset, length, 1)


def masked_scores(query_seq, key_seq, score_bias, visible):
    scores = (
        jnp.einsum("qhe,khe->hqk", query_seq, key_seq, preferred_element_type=jnp.float32)
        + score_bias
    )
    return jnp.where(visible[None], scores, NEGATIVE)


def attend_forward(query_seq, key_seq, value_seq, score_bias, visible):
    scores = masked_scores(query_seq, key_seq, score_bias, visible)
    highest = jnp.max(scores, axis=-1, keepdims=True)
    denominator = jnp.sum(jnp.exp(scores - highest), axis=-1, keepdims=True)
    logsum = highest + jnp.log(denominator)
    weights_low = jnp.exp(scores - logsum).astype(jnp.bfloat16)
    attended = jnp.einsum(
        "hqk,khe->qhe", weights_low, value_seq, preferred_element_type=jnp.float32
    )
    return (attended.astype(jnp.bfloat16), logsum)


def attend_backward(query_seq, key_seq, value_seq, score_bias, visible, logsum, grad_seq):
    scores = masked_scores(query_seq, key_seq, score_bias, visible)
    weights = jnp.exp(scores - logsum)
    weights_low = weights.astype(jnp.bfloat16)
    grad_values = jnp.einsum(
        "hqk,qhe->khe", weights_low, grad_seq, preferred_element_type=jnp.float32
    )
    grad_weights = jnp.einsum(
        "qhe,khe->hqk", grad_seq, value_seq, preferred_element_type=jnp.float32
    )
    inner_sum = jnp.sum(grad_weights * weights, axis=-1, keepdims=True)
    grad_scores = (weights * (grad_weights - inner_sum)).astype(jnp.bfloat16)
    grad_queries = jnp.einsum(
        "hqk,khe->qhe", grad_scores, key_seq, preferred_element_type=jnp.float32
    ).astype(jnp.bfloat16)
    grad_keys = jnp.einsum(
        "hqk,qhe->khe", grad_scores, query_seq, preferred_element_type=jnp.float32
    )
    return (grad_queries, grad_keys, grad_values, grad_scores)


def attend_sequences(query_all, key_all, value_all, score_bias, visible_all):

    def single(slices):
        return attend_forward(slices[0], slices[1], slices[2], score_bias, slices[3])

    return lax.map(single, (query_all, key_all, value_all, visible_all))


def attend_sequences_back(
    query_all, key_all, value_all, score_bias, visible_all, logsum_all, grad_all, keep_scores
):
    if keep_scores:
        starting = jnp.zeros(
            (query_all.shape[2], query_all.shape[1], key_all.shape[1]), jnp.float32
        )
    else:
        starting = jnp.zeros((), jnp.float32)

    def single(running, slices):
        grad_queries, grad_keys, grad_values, grad_scores = attend_backward(
            slices[0], slices[1], slices[2], score_bias, slices[3], slices[4], slices[5]
        )
        if keep_scores:
            running = running + grad_scores.astype(jnp.float32)
        return (running, (grad_queries, grad_keys, grad_values))

    running, (grad_queries, grad_keys, grad_values) = lax.scan(
        single, starting, (query_all, key_all, value_all, visible_all, logsum_all, grad_all)
    )
    return (grad_queries, grad_keys, grad_values, running)


def branch_total(partial_value):
    return lax.psum(partial_value.astype(jnp.bfloat16), "tp").astype(jnp.float32)


def backward_total(partial_value):
    return lax.psum(partial_value.astype(jnp.bfloat16), "tp").astype(jnp.float32)


def body(
    hidden_in,
    encoder_states,
    dec_segments,
    enc_segments,
    bucket_table,
    out_cotangent,
    self_gain,
    self_query,
    self_key,
    self_value,
    self_output,
    position_bias,
    cross_gain,
    cross_query,
    cross_key,
    cross_value,
    cross_output,
    ffn_gain,
    ffn_gate,
    ffn_up,
    ffn_down,
):
    gathered = (
        lax.all_gather(self_gain, "fsdp", axis=0, tiled=True),
        lax.all_gather(self_query, "fsdp", axis=0, tiled=True),
        lax.all_gather(self_key, "fsdp", axis=0, tiled=True),
        lax.all_gather(self_value, "fsdp", axis=0, tiled=True),
        lax.all_gather(self_output, "fsdp", axis=1, tiled=True),
        lax.all_gather(position_bias, "fsdp", axis=0, tiled=True),
        lax.all_gather(cross_gain, "fsdp", axis=0, tiled=True),
        lax.all_gather(cross_query, "fsdp", axis=0, tiled=True),
        lax.all_gather(cross_key, "fsdp", axis=0, tiled=True),
        lax.all_gather(cross_value, "fsdp", axis=0, tiled=True),
        lax.all_gather(cross_output, "fsdp", axis=1, tiled=True),
        lax.all_gather(ffn_gain, "fsdp", axis=0, tiled=True),
        lax.all_gather(ffn_gate, "fsdp", axis=0, tiled=True),
        lax.all_gather(ffn_up, "fsdp", axis=0, tiled=True),
        lax.all_gather(ffn_down, "fsdp", axis=1, tiled=True),
    )
    (
        gain_self,
        query_self,
        key_self,
        self_value_weight,
        output_self,
        bias_table,
        gain_cross,
        query_cross,
        key_cross,
        value_cross,
        output_cross,
        gain_ffn,
        gate_ffn,
        up_ffn,
        down_ffn,
    ) = gathered
    seq_count, row_count, width = hidden_in.shape
    length = dec_segments.shape[1]
    bucket_count, head_count = bias_table.shape
    offset = lax.axis_index("ctx") * row_count
    query_places = offset + jnp.arange(row_count, dtype=jnp.int32)
    key_places = jnp.arange(length, dtype=jnp.int32)
    query_docs = lax.dynamic_slice_in_dim(dec_segments, offset, row_count, 1)
    self_visible = (query_places[:, None] >= key_places[None, :])[None] & (
        query_docs[:, :, None] == dec_segments[:, None, :]
    )
    cross_visible = query_docs[:, :, None] == enc_segments[:, None, :]
    bucket_onehot = (
        bucket_table[:, None] == jnp.arange(bucket_count, dtype=jnp.int32)[None, :]
    ).astype(jnp.float32)
    distance_bias = jnp.dot(
        bucket_onehot, bias_table.astype(jnp.float32), precision=lax.Precision.HIGHEST
    )
    score_bias = toeplitz_rows(distance_bias.T, offset, row_count)
    source = hidden_in.astype(jnp.float32)
    unit_one, inverse_one, normed = rms_forward(source, gain_self.astype(jnp.float32))
    normed_one = normed.astype(jnp.bfloat16)
    queries_one = project(normed_one, query_self).astype(jnp.bfloat16)
    keys_part = project(normed_one, key_self).astype(jnp.bfloat16)
    values_part = project(normed_one, self_value_weight).astype(jnp.bfloat16)
    keys_one, values_one = (
        lax.all_gather(keys_part, "ctx", axis=1, tiled=True),
        lax.all_gather(values_part, "ctx", axis=1, tiled=True),
    )
    query_heads_one = split_heads(queries_one, head_count)
    key_heads_one = split_heads(keys_one, head_count)
    value_heads_one = split_heads(values_one, head_count)
    attended_one, logsum_one = attend_sequences(
        query_heads_one, key_heads_one, value_heads_one, score_bias, self_visible
    )
    attended_one = combine_heads(attended_one)
    after_one = source + branch_total(project(attended_one, output_self))
    unit_two, inverse_two, normed = rms_forward(after_one, gain_cross.astype(jnp.float32))
    normed_two = normed.astype(jnp.bfloat16)
    queries_two = project(normed_two, query_cross).astype(jnp.bfloat16)
    enc_keys_part = project(encoder_states, key_cross).astype(jnp.bfloat16)
    enc_values_part = project(encoder_states, value_cross).astype(jnp.bfloat16)
    keys_two, values_two = (
        lax.all_gather(enc_keys_part, "ctx", axis=1, tiled=True),
        lax.all_gather(enc_values_part, "ctx", axis=1, tiled=True),
    )
    query_heads_two = split_heads(queries_two, head_count)
    key_heads_two = split_heads(keys_two, head_count)
    value_heads_two = split_heads(values_two, head_count)
    attended_two, logsum_two = attend_sequences(
        query_heads_two, key_heads_two, value_heads_two, 0.0, cross_visible
    )
    attended_two = combine_heads(attended_two)
    after_two = after_one + branch_total(project(attended_two, output_cross))
    unit_three, inverse_three, normed = rms_forward(after_two, gain_ffn.astype(jnp.float32))
    normed_three = normed.astype(jnp.bfloat16)
    gate_rows = project(normed_three, gate_ffn)
    up_rows = project(normed_three, up_ffn)
    activated, gelu_pull = jax.vjp(gelu_tanh, gate_rows)
    hidden_units = (activated * up_rows).astype(jnp.bfloat16)
    layer_output = after_two + branch_total(project(hidden_units, down_ffn))
    grad_res = out_cotangent.astype(jnp.float32)
    grad_down = weight_grad(hidden_units, out_cotangent)
    grad_units = project_back(out_cotangent, down_ffn)
    grad_gate_rows = gelu_pull(grad_units * up_rows)[0].astype(jnp.bfloat16)
    grad_up_rows = (grad_units * activated).astype(jnp.bfloat16)
    grad_gate = weight_grad(normed_three, grad_gate_rows)
    grad_up = weight_grad(normed_three, grad_up_rows)
    grad_normed = backward_total(
        project_back(grad_gate_rows, gate_ffn) + project_back(grad_up_rows, up_ffn)
    )
    grad_from, grad_gain_ffn = rms_backward(
        grad_normed, unit_three, inverse_three, gain_ffn.astype(jnp.float32)
    )
    grad_res = grad_res + grad_from
    grad_low = grad_res.astype(jnp.bfloat16)
    grad_out_cross = weight_grad(attended_two, grad_low)
    grad_attended = project_back(grad_low, output_cross).astype(jnp.bfloat16)
    grad_q_two, grad_k_two, grad_v_two, unused_total = attend_sequences_back(
        query_heads_two,
        key_heads_two,
        value_heads_two,
        0.0,
        cross_visible,
        logsum_two,
        split_heads(grad_attended, head_count),
        False,
    )
    grad_keys_two, grad_values_two = (
        lax.psum_scatter(
            combine_heads(grad_k_two).astype(jnp.bfloat16), "ctx", scatter_dimension=1, tiled=True
        ).astype(jnp.float32),
        lax.psum_scatter(
            combine_heads(grad_v_two).astype(jnp.bfloat16), "ctx", scatter_dimension=1, tiled=True
        ).astype(jnp.float32),
    )
    grad_keys_two = grad_keys_two.astype(jnp.bfloat16)
    grad_values_two = grad_values_two.astype(jnp.bfloat16)
    grad_queries_two = combine_heads(grad_q_two)
    grad_query_cross = weight_grad(normed_two, grad_queries_two)
    grad_key_cross = weight_grad(encoder_states, grad_keys_two)
    grad_value_cross = weight_grad(encoder_states, grad_values_two)
    grad_normed, grad_states = (
        lax.psum(project_back(grad_queries_two, query_cross).astype(jnp.bfloat16), "tp").astype(
            jnp.float32
        ),
        lax.psum(
            (
                project_back(grad_keys_two, key_cross) + project_back(grad_values_two, value_cross)
            ).astype(jnp.bfloat16),
            "tp",
        ).astype(jnp.float32),
    )
    grad_from, grad_gain_cross = rms_backward(
        grad_normed, unit_two, inverse_two, gain_cross.astype(jnp.float32)
    )
    grad_res = grad_res + grad_from
    grad_low = grad_res.astype(jnp.bfloat16)
    grad_out_self = weight_grad(attended_one, grad_low)
    grad_attended = project_back(grad_low, output_self).astype(jnp.bfloat16)
    grad_q_one, grad_k_one, grad_v_one, score_total = attend_sequences_back(
        query_heads_one,
        key_heads_one,
        value_heads_one,
        score_bias,
        self_visible,
        logsum_one,
        split_heads(grad_attended, head_count),
        True,
    )
    grad_keys_one, grad_values_one = (
        lax.psum_scatter(
            combine_heads(grad_k_one).astype(jnp.bfloat16), "ctx", scatter_dimension=1, tiled=True
        ).astype(jnp.float32),
        lax.psum_scatter(
            combine_heads(grad_v_one).astype(jnp.bfloat16), "ctx", scatter_dimension=1, tiled=True
        ).astype(jnp.float32),
    )
    grad_keys_one = grad_keys_one.astype(jnp.bfloat16)
    grad_values_one = grad_values_one.astype(jnp.bfloat16)
    grad_queries_one = combine_heads(grad_q_one)
    grad_query_self = weight_grad(normed_one, grad_queries_one)
    grad_key_self = weight_grad(normed_one, grad_keys_one)
    grad_value_self = weight_grad(normed_one, grad_values_one)
    grad_bias = jnp.dot(
        bucket_onehot.T, diagonal_sums(score_total, offset).T, precision=lax.Precision.HIGHEST
    )
    grad_normed = backward_total(
        project_back(grad_queries_one, query_self)
        + project_back(grad_keys_one, key_self)
        + project_back(grad_values_one, self_value_weight)
    )
    grad_from, grad_gain_self = rms_backward(
        grad_normed, unit_one, inverse_one, gain_self.astype(jnp.float32)
    )
    grad_input = (grad_res + grad_from).astype(jnp.bfloat16)
    shard_sums = (
        lax.psum_scatter(
            grad_gain_self.astype(jnp.bfloat16), "fsdp", scatter_dimension=0, tiled=True
        ).astype(jnp.float32),
        lax.psum_scatter(
            grad_query_self.astype(jnp.bfloat16), "fsdp", scatter_dimension=0, tiled=True
        ).astype(jnp.float32),
        lax.psum_scatter(
            grad_key_self.astype(jnp.bfloat16), "fsdp", scatter_dimension=0, tiled=True
        ).astype(jnp.float32),
        lax.psum_scatter(
            grad_value_self.astype(jnp.bfloat16), "fsdp", scatter_dimension=0, tiled=True
        ).astype(jnp.float32),
        lax.psum_scatter(
            grad_out_self.astype(jnp.bfloat16), "fsdp", scatter_dimension=1, tiled=True
        ).astype(jnp.float32),
        lax.psum_scatter(
            grad_bias.astype(jnp.bfloat16), "fsdp", scatter_dimension=0, tiled=True
        ).astype(jnp.float32),
        lax.psum_scatter(
            grad_gain_cross.astype(jnp.bfloat16), "fsdp", scatter_dimension=0, tiled=True
        ).astype(jnp.float32),
        lax.psum_scatter(
            grad_query_cross.astype(jnp.bfloat16), "fsdp", scatter_dimension=0, tiled=True
        ).astype(jnp.float32),
        lax.psum_scatter(
            grad_key_cross.astype(jnp.bfloat16), "fsdp", scatter_dimension=0, tiled=True
        ).astype(jnp.float32),
        lax.psum_scatter(
            grad_value_cross.astype(jnp.bfloat16), "fsdp", scatter_dimension=0, tiled=True
        ).astype(jnp.float32),
        lax.psum_scatter(
            grad_out_cross.astype(jnp.bfloat16), "fsdp", scatter_dimension=1, tiled=True
        ).astype(jnp.float32),
        lax.psum_scatter(
            grad_gain_ffn.astype(jnp.bfloat16), "fsdp", scatter_dimension=0, tiled=True
        ).astype(jnp.float32),
        lax.psum_scatter(
            grad_gate.astype(jnp.bfloat16), "fsdp", scatter_dimension=0, tiled=True
        ).astype(jnp.float32),
        lax.psum_scatter(
            grad_up.astype(jnp.bfloat16), "fsdp", scatter_dimension=0, tiled=True
        ).astype(jnp.float32),
        lax.psum_scatter(
            grad_down.astype(jnp.bfloat16), "fsdp", scatter_dimension=1, tiled=True
        ).astype(jnp.float32),
    )
    totals = (
        lax.psum(shard_sums[0].astype(jnp.bfloat16), "ctx").astype(jnp.float32),
        lax.psum(shard_sums[1].astype(jnp.bfloat16), "ctx").astype(jnp.float32),
        lax.psum(shard_sums[2].astype(jnp.bfloat16), "ctx").astype(jnp.float32),
        lax.psum(shard_sums[3].astype(jnp.bfloat16), "ctx").astype(jnp.float32),
        lax.psum(shard_sums[4].astype(jnp.bfloat16), "ctx").astype(jnp.float32),
        lax.psum(shard_sums[5].astype(jnp.bfloat16), "ctx").astype(jnp.float32),
        lax.psum(shard_sums[6].astype(jnp.bfloat16), "ctx").astype(jnp.float32),
        lax.psum(shard_sums[7].astype(jnp.bfloat16), "ctx").astype(jnp.float32),
        lax.psum(shard_sums[8].astype(jnp.bfloat16), "ctx").astype(jnp.float32),
        lax.psum(shard_sums[9].astype(jnp.bfloat16), "ctx").astype(jnp.float32),
        lax.psum(shard_sums[10].astype(jnp.bfloat16), "ctx").astype(jnp.float32),
        lax.psum(shard_sums[11].astype(jnp.bfloat16), "ctx").astype(jnp.float32),
        lax.psum(shard_sums[12].astype(jnp.bfloat16), "ctx").astype(jnp.float32),
        lax.psum(shard_sums[13].astype(jnp.bfloat16), "ctx").astype(jnp.float32),
        lax.psum(shard_sums[14].astype(jnp.bfloat16), "ctx").astype(jnp.float32),
    )
    return (
        layer_output.astype(jnp.bfloat16),
        grad_input,
        grad_states.astype(jnp.bfloat16),
        totals[0],
        totals[1],
        totals[2],
        totals[3],
        totals[4],
        totals[5],
        totals[6],
        totals[7],
        totals[8],
        totals[9],
        totals[10],
        totals[11],
        totals[12],
        totals[13],
        totals[14],
    )


def solution(mesh):
    in_specs = (
        P("fsdp", "ctx", None),
        P("fsdp", "ctx", None),
        P("fsdp", None),
        P("fsdp", None),
        P(),
        P("fsdp", "ctx", None),
        P("fsdp"),
        P("fsdp", "tp"),
        P("fsdp", "tp"),
        P("fsdp", "tp"),
        P("tp", "fsdp"),
        P("fsdp", "tp"),
        P("fsdp"),
        P("fsdp", "tp"),
        P("fsdp", "tp"),
        P("fsdp", "tp"),
        P("tp", "fsdp"),
        P("fsdp"),
        P("fsdp", "tp"),
        P("fsdp", "tp"),
        P("tp", "fsdp"),
    )
    out_specs = (
        P("fsdp", "ctx", None),
        P("fsdp", "ctx", None),
        P("fsdp", "ctx", None),
        P("fsdp"),
        P("fsdp", "tp"),
        P("fsdp", "tp"),
        P("fsdp", "tp"),
        P("tp", "fsdp"),
        P("fsdp", "tp"),
        P("fsdp"),
        P("fsdp", "tp"),
        P("fsdp", "tp"),
        P("fsdp", "tp"),
        P("tp", "fsdp"),
        P("fsdp"),
        P("fsdp", "tp"),
        P("fsdp", "tp"),
        P("tp", "fsdp"),
    )
    return jax.shard_map(body, mesh=mesh, in_specs=in_specs, out_specs=out_specs, check_vma=False)
```

profile of v0, /device:TPU:0, one launch (start us, length us, event | category | flops | bytes accessed | tf_op | source)
XLA Modules:
  0.0 1455.8 jit_solution(8457974438053589937)
XLA Ops:
  25.6 14.8 %all-gather.19.cloned.1.call-done = bf16[1024,512]{1,0:T(8,128)(2,1)} async-done(((bf16[256,512]{1,0:T(8,128)(2,1)}), bf16[1024,512]{1,0:T(8,128)(2,1)}) %all-gather.19.cloned.1.call-update) | async-done | bytes 1048592 | tf_op jit(solution)/shard_map/all_gather | solution.py:189
  43.2 26.1 %all-gather.25.cloned.1.call-done = bf16[1024,512]{1,0:T(8,128)(2,1)} async-done(((bf16[256,512]{1,0:T(8,128)(2,1)}), bf16[1024,512]{1,0:T(8,128)(2,1)}) %all-gather.25.cloned.1.call-update) | async-done | bytes 1048592 | tf_op jit(solution)/shard_map/all_gather | solution.py:188
  114.9 20.5 %reshape.217 = f32[8,256,1279]{2,1,0:T(8,128)} reshape(f32[2619392]{0:T(1024)} %reshape.268) | data formatting | bytes 20955136 | tf_op jit(solution)/shard_map/reshape | solution.py:60
  158.8 21.5 %all-gather.21.cloned.1.call-done = bf16[2,1024,512]{2,1,0:T(8,128)(2,1)} async-done(((bf16[2,256,512]{2,1,0:T(8,128)(2,1)}), bf16[2,1024,512]{2,1,0:T(8,128)(2,1)}) %all-gather.21.cloned.1.call-update) | async-done | bytes 2097168 | tf_op jit(solution)/shard_map/all_gather | solution.py:245
  184.2 20.8 %all-gather.27.cloned.1.call-done = bf16[2,1024,512]{2,1,0:T(8,128)(2,1)} async-done(((bf16[2,256,512]{2,1,0:T(8,128)(2,1)}), bf16[2,1024,512]{2,1,0:T(8,128)(2,1)}) %all-gather.27.cloned.1.call-update) | async-done | bytes 2097168 | tf_op jit(solution)/shard_map/all_gather | solution.py:244
  208.8 21.2 %while.55 = (s32[]{:T(128)}, bf16[2,256,8,64]{1,3,2,0:T(8,128)(2,1)}, f32[2,8,256,1]{2,1,3,0:T(8,128)S(1)}, bf16[2,1024,8,64]{1,3,2,0:T(8,128)(2,1)}, pred[2,256...) while((s32[]{:T(128)}, ...), condition=%wide.region_4.5_spmd, body=%wide.region_1.4_spmd.sunk | while | flops 551680000 | bytes 49612984 | solution.py:127
  256.3 16.5 %all-gather.39.cloned.1.call-done = bf16[2,512,512]{2,1,0:T(8,128)(2,1)} async-done(((bf16[2,128,512]{2,1,0:T(8,128)(2,1)}), bf16[2,512,512]{2,1,0:T(8,128)(2,1)}) %all-gather.39.cloned.1.call-update) | async-done | bytes 1048592 | tf_op jit(solution)/shard_map/all_gather | solution.py:261
  275.0 40.7 %all-reduce.18.cloned.1.call-done = bf16[2,256,1024]{2,1,0:T(8,128)(2,1)} async-done(((bf16[2,256,1024]{2,1,0:T(8,128)(2,1)}), bf16[2,256,1024]{2,1,0:T(8,128)(2,1)}) %all-reduce.18.cloned.1.call-update) | async-done | bytes 1048592 | tf_op jit(solution)/shard_map/psum | solution.py:155
  317.6 27.5 %all-gather.35.cloned.1.call-done = bf16[1024,512]{1,0:T(8,128)(2,1)} async-done(((bf16[256,512]{1,0:T(8,128)(2,1)}), bf16[1024,512]{1,0:T(8,128)(2,1)}) %all-gather.35.cloned.1.call-update) | async-done | bytes 1048592 | tf_op jit(solution)/shard_map/all_gather | solution.py:193
  391.5 43.9 %all-gather.47.cloned.1.call-done = bf16[1408,1024]{1,0:T(8,128)(2,1)} async-done(((bf16[1408,256]{1,0:T(8,128)(2,1)}), bf16[1408,1024]{1,0:T(8,128)(2,1)}) %all-gather.47.cloned.1.call-update) | async-done | bytes 2883600 | tf_op jit(solution)/shard_map/all_gather | solution.py:200
  441.0 35.5 %all-reduce.20.cloned.1.call-done = bf16[2,256,1024]{2,1,0:T(8,128)(2,1)} async-done(((bf16[2,256,1024]{2,1,0:T(8,128)(2,1)}), bf16[2,256,1024]{2,1,0:T(8,128)(2,1)}) %all-reduce.20.cloned.1.call-update) | async-done | bytes 1048592 | tf_op jit(solution)/shard_map/psum | solution.py:155
  481.5 55.7 %all-gather.45.cloned.1.call-done = bf16[1024,1408]{1,0:T(8,128)(2,1)} async-done(((bf16[256,1408]{1,0:T(8,128)(2,1)}), bf16[1024,1408]{1,0:T(8,128)(2,1)}) %all-gather.45.cloned.1.call-update) | async-done | bytes 2883600 | tf_op jit(solution)/shard_map/all_gather | solution.py:199
  542.7 53.8 %all-gather.43.cloned.1.call-done = bf16[1024,1408]{1,0:T(8,128)(2,1)} async-done(((bf16[256,1408]{1,0:T(8,128)(2,1)}), bf16[1024,1408]{1,0:T(8,128)(2,1)}) %all-gather.43.cloned.1.call-update) | async-done | bytes 2883600 | tf_op jit(solution)/shard_map/all_gather | solution.py:198
  611.3 38.6 %all-reduce.22.cloned.1.call-done = bf16[2,256,1024]{2,1,0:T(8,128)(2,1)} async-done(((bf16[2,256,1024]{2,1,0:T(8,128)(2,1)}), bf16[2,256,1024]{2,1,0:T(8,128)(2,1)}) %all-reduce.22.cloned.1.call-update) | async-done | bytes 1048592 | tf_op jit(solution)/shard_map/psum | solution.py:159
  661.1 19.9 %while.57 = (s32[]{:T(128)}, bf16[2,256,8,64]{1,3,2,0:T(8,128)(2,1)}, bf16[2,512,8,64]{1,3,2,0:T(8,128)(2,1)}, bf16[2,512,8,64]{1,3,2,0:T(8,128)(2,1)}, bf16[2,5...) while((s32[]{:T(128)}, ...), condition=%wide.region_18.19_spmd, body=%wide.region_16.18_spmd.sunk | while | flops 683800576 | bytes 62322004 | solution.py:148
  696.9 27.5 %all-reduce.24.cloned.1.call-done = bf16[2,256,1024]{2,1,0:T(8,128)(2,1)} async-done(((bf16[2,256,1024]{2,1,0:T(8,128)(2,1)}), bf16[2,256,1024]{2,1,0:T(8,128)(2,1)}) %all-reduce.24.cloned.1.call-update) | async-done | bytes 1048592 | tf_op jit(solution)/shard_map/psum | solution.py:321
  736.1 59.6 %while.58 = (s32[]{:T(128)}, f32[8,256,1024]{2,1,0:T(8,128)}, bf16[2,256,8,64]{1,3,2,0:T(8,128)(2,1)}, bf16[2,1024,8,64]{1,3,2,0:T(8,128)(2,1)}, bf16[2,1024,8,6...) while((s32[]{:T(128)}, f32[8,256,1024]{2,1,0:T(8,128)}, ...), condition=%wide.region_23.24_spmd.clone, body=%wide.region_21.23_spmd.clone.sunk | while | flops 1367472128 | bytes 198227360 | solution.py:148
  842.0 23.3 %reduce-scatter.22.cloned.1.call-done = bf16[2,256,512]{2,1,0:T(8,128)(2,1)} async-done(((bf16[2,1024,512]{2,1,0:T(8,128)(2,1)}), bf16[2,256,512]{2,1,0:T(8,128)(2,1)}) %reduce-scatter.22.cloned.1.call-update) | async-done | bytes 524304 | tf_op jit(solution)/shard_map/reduce_scatter | solution.py:352
  894.5 28.2 %reduce-scatter.38.cloned.1.call-done = bf16[512,256]{1,0:T(8,128)(2,1)} async-done(((bf16[512,1024]{1,0:T(8,128)(2,1)}), bf16[512,256]{1,0:T(8,128)(2,1)}) %reduce-scatter.38.cloned.1.call-update) | async-done | bytes 262160 | tf_op jit(solution)/shard_map/reduce_scatter | solution.py:405
  922.8 28.0 %reduce-scatter.30.cloned.1.call-done = bf16[512,256]{1,0:T(8,128)(2,1)} async-done(((bf16[512,1024]{1,0:T(8,128)(2,1)}), bf16[512,256]{1,0:T(8,128)(2,1)}) %reduce-scatter.30.cloned.1.call-update) | async-done | bytes 262160 | tf_op jit(solution)/shard_map/reduce_scatter | solution.py:387
  950.7 28.1 %reduce-scatter.24.cloned.1.call-done = bf16[256,512]{1,0:T(8,128)(2,1)} async-done(((bf16[1024,512]{1,0:T(8,128)(2,1)}), bf16[256,512]{1,0:T(8,128)(2,1)}) %reduce-scatter.24.cloned.1.call-update) | async-done | bytes 262160 | tf_op jit(solution)/shard_map/reduce_scatter | solution.py:378
  978.8 28.1 %reduce-scatter.34.cloned.1.call-done = bf16[256,512]{0,1:T(8,128)(2,1)} async-done(((bf16[1024,512]{0,1:T(8,128)(2,1)}), bf16[256,512]{0,1:T(8,128)(2,1)}) %reduce-scatter.34.cloned.1.call-update) | async-done | bytes 262160 | tf_op jit(solution)/shard_map/reduce_scatter | solution.py:399
  1006.9 28.2 %reduce-scatter.36.cloned.1.call-done = bf16[256,512]{0,1:T(8,128)(2,1)} async-done(((bf16[1024,512]{0,1:T(8,128)(2,1)}), bf16[256,512]{0,1:T(8,128)(2,1)}) %reduce-scatter.36.cloned.1.call-update) | async-done | bytes 262160 | tf_op jit(solution)/shard_map/reduce_scatter | solution.py:402
  1035.2 57.0 %reduce-scatter.40.cloned.1.call-done = bf16[256,1408]{1,0:T(8,128)(2,1)} async-done(((bf16[1024,1408]{1,0:T(8,128)(2,1)}), bf16[256,1408]{1,0:T(8,128)(2,1)}) %reduce-scatter.40.cloned.1.call-update) | async-done | bytes 720912 | tf_op jit(solution)/shard_map/reduce_scatter | solution.py:411
  1092.2 58.4 %reduce-scatter.42.cloned.1.call-done = bf16[256,1408]{1,0:T(8,128)(2,1)} async-done(((bf16[1024,1408]{1,0:T(8,128)(2,1)}), bf16[256,1408]{1,0:T(8,128)(2,1)}) %reduce-scatter.42.cloned.1.call-update) | async-done | bytes 720912 | tf_op jit(solution)/shard_map/reduce_scatter | solution.py:414
  1150.6 58.4 %reduce-scatter.44.cloned.1.call-done = bf16[1408,256]{1,0:T(8,128)(2,1)} async-done(((bf16[1408,1024]{1,0:T(8,128)(2,1)}), bf16[1408,256]{1,0:T(8,128)(2,1)}) %reduce-scatter.44.cloned.1.call-update) | async-done | bytes 720912 | tf_op jit(solution)/shard_map/reduce_scatter | solution.py:417
  1209.0 29.7 %reduce-scatter.26.cloned.1.call-done = bf16[256,512]{1,0:T(8,128)(2,1)} async-done(((bf16[1024,512]{1,0:T(8,128)(2,1)}), bf16[256,512]{1,0:T(8,128)(2,1)}) %reduce-scatter.26.cloned.1.call-update) | async-done | bytes 262160 | tf_op jit(solution)/shard_map/reduce_scatter | solution.py:381
  1238.7 28.8 %reduce-scatter.28.cloned.1.call-done = bf16[256,512]{1,0:T(8,128)(2,1)} async-done(((bf16[1024,512]{1,0:T(8,128)(2,1)}), bf16[256,512]{1,0:T(8,128)(2,1)}) %reduce-scatter.28.cloned.1.call-update) | async-done | bytes 262160 | tf_op jit(solution)/shard_map/reduce_scatter | solution.py:384
  1278.7 16.4 %reshape.270 = f32[2619392]{0:T(1024)} reshape(f32[8,256,1279]{2,1,0:T(8,128)} %concatenate.22) | data formatting | bytes 20955136
  1321.5 23.0 %all-reduce.28.cloned.1.call-done = (bf16[2,256,1024]{2,1,0:T(8,128)(2,1)}, bf16[2,256,1024]{2,1,0:T(8,128)(2,1)}, bf16[2,128,1024]{2,1,0:T(8,128)(2,1)}) async-done(((bf16[2,256,1024]{2,1,0:T(8,128)(2,1)}, bf16[2,256,1024]{2,1,0:T(8,128)(2,1)}, bf16[2,128,1024]{2,1,0:T(8,128)(2,1)}), (bf16[2,256,1024]{2,1,0:T(8,128)(2,1)}, bf16[2,256,1024]{2,1,0:T(8,128)(2,1)}, ...) | async-done | bytes 2621456 | tf_op jit(solution)/shard_map/psum | solution.py:155
  1346.9 18.7 %all-reduce.9 = (bf16[1024]{0:T(1024)(128)(2,1)S(1)}, bf16[32,8]{1,0:T(8,128)(2,1)S(1)}, bf16[1024]{0:T(1024)(128)(2,1)S(1)}, bf16[1024]{0:T(1024)(128)(2,1)S(1)}) all-reduce(bf16[1024]{0:T(1024)(128)(2,1)S(1)} %get-tuple-element.363, ...), channel_id=6, replica_groups=mesh['fsdp'=4,'ctx'=4,'tp'=2] {'fsdp'}, use_global_device_ids=true, to_apply=%region_32.33.clone | all-reduce | flops 3328 | bytes 13312
  1379.2 57.3 %all-reduce.26.cloned.1.call-done = (bf16[256,512]{0,1:T(8,128)(2,1)}, bf16[256,512]{0,1:T(8,128)(2,1)}, bf16[256,512]{1,0:T(8,128)(2,1)}, bf16[256,512]{1,0:T(8...) async-done(((bf16[256,512]{0,1:T(8,128)(2,1)}, ...) | async-done | bytes 4259856 | tf_op jit(solution)/shard_map/psum | solution.py:430
  (468 shorter events, 494.5 us)
Async XLA Ops:
  9.4 135.8 %all-gather.23.cloned.1.call-start = ((), (), s32[]{:S(2)}) async-start(), calls=%async_computation.17 | async-start | bytes 1310720 | tf_op jit(solution)/shard_map/all_gather | solution.py:187
  10.0 146.1 %all-gather.37.cloned.1.call-start = ((), (), s32[]{:S(2)}) async-start(), calls=%async_computation.25 | async-start | bytes 1310720 | tf_op jit(solution)/shard_map/all_gather | solution.py:194
  10.6 169.6 %all-gather.21.cloned.1.call-start = ((), (), s32[]{:S(2)}) async-start(), calls=%async_computation.16 | async-start | bytes 2621440 | tf_op jit(solution)/shard_map/all_gather | solution.py:245
  43.1 161.8 %all-gather.27.cloned.1.call-start = ((), (), s32[]{:S(2)}) async-start(), calls=%async_computation.19 | async-start | bytes 2621440 | tf_op jit(solution)/shard_map/all_gather | solution.py:244
  72.1 164.7 %all-gather.29.cloned.1.call-start = ((), (), s32[]{:S(2)}) async-start(), calls=%async_computation.20 | async-start | bytes 1310720 | tf_op jit(solution)/shard_map/all_gather | solution.py:190
  72.9 181.1 %all-gather.33.cloned.1.call-start = ((), (), s32[]{:S(2)}) async-start(), calls=%async_computation.23 | async-start | bytes 1310720 | tf_op jit(solution)/shard_map/all_gather | solution.py:262
  100.8 171.9 %all-gather.39.cloned.1.call-start = ((), (), s32[]{:S(2)}) async-start(), calls=%async_computation.26 | async-start | bytes 1310720 | tf_op jit(solution)/shard_map/all_gather | solution.py:261
  158.5 157.2 %all-reduce.18.cloned.1.call-start = ((), (), s32[]{:S(2)}) async-start(), calls=%async_computation.21 | async-start | bytes 2097152 | tf_op jit(solution)/shard_map/psum | solution.py:155
  239.9 105.2 %all-gather.35.cloned.1.call-start = ((), (), s32[]{:S(2)}) async-start(), calls=%async_computation.24 | async-start | bytes 1310720 | tf_op jit(solution)/shard_map/all_gather | solution.py:193
  240.5 136.0 %all-gather.41.cloned.1.call-start = ((), (), s32[]{:S(2)}) async-start(), calls=%async_computation.27 | async-start | bytes 1310720 | tf_op jit(solution)/shard_map/all_gather | solution.py:196
  241.2 194.2 %all-gather.47.cloned.1.call-start = ((), (), s32[]{:S(2)}) async-start(), calls=%async_computation.31 | async-start | bytes 3604480 | tf_op jit(solution)/shard_map/all_gather | solution.py:200
  241.8 234.7 %all-reduce.20.cloned.1.call-start = ((), (), s32[]{:S(2)}) async-start(), calls=%async_computation.28 | async-start | bytes 2097152 | tf_op jit(solution)/shard_map/psum | solution.py:155
  379.6 157.6 %all-gather.45.cloned.1.call-start = ((), (), s32[]{:S(2)}) async-start(), calls=%async_computation.30 | async-start | bytes 3604480 | tf_op jit(solution)/shard_map/all_gather | solution.py:199
  380.2 216.3 %all-gather.43.cloned.1.call-start = ((), (), s32[]{:S(2)}) async-start(), calls=%async_computation.29 | async-start | bytes 3604480 | tf_op jit(solution)/shard_map/all_gather | solution.py:198
  380.8 269.2 %all-reduce.22.cloned.1.call-start = ((), (), s32[]{:S(2)}) async-start(), calls=%async_computation.32 | async-start | bytes 2097152 | tf_op jit(solution)/shard_map/psum | solution.py:159
  611.1 113.2 %all-reduce.24.cloned.1.call-start = ((), (), s32[]{:S(2)}) async-start(), calls=%async_computation.33 | async-start | bytes 2097152 | tf_op jit(solution)/shard_map/psum | solution.py:321
  684.1 133.7 %reduce-scatter.46.cloned.1.call-start = ((), (), s32[]{:S(2)}) async-start(), calls=%async_computation.47 | async-start | bytes 1310720
  690.4 130.4 %reduce-scatter.48.cloned.1.call-start = ((), (), s32[]{:S(2)}) async-start(), calls=%async_computation.48 | async-start | bytes 1310720
  696.6 142.4 %reduce-scatter.20.cloned.1.call-start = ((), (), s32[]{:S(2)}) async-start(), calls=%async_computation.34 | async-start | bytes 2621440 | tf_op jit(solution)/shard_map/reduce_scatter | solution.py:349
  803.7 90.8 %reduce-scatter.32.cloned.1.call-start = ((), (), s32[]{:S(2)}) async-start(), calls=%async_computation.40 | async-start | bytes 1310720 | tf_op jit(solution)/shard_map/reduce_scatter | solution.py:396
  808.4 114.4 %reduce-scatter.38.cloned.1.call-start = ((), (), s32[]{:S(2)}) async-start(), calls=%async_computation.43 | async-start | bytes 1310720 | tf_op jit(solution)/shard_map/reduce_scatter | solution.py:405
  811.9 138.8 %reduce-scatter.30.cloned.1.call-start = ((), (), s32[]{:S(2)}) async-start(), calls=%async_computation.39 | async-start | bytes 1310720 | tf_op jit(solution)/shard_map/reduce_scatter | solution.py:387
  815.3 163.5 %reduce-scatter.24.cloned.1.call-start = ((), (), s32[]{:S(2)}) async-start(), calls=%async_computation.36 | async-start | bytes 1310720 | tf_op jit(solution)/shard_map/reduce_scatter | solution.py:378
  817.7 189.2 %reduce-scatter.34.cloned.1.call-start = ((), (), s32[]{:S(2)}) async-start(), calls=%async_computation.41 | async-start | bytes 1310720 | tf_op jit(solution)/shard_map/reduce_scatter | solution.py:399
  820.7 214.5 %reduce-scatter.36.cloned.1.call-start = ((), (), s32[]{:S(2)}) async-start(), calls=%async_computation.42 | async-start | bytes 1310720 | tf_op jit(solution)/shard_map/reduce_scatter | solution.py:402
  823.6 268.6 %reduce-scatter.40.cloned.1.call-start = ((), (), s32[]{:S(2)}) async-start(), calls=%async_computation.44 | async-start | bytes 3604480 | tf_op jit(solution)/shard_map/reduce_scatter | solution.py:411
  828.8 321.8 %reduce-scatter.42.cloned.1.call-start = ((), (), s32[]{:S(2)}) async-start(), calls=%async_computation.45 | async-start | bytes 3604480 | tf_op jit(solution)/shard_map/reduce_scatter | solution.py:414
  833.9 375.0 %reduce-scatter.44.cloned.1.call-start = ((), (), s32[]{:S(2)}) async-start(), calls=%async_computation.46 | async-start | bytes 3604480 | tf_op jit(solution)/shard_map/reduce_scatter | solution.py:417
  838.9 399.8 %reduce-scatter.26.cloned.1.call-start = ((), (), s32[]{:S(2)}) async-start(), calls=%async_computation.37 | async-start | bytes 1310720 | tf_op jit(solution)/shard_map/reduce_scatter | solution.py:381
  841.9 425.6 %reduce-scatter.28.cloned.1.call-start = ((), (), s32[]{:S(2)}) async-start(), calls=%async_computation.38 | async-start | bytes 1310720 | tf_op jit(solution)/shard_map/reduce_scatter | solution.py:384
  868.1 476.4 %all-reduce.28.cloned.1.call-start = ((), (), s32[]{:S(2)}) async-start(), calls=%async_computation.50 | async-start | bytes 5242880 | tf_op jit(solution)/shard_map/psum | solution.py:155
  880.1 556.4 %all-reduce.26.cloned.1.call-start = ((), (), s32[]{:S(2)}) async-start(), calls=%async_computation.49 | async-start | bytes 8519680 | tf_op jit(solution)/shard_map/psum | solution.py:430
  (103 other events, 1091.9 us)
Sparse Core Ops, SparseCore 0:
  9.6 30.6 all-gather.18
  41.9 27.3 all-gather.24
  70.9 27.4 all-gather.30
  99.8 27.3 all-gather.22
  128.7 27.4 all-gather.36
  206.5 30.1 all-gather.28
  275.6 40.0 all-reduce.17
  317.2 27.9 all-gather.34
  346.8 29.6 all-gather.40
  378.0 57.4 all-gather.46
  438.3 38.2 all-reduce.19
  478.0 59.1 all-gather.44
  538.6 57.8 all-gather.42
  611.2 38.7 all-reduce.21
  684.2 40.0 all-reduce.23
  726.7 24.8 reduce-scatter.45
  754.3 24.9 reduce-scatter.47
  799.8 31.2 reduce-scatter.19
  833.8 31.3 reduce-scatter.21
  867.4 27.1 reduce-scatter.31
  896.9 25.7 reduce-scatter.37
  924.9 25.7 reduce-scatter.29
  953.0 25.7 reduce-scatter.23
  981.1 25.7 reduce-scatter.33
  1009.3 25.7 reduce-scatter.35
  1037.3 54.8 reduce-scatter.39
  1094.5 56.0 reduce-scatter.41
  1152.9 56.0 reduce-scatter.43
  1211.7 26.9 reduce-scatter.25
  1241.7 25.7 reduce-scatter.27
  1271.1 73.3 all-reduce.27
  1347.9 88.5 all-reduce.25
  (4 shorter events, 76.2 us)
where the time goes:
time: 1460 us
  waiting for transfers between devices  965 us (66%)
  local copies, waits for them, and re-layouts  163 us (11%)
  matrix products  161 us (11%)
  other arithmetic  75.8 us (5%)
  blocking collectives  70.7 us (5%)
  between operations  16.4 us (1%)
    psum x3, waiting for transfers between devices, branch_total(): lax.psum(partial_value.astype(jnp.bfloat16), 'tp').astype(jnp.float32)  99.2 us
    reduce_scatter x1, waiting for transfers between devices, body(): lax.psum_scatter(grad_down.astype(jnp.bfloat16), 'fsdp', scatter_dimensio...  58.4 us
    reduce_scatter x1, waiting for transfers between devices, body(): lax.psum_scatter(grad_up.astype(jnp.bfloat16), 'fsdp', scatter_dimension=...  58.4 us
    psum x1, waiting for transfers between devices, body(): lax.psum(shard_sums[8].astype(jnp.bfloat16), 'ctx').astype(jnp.float32)  57.3 us
    reduce_scatter x1, waiting for transfers between devices, body(): lax.psum_scatter(grad_gate.astype(jnp.bfloat16), 'fsdp', scatter_dimensio...  57 us
    all_gather x1, waiting for transfers between devices, body(): lax.all_gather(ffn_up, 'fsdp', axis=0, tiled=True)  55.7 us
    all_gather x1, waiting for transfers between devices, body(): lax.all_gather(ffn_gate, 'fsdp', axis=0, tiled=True)  53.8 us
    unnamed x127, local copies, waits for them, and re-layouts  53.5 us
  transfers between devices with their start and end apart: 36, of which 32 were waited for; matrix products, arithmetic and copies ran while one was open for 22% of the time, Pallas kernels for 0%

commit v1 on v0

v1 whole, which is shorter than its diff:
```python
import functools
import jax
import jax.numpy as jnp
from jax import lax
from jax.experimental import pallas as pl
from jax.experimental.pallas import tpu as pltpu
from jax.sharding import PartitionSpec as P

EPSILON = 1e-06
NEGATIVE = -1e30
LANES = 128
CHUNK = 256
NT = (((1,), (1,)), ((), ()))
NN = (((1,), (0,)), ((), ()))


def dot(lhs, rhs, dims=NN):
    return lax.dot_general(lhs, rhs, dims, preferred_element_type=jnp.float32)


def fill_mask(mask_ref, seg_row, seg_col_ref, offset_ref, causal):
    rows = seg_row.shape[1]
    keys = mask_ref.shape[0]
    for start in range(0, keys, CHUNK):
        size = min(CHUNK, keys - start)
        seen = seg_col_ref[0, pl.ds(start, size), :] == seg_row
        if causal:
            key_place = lax.broadcasted_iota(jnp.int32, (size, rows), 0) + start
            query_place = lax.broadcasted_iota(jnp.int32, (size, rows), 1) + offset_ref[0, 0]
            seen = seen & (key_place <= query_place)
        mask_ref[pl.ds(start, size), :] = jnp.where(seen, 0.0, NEGATIVE)


def fill_bias(bias_ref, head, line):
    width = line.shape[1]
    base = jnp.broadcast_to(line, (8, width))
    row = lax.broadcasted_iota(jnp.int32, (8, width), 0)
    for bit in (1, 2, 4):
        base = jnp.where((row & bit) != 0, pltpu.roll(base, bit, 1), base)
    for block in range(LANES // 8):
        bias_ref[head, pl.ds(8 * block, 8), :] = pltpu.roll(base, 8 * block, 1) if block else base


def fold_diagonals(total):
    width = total.shape[1]
    half = total.shape[0] // 2
    while half >= 8:
        total = total[:half] + pltpu.roll(total[half:], width - half, 1)
        half //= 2
    row = lax.broadcasted_iota(jnp.int32, (8, width), 0)
    for bit in (4, 2, 1):
        total = jnp.where((row & bit) != 0, pltpu.roll(total, width - bit, 1), total)
    return jnp.sum(total, axis=0, keepdims=True)


def head_mask(rows, head):
    lane = lax.broadcasted_iota(jnp.int32, (rows, LANES), 1)
    return (lane // (LANES // 2)) == head


def add_bias(scores, bias_ref, head, start, keys, rows):
    parts = []
    for sub in range(0, scores.shape[0], LANES):
        at = keys - (start + sub)
        parts.append(scores[sub : sub + LANES] + bias_ref[head, :, at : at + rows])
    return jnp.concatenate(parts, axis=0)


def forward_kernel(causal, *refs):
    if causal:
        (offset_ref, line_ref, seg_row_ref, seg_col_ref, q_ref, k_ref, v_ref, out_ref, log_ref,
         mask_ref, score_ref, bias_ref) = refs
    else:
        (seg_row_ref, seg_col_ref, q_ref, k_ref, v_ref, out_ref, log_ref,
         mask_ref, score_ref) = refs
        offset_ref = None
    pair = pl.program_id(0)
    seq = pl.program_id(1)
    rows = q_ref.shape[1]
    keys = k_ref.shape[1]

    @pl.when(pair == 0)
    def _():
        fill_mask(mask_ref.at[seq], seg_row_ref[0], seg_col_ref, offset_ref, causal)

    if causal:

        @pl.when(seq == 0)
        def _():
            for head in range(2):
                fill_bias(bias_ref, head, line_ref[0, pl.ds(head, 1), :])

    q = q_ref[0]
    v_turned = v_ref[0].T
    half = LANES // 2
    outs = []
    logs = []
    for head in range(2):
        q_head = jnp.where(head_mask(rows, head), q, jnp.zeros_like(q))
        highest = None
        for start in range(0, keys, CHUNK):
            scores = dot(k_ref[0, pl.ds(start, CHUNK), :], q_head, NT)
            scores = scores + mask_ref[seq, pl.ds(start, CHUNK), :]
            if causal:
                scores = add_bias(scores, bias_ref, head, start, keys, rows)
            score_ref[pl.ds(start, CHUNK), :] = scores
            top = jnp.max(scores, axis=0, keepdims=True)
            highest = top if highest is None else jnp.maximum(highest, top)
        total = None
        attended = None
        for start in range(0, keys, CHUNK):
            grown = jnp.exp(score_ref[pl.ds(start, CHUNK), :] - highest)
            part = jnp.sum(grown, axis=0, keepdims=True)
            piece = dot(v_turned[half * head : half * head + half, start : start + CHUNK],
                        grown.astype(jnp.bfloat16))
            total = part if total is None else total + part
            attended = piece if attended is None else attended + piece
        outs.append(attended / total)
        logs.append(highest + jnp.log(total))
    out_ref[0] = jnp.concatenate(outs, axis=0).T.astype(jnp.bfloat16)
    log_ref[0, 0] = jnp.concatenate(logs + [jnp.zeros((6, rows), jnp.float32)], axis=0)


def backward_kernel(causal, *refs):
    if causal:
        (offset_ref, line_ref, seg_row_ref, seg_col_ref, q_ref, k_ref, v_ref, out_ref, log_ref,
         grad_ref, dq_ref, dk_ref, dv_ref, line_grad_ref, mask_ref, bias_ref, total_ref) = refs
    else:
        (seg_row_ref, seg_col_ref, q_ref, k_ref, v_ref, out_ref, log_ref,
         grad_ref, dq_ref, dk_ref, dv_ref, mask_ref) = refs
        offset_ref = None
    pair = pl.program_id(0)
    seq = pl.program_id(1)
    rows = q_ref.shape[1]
    keys = k_ref.shape[1]
    half = LANES // 2

    @pl.when(pair == 0)
    def _():
        fill_mask(mask_ref.at[seq], seg_row_ref[0], seg_col_ref, offset_ref, causal)

    if causal:

        @pl.when(seq == 0)
        def _():
            for head in range(2):
                fill_bias(bias_ref, head, line_ref[0, pl.ds(head, 1), :])
            total_ref[...] = jnp.zeros_like(total_ref)

    q = q_ref[0]
    grad = grad_ref[0]
    product = grad.astype(jnp.float32) * out_ref[0].astype(jnp.float32)
    chooser = (
        lax.broadcasted_iota(jnp.int32, (8, LANES), 1) // half
        == lax.broadcasted_iota(jnp.int32, (8, LANES), 0)
    ).astype(jnp.float32)
    inner = lax.dot_general(chooser, product, NT, precision=lax.Precision.HIGHEST,
                            preferred_element_type=jnp.float32)
    q_heads = [jnp.where(head_mask(rows, h), q, jnp.zeros_like(q)) for h in range(2)]
    grad_heads = [jnp.where(head_mask(rows, h), grad, jnp.zeros_like(grad)) for h in range(2)]
    dq = [None, None]
    for start in range(0, keys, CHUNK):
        k = k_ref[0, pl.ds(start, CHUNK), :]
        v = v_ref[0, pl.ds(start, CHUNK), :]
        k_turned = k.T
        dk = None
        dv = None
        for head in range(2):
            scores = dot(k, q_heads[head], NT)
            scores = scores + mask_ref[seq, pl.ds(start, CHUNK), :]
            if causal:
                scores = add_bias(scores, bias_ref, head, start, keys, rows)
            weights = jnp.exp(scores - log_ref[0, 0, pl.ds(head, 1), :])
            dv_part = dot(weights.astype(jnp.bfloat16), grad_heads[head])
            dw = dot(v, grad_heads[head], NT)
            ds = weights * (dw - inner[head : head + 1])
            ds_low = ds.astype(jnp.bfloat16)
            dk_part = dot(ds_low, q_heads[head])
            dq_part = dot(k_turned[half * head : half * head + half], ds_low)
            dv = dv_part if dv is None else dv + dv_part
            dk = dk_part if dk is None else dk + dk_part
            dq[head] = dq_part if dq[head] is None else dq[head] + dq_part
            if causal:
                for sub in range(0, CHUNK, LANES):
                    at = keys - (start + sub)
                    total_ref[head, :, at : at + rows] += ds[sub : sub + LANES]
        dk_ref[0, pl.ds(start, CHUNK), :] = dk.astype(jnp.bfloat16)
        dv_ref[0, pl.ds(start, CHUNK), :] = dv.astype(jnp.bfloat16)
    dq_ref[0] = jnp.concatenate(dq, axis=0).T.astype(jnp.bfloat16)
    if causal:

        @pl.when(seq == pl.num_programs(1) - 1)
        def _():
            lines = [fold_diagonals(total_ref[head]) for head in range(2)]
            lines.append(jnp.zeros((6, lines[0].shape[1]), jnp.float32))
            line_grad_ref[0] = jnp.concatenate(lines, axis=0)


def specs_for(rows, keys, pairs, causal):
    def wide(count, shift=0):
        return pl.BlockSpec((1, count, LANES), lambda p, s: (s, 0, p + shift))

    lead = []
    if causal:
        lead = [
            pl.BlockSpec((1, 1), lambda p, s: (0, 0), memory_space=pltpu.SMEM),
            pl.BlockSpec((1, 8, rows + keys), lambda p, s: (p, 0, 0)),
        ]
    lead += [
        pl.BlockSpec((1, 1, rows), lambda p, s: (s, 0, 0)),
        pl.BlockSpec((1, keys, 1), lambda p, s: (s, 0, 0)),
        wide(rows),
        wide(keys),
        wide(keys, pairs),
    ]
    return lead, wide, pl.BlockSpec((1, 1, 8, rows), lambda p, s: (s, p, 0, 0))


def attend_forward(q, kv, seg_row, seg_col, offset=None, lines=None):
    seqs, rows, width = q.shape
    keys = kv.shape[1]
    pairs = width // LANES
    causal = lines is not None
    lead, wide, logs = specs_for(rows, keys, pairs, causal)
    scratch = [pltpu.VMEM((seqs, keys, rows), jnp.float32), pltpu.VMEM((keys, rows), jnp.float32)]
    args = [seg_row, seg_col, q, kv, kv]
    if causal:
        args = [offset, lines] + args
        scratch.append(pltpu.VMEM((2, LANES, rows + keys), jnp.float32))
    return pl.pallas_call(
        functools.partial(forward_kernel, causal),
        grid=(pairs, seqs),
        in_specs=lead,
        out_specs=[wide(rows), logs],
        out_shape=[
            jax.ShapeDtypeStruct((seqs, rows, width), jnp.bfloat16),
            jax.ShapeDtypeStruct((seqs, pairs, 8, rows), jnp.float32),
        ],
        scratch_shapes=scratch,
        compiler_params=pltpu.CompilerParams(vmem_limit_bytes=40 * 1024 * 1024),
        cost_estimate=pl.CostEstimate(
            flops=seqs * pairs * 4 * 2 * rows * keys * 128,
            bytes_accessed=4 * seqs * (rows + keys) * width,
            transcendentals=seqs * pairs * 2 * rows * keys,
        ),
        name="attend_forward",
    )(*args)


def attend_backward(q, kv, seg_row, seg_col, out, logs_value, grad, offset=None, lines=None):
    seqs, rows, width = q.shape
    keys = kv.shape[1]
    pairs = width // LANES
    causal = lines is not None
    lead, wide, logs = specs_for(rows, keys, pairs, causal)
    scratch = [pltpu.VMEM((seqs, keys, rows), jnp.float32)]
    args = [seg_row, seg_col, q, kv, kv, out, logs_value, grad]
    out_shape = [
        jax.ShapeDtypeStruct((seqs, rows, width), jnp.bfloat16),
        jax.ShapeDtypeStruct((seqs, keys, width), jnp.bfloat16),
        jax.ShapeDtypeStruct((seqs, keys, width), jnp.bfloat16),
    ]
    out_specs = [wide(rows), wide(keys), wide(keys)]
    if causal:
        args = [offset, lines] + args
        scratch.append(pltpu.VMEM((2, LANES, rows + keys), jnp.float32))
        scratch.append(pltpu.VMEM((2, LANES, rows + keys), jnp.float32))
        out_shape.append(jax.ShapeDtypeStruct((pairs, 8, rows + keys), jnp.float32))
        out_specs.append(pl.BlockSpec((1, 8, rows + keys), lambda p, s: (p, 0, 0)))
    return pl.pallas_call(
        functools.partial(backward_kernel, causal),
        grid=(pairs, seqs),
        in_specs=lead + [wide(rows), logs, wide(rows)],
        out_specs=out_specs,
        out_shape=out_shape,
        scratch_shapes=scratch,
        compiler_params=pltpu.CompilerParams(vmem_limit_bytes=40 * 1024 * 1024),
        cost_estimate=pl.CostEstimate(
            flops=seqs * pairs * 10 * 2 * rows * keys * 128,
            bytes_accessed=8 * seqs * (rows + keys) * width,
            transcendentals=seqs * pairs * 2 * rows * keys,
        ),
        name="attend_backward",
    )(*args)


def mm(lhs, rhs):
    return lax.dot_general(lhs, rhs, (((lhs.ndim - 1,), (0,)), ((), ())),
                           preferred_element_type=jnp.float32)


def mm_back(lhs, rhs):
    return lax.dot_general(lhs, rhs, (((lhs.ndim - 1,), (1,)), ((), ())),
                           preferred_element_type=jnp.float32)


def weight_grad(rows, grads):
    return lax.dot_general(rows, grads, (((0, 1), (0, 1)), ((), ())),
                           preferred_element_type=jnp.float32).astype(jnp.bfloat16)


def rms_forward(values, gain_row):
    inverse_rms = lax.rsqrt(jnp.mean(values * values, axis=-1, keepdims=True) + EPSILON)
    unit_rows = values * inverse_rms
    return unit_rows, inverse_rms, (unit_rows * gain_row).astype(jnp.bfloat16)


def rms_backward(grad_normed, unit_rows, inverse_rms, gain_row):
    grad_unit = grad_normed * gain_row
    grad_gain = jnp.sum(grad_normed * unit_rows, axis=(0, 1))
    inner_sum = jnp.mean(grad_unit * unit_rows, axis=-1, keepdims=True)
    return inverse_rms * (grad_unit - unit_rows * inner_sum), grad_gain


def ctx_shape():
    count = lax.axis_size("ctx")
    low = 2 if count % 2 == 0 else 1
    return count // low, low


def ctx_place():
    high, low = ctx_shape()
    index = lax.axis_index("ctx")
    return index // low, index % low


def swap_low(value):
    high, low = ctx_shape()
    return lax.ppermute(value, "ctx", [(i, i ^ 1) for i in range(high * low)])


def shift_high(value, step, wrap):
    high, low = ctx_shape()
    pairs = []
    for i in range(high * low):
        target = i // low + step
        if wrap or 0 <= target < high:
            pairs.append((i, (target % high) * low + i % low))
    return lax.ppermute(value, "ctx", pairs)


def ctx_gather(value, axis, causal):
    high, low = ctx_shape()
    at_high, at_low = ctx_place()
    got = [value] + [shift_high(value, step, not causal) for step in range(1, high)]
    slots = []
    for slot in range(high):
        block = jnp.zeros_like(value) if causal else value
        for place in range(high):
            if place >= slot or not causal:
                block = jnp.where(at_high == place, got[(place - slot) % high], block)
        slots.append(block)
    held = jnp.stack(slots, axis)
    if low == 2:
        other = swap_low(held)
        first = jnp.where(at_low == 0, held, other)
        second = jnp.where(at_low == 0, other, held)
        held = jnp.stack([first, second], axis + 1)
    shape = value.shape[:axis] + (high * low * value.shape[axis],) + value.shape[axis + 1 :]
    return held.reshape(shape)


def ctx_fold(value, axis, causal):
    high, low = ctx_shape()
    at_high, at_low = ctx_place()
    size = value.shape[axis] // (high * low)
    view = value.reshape(value.shape[:axis] + (high, low, size) + value.shape[axis + 1 :])
    if low == 2:
        mine = lax.dynamic_index_in_dim(view, at_low, axis + 1, False)
        other = swap_low(lax.dynamic_index_in_dim(view, 1 - at_low, axis + 1, False))
        held = (mine.astype(jnp.float32) + other.astype(jnp.float32)).astype(jnp.bfloat16)
    else:
        held = lax.squeeze(view, (axis + 1,))
    total = lax.dynamic_index_in_dim(held, at_high, axis, False).astype(jnp.float32)
    for step in range(1, high):
        target = at_high - step
        piece = lax.dynamic_index_in_dim(held, target % high, axis, False)
        total = total + shift_high(piece, -step, not causal).astype(jnp.float32)
    return total


def gather_rows(shards):
    count = lax.axis_size("ctx")
    rows = shards[0].shape[0] // count
    start = lax.axis_index("ctx") * rows
    parts = [lax.dynamic_slice_in_dim(s, start, rows, 0) for s in shards]
    part = jnp.concatenate(parts, axis=1) if len(parts) > 1 else parts[0]
    return lax.all_gather(part, ("fsdp", "ctx"), axis=0, tiled=True)


def scatter_rows(grads):
    part = lax.psum_scatter(grads, ("fsdp", "ctx"), scatter_dimension=0, tiled=True)
    return ctx_gather(part, 0, False).astype(jnp.float32)


def pair_total(partial):
    own = partial.astype(jnp.bfloat16)
    count = lax.axis_size("tp")
    total = own.astype(jnp.float32)
    for step in range(1, count):
        moved = lax.ppermute(own, "tp", [(i, (i + step) % count) for i in range(count)])
        total = total + moved.astype(jnp.float32)
    return total


def body(
    hidden_in,
    encoder_states,
    dec_segments,
    enc_segments,
    bucket_table,
    out_cotangent,
    self_gain,
    self_query,
    self_key,
    self_value,
    self_output,
    position_bias,
    cross_gain,
    cross_query,
    cross_key,
    cross_value,
    cross_output,
    ffn_gain,
    ffn_gate,
    ffn_up,
    ffn_down,
):
    shards = lax.axis_size("fsdp")
    seq_count, row_count, width = hidden_in.shape
    length = dec_segments.shape[1]
    heads_width = self_query.shape[1]
    units = ffn_gate.shape[1]
    bucket_rows, head_count = position_bias.shape
    bucket_count = bucket_rows * shards
    gain_rows = self_gain.shape[0]
    offset = lax.axis_index("ctx") * row_count

    small = jnp.concatenate([self_gain, cross_gain, ffn_gain, position_bias.reshape(-1)])
    small = lax.all_gather(small, "fsdp", axis=0, tiled=False)
    gain_self, gain_cross, gain_ffn = [
        small[:, gain_rows * i : gain_rows * (i + 1)].reshape(width).astype(jnp.float32)
        for i in range(3)
    ]
    bias_table = small[:, 3 * gain_rows :].reshape(bucket_count, head_count).astype(jnp.float32)
    hidden_all = ctx_gather(hidden_in, 1, True)
    encoder_all = ctx_gather(encoder_states, 1, False)
    self_weights = gather_rows([self_query, self_key, self_value])
    middle_weights = gather_rows(
        [cross_query, cross_key, cross_value, self_output.T, cross_output.T]
    )
    ffn_weights = gather_rows([ffn_gate, ffn_up, ffn_down.T])
    query_self = self_weights[:, :heads_width]
    pair_self = self_weights[:, heads_width:]
    query_cross = middle_weights[:, :heads_width]
    pair_cross = middle_weights[:, heads_width : 3 * heads_width]
    output_self = middle_weights[:, 3 * heads_width : 4 * heads_width]
    output_cross = middle_weights[:, 4 * heads_width :]
    gate_up = ffn_weights[:, : 2 * units]
    down = ffn_weights[:, 2 * units :]

    query_docs = lax.dynamic_slice_in_dim(dec_segments, offset, row_count, 1)[:, None, :]
    dec_docs = dec_segments[:, :, None]
    enc_docs = enc_segments[:, :, None]
    bucket_onehot = (
        bucket_table[:, None] == jnp.arange(bucket_count, dtype=jnp.int32)[None, :]
    ).astype(jnp.float32)
    distance_bias = jnp.dot(bucket_onehot, bias_table, precision=lax.Precision.HIGHEST).T
    padded = jnp.concatenate([jnp.zeros_like(distance_bias), distance_bias], axis=1)
    lines = lax.dynamic_slice_in_dim(padded, offset, row_count + length, 1)
    lines = lines.reshape(head_count // 2, 2, row_count + length)
    lines = jnp.concatenate([lines, jnp.zeros_like(lines), jnp.zeros_like(lines),
                             jnp.zeros_like(lines)], axis=1)
    place = jnp.full((1, 1), offset, jnp.int32)

    source = hidden_in.astype(jnp.float32)
    unit_one, inverse_one, normed_one = rms_forward(source, gain_self)
    unused_unit, unused_inverse, normed_all = rms_forward(
        hidden_all.astype(jnp.float32), gain_self
    )
    queries_one = mm(normed_one, query_self).astype(jnp.bfloat16)
    pair_one = mm(normed_all, pair_self).astype(jnp.bfloat16)
    attended_one, logs_one = attend_forward(
        queries_one, pair_one, query_docs, dec_docs, place, lines
    )
    after_one = source + pair_total(mm_back(attended_one, output_self))

    pair_two = mm(encoder_all, pair_cross).astype(jnp.bfloat16)
    unit_two, inverse_two, normed_two = rms_forward(after_one, gain_cross)
    queries_two = mm(normed_two, query_cross).astype(jnp.bfloat16)
    attended_two, logs_two = attend_forward(queries_two, pair_two, query_docs, enc_docs)
    after_two = after_one + pair_total(mm_back(attended_two, output_cross))

    grad_units = mm(out_cotangent, down)
    unit_three, inverse_three, normed_three = rms_forward(after_two, gain_ffn)
    both_rows = mm(normed_three, gate_up)
    gate_rows = both_rows[..., :units]
    up_rows = both_rows[..., units:]
    activated, gelu_pull = jax.vjp(lambda v: jax.nn.gelu(v, approximate=True), gate_rows)
    hidden_units = (activated * up_rows).astype(jnp.bfloat16)
    grad_gate_rows = gelu_pull(grad_units * up_rows)[0].astype(jnp.bfloat16)
    grad_up_rows = (grad_units * activated).astype(jnp.bfloat16)
    grad_both = jnp.concatenate([grad_gate_rows, grad_up_rows], axis=-1)
    grad_normed = pair_total(mm_back(grad_both, gate_up))
    layer_output = after_two + pair_total(mm_back(hidden_units, down))
    grads_ffn = scatter_rows(
        jnp.concatenate(
            [weight_grad(normed_three, grad_both), weight_grad(out_cotangent, hidden_units)],
            axis=1,
        )
    )
    grad_from, grad_gain_ffn = rms_backward(grad_normed, unit_three, inverse_three, gain_ffn)
    grad_res = out_cotangent.astype(jnp.float32) + grad_from

    grad_low = grad_res.astype(jnp.bfloat16)
    grad_attended = mm(grad_low, output_cross).astype(jnp.bfloat16)
    grad_out_cross = weight_grad(grad_low, attended_two)
    grad_q_two, grad_k_two, grad_v_two = attend_backward(
        queries_two, pair_two, query_docs, enc_docs, attended_two, logs_two, grad_attended
    )
    grad_normed = pair_total(mm_back(grad_q_two, query_cross))
    grad_pair_two = jnp.concatenate([grad_k_two, grad_v_two], axis=-1)
    grad_query_cross = weight_grad(normed_two, grad_q_two)
    grad_pair_cross = weight_grad(encoder_all, grad_pair_two)
    folded_two = ctx_fold(grad_pair_two, 1, False).astype(jnp.bfloat16)
    grad_states = pair_total(mm_back(folded_two, pair_cross))
    grad_from, grad_gain_cross = rms_backward(grad_normed, unit_two, inverse_two, gain_cross)
    grad_res = grad_res + grad_from

    grad_low = grad_res.astype(jnp.bfloat16)
    grad_attended = mm(grad_low, output_self).astype(jnp.bfloat16)
    grad_out_self = weight_grad(grad_low, attended_one)
    grads_middle = scatter_rows(
        jnp.concatenate([grad_query_cross, grad_pair_cross, grad_out_self, grad_out_cross], axis=1)
    )
    grad_q_one, grad_k_one, grad_v_one, line_grads = attend_backward(
        queries_one, pair_one, query_docs, dec_docs, attended_one, logs_one, grad_attended,
        place, lines,
    )
    grad_pair_one = jnp.concatenate([grad_k_one, grad_v_one], axis=-1)
    folded_one = ctx_fold(grad_pair_one, 1, True).astype(jnp.bfloat16)
    grads_self = scatter_rows(
        jnp.concatenate(
            [weight_grad(normed_one, grad_q_one), weight_grad(normed_all, grad_pair_one)], axis=1
        )
    )
    grad_normed = pair_total(
        mm_back(grad_q_one, query_self) + mm_back(folded_one, pair_self)
    )
    grad_from, grad_gain_self = rms_backward(grad_normed, unit_one, inverse_one, gain_self)
    grad_input = (grad_res + grad_from).astype(jnp.bfloat16)

    line_grads = line_grads[:, :2].reshape(head_count, row_count + length)
    spread = lax.dynamic_update_slice_in_dim(
        jnp.zeros((head_count, 2 * length), jnp.float32), line_grads, offset, 1
    )[:, length:]
    grad_bias = jnp.dot(spread, bucket_onehot, precision=lax.Precision.HIGHEST).T
    totals = jnp.concatenate(
        [grad_gain_self, grad_gain_cross, grad_gain_ffn, grad_bias.reshape(-1)]
    )
    totals = lax.psum(totals, ("fsdp", "ctx"))
    shard = lax.axis_index("fsdp")
    gain_grads = [
        lax.dynamic_slice_in_dim(totals, width * i + shard * gain_rows, gain_rows, 0)
        for i in range(3)
    ]
    bias_grad = lax.dynamic_slice_in_dim(
        totals, 3 * width + shard * bucket_rows * head_count, bucket_rows * head_count, 0
    ).reshape(bucket_rows, head_count)
    hw = heads_width
    return (
        layer_output.astype(jnp.bfloat16),
        grad_input,
        grad_states.astype(jnp.bfloat16),
        gain_grads[0],
        grads_self[:, :hw],
        grads_self[:, hw : 2 * hw],
        grads_self[:, 2 * hw :],
        grads_middle[:, 3 * hw : 4 * hw].T,
        bias_grad,
        gain_grads[1],
        grads_middle[:, :hw],
        grads_middle[:, hw : 2 * hw],
        grads_middle[:, 2 * hw : 3 * hw],
        grads_middle[:, 4 * hw :].T,
        gain_grads[2],
        grads_ffn[:, :units],
        grads_ffn[:, units : 2 * units],
        grads_ffn[:, 2 * units :].T,
    )


def solution(mesh):
    in_specs = (
        P("fsdp", "ctx", None),
        P("fsdp", "ctx", None),
        P("fsdp", None),
        P("fsdp", None),
        P(),
        P("fsdp", "ctx", None),
        P("fsdp"),
        P("fsdp", "tp"),
        P("fsdp", "tp"),
        P("fsdp", "tp"),
        P("tp", "fsdp"),
        P("fsdp", "tp"),
        P("fsdp"),
        P("fsdp", "tp"),
        P("fsdp", "tp"),
        P("fsdp", "tp"),
        P("tp", "fsdp"),
        P("fsdp"),
        P("fsdp", "tp"),
        P("fsdp", "tp"),
        P("tp", "fsdp"),
    )
    out_specs = (
        P("fsdp", "ctx", None),
        P("fsdp", "ctx", None),
        P("fsdp", "ctx", None),
        P("fsdp"),
        P("fsdp", "tp"),
        P("fsdp", "tp"),
        P("fsdp", "tp"),
        P("tp", "fsdp"),
        P("fsdp", "tp"),
        P("fsdp"),
        P("fsdp", "tp"),
        P("fsdp", "tp"),
        P("fsdp", "tp"),
        P("tp", "fsdp"),
        P("fsdp"),
        P("fsdp", "tp"),
        P("fsdp", "tp"),
        P("tp", "fsdp"),
    )
    return jax.shard_map(body, mesh=mesh, in_specs=in_specs, out_specs=out_specs, check_vma=False)
```

time: 1460 us -> 648 us (0.44)
  waiting for transfers between devices: 965 us -> 283 us
  local copies, waits for them, and re-layouts: 163 us -> 60.7 us
  matrix products: 161 us -> 61.8 us
  Pallas kernels: 0 us -> 64.3 us
  starting transfers between devices: 2.81 us -> 21.7 us
    reduce_scatter x13 -> x3, waiting for transfers between devices: 410 us -> 35.1 us  [scatter_rows(): lax.psum_scatter(grads, ('fsdp', 'ctx'), scatter_dimension=0, tiled=True)]
    all_gather x15 -> x3, waiting for transfers between devices: 325 us -> 27 us  [gather_rows(): return lax.all_gather(part, ('fsdp', 'ctx'), axis=0, tiled=True)]
    psum x6 -> x0, waiting for transfers between devices: 223 us -> none  [the longest x3 99.2 us: branch_total(): lax.psum(partial_value.astype(jnp.bfloat16), 'tp').astype(jnp.float32)]
    ppermute x0 -> x21, waiting for transfers between devices: none -> 221 us  [the longest x7 130 us: pair_total(): lax.ppermute(own, 'tp', [(i, (i + step) % count) for i in range(count)])]
    dot_general x63 -> x26, matrix products: 161 us -> 61.8 us  [the longest x8 26.1 us: mm(): lax.dot_general(lhs, rhs, (((lhs.ndim - 1,), (0,)), ((), ())), preferred_...]
    pallas_call x0 -> x4, Pallas kernels: none -> 64.3 us  [the longest x2 38.7 us: attend_backward(): pl.pallas_call(functools.partial(backward_kernel, causal), grid=(pairs, s...]
    psum x1, blocking collectives: 6.55 us -> 58.6 us  [body(): totals = lax.psum(totals, ('fsdp', 'ctx'))]
    all_gather x4 -> x0, blocking collectives: 45.4 us -> none  [the longest x1 12.7 us: body(): lax.all_gather(self_gain, 'fsdp', axis=0, tiled=True)]
  transfers between devices with their start and end apart: 36 -> 27, of which waited for: 32 -> 16; matrix products, arithmetic and copies ran while one was open for 22% -> 20% of each run, Pallas kernels for 0% -> 4%
where the time goes in v1:
time: 648 us; the launch traced here: 644 us
  waiting for transfers between devices  283 us (44%)
  blocking collectives  70.8 us (11%)
  other arithmetic  64.4 us (10%)
  Pallas kernels  64.3 us (10%)
  matrix products  61.8 us (10%)
  local copies, waits for them, and re-layouts  60.7 us (9%)
  starting transfers between devices  21.7 us (3%)
  between operations  16.6 us (3%)
    ppermute x7, waiting for transfers between devices, pair_total(): lax.ppermute(own, 'tp', [(i, (i + step) % count) for i in range(count)])  130 us
    ppermute x7, waiting for transfers between devices, shift_high(): return lax.ppermute(value, 'ctx', pairs)  90.1 us
    psum x1, blocking collectives, body(): totals = lax.psum(totals, ('fsdp', 'ctx'))  58.6 us
    pallas_call x2, Pallas kernels, attend_backward(): pl.pallas_call(functools.partial(backward_kernel, causal), grid=(pairs, s...  38.7 us
    unnamed x192, local copies, waits for them, and re-layouts  37.8 us
    reduce_scatter x3, waiting for transfers between devices, scatter_rows(): lax.psum_scatter(grads, ('fsdp', 'ctx'), scatter_dimension=0, tiled=True)  35.1 us
    all_gather x3, waiting for transfers between devices, gather_rows(): return lax.all_gather(part, ('fsdp', 'ctx'), axis=0, tiled=True)  27 us
    dot_general x8, matrix products, mm(): lax.dot_general(lhs, rhs, (((lhs.ndim - 1,), (0,)), ((), ())), preferred_...  26.1 us
  transfers between devices with their start and end apart: 27, of which 16 were waited for; matrix products, arithmetic and copies ran while one was open for 20% of the time, Pallas kernels for 4%

profile of v1, /device:TPU:0, one launch (start us, length us, event | category | flops | bytes accessed | tf_op | source)
XLA Modules:
  0.0 643.7 jit_solution(7736277652560168012)
XLA Ops:
  16.9 4.9 collective-permute-start
  22.0 30.2 %collective-permute-done = bf16[2,256,1024]{2,1,0:T(8,128)(2,1)S(1)} collective-permute-done((bf16[2,256,1024]{2,1,0:T(8,128)(2,1)S(1)}, bf16[2,256,1024]{2,1,0:T(8,128)(2,1)S(1)}, u32[]{:S(2)}, u32[]{:S(2)}) %collective-permute-start) | collective-permute-done | bytes 1048608 | tf_op jit(solution)/shard_map/ppermute | solution.py:339
  55.9 12.3 %all-reduce.1 = bf16[3328]{0:T(1024)(128)(2,1)S(1)} all-reduce(bf16[3328]{0:T(1024)(128)(2,1)S(1)} %dynamic-update-slice), channel_id=2, replica_groups=mesh['fsdp'=4,'ctx'=4,'tp'=2] {'fsdp'}, use_global_device_ids=true, to_apply=%add.1 | all-reduce | flops 3328 | bytes 13312
  82.7 7.4 %convolution_convert_fusion.refs_5_.refs_6_ = bf16[2,1024,1024]{2,1,0:T(8,128)(2,1)S(1)} fusion(bf16[2,1024,1024]{2,1,0:T(8,128)(2,1)} %fusion.1, bf16[1024,1536]{1,0:T(8,128)(2,1)} %all-gather.5.cloned.1.call-done), kind=kOutput, calls=%fused_computation.40 | convolution fusion | flops 4297064448 | bytes 10485760 | tf_op jit(solution)/shard_map/dot_general | solution.py:288
  92.9 16.7 %attend_forward.2 = (bf16[2,256,512]{2,1,0:T(8,128)(2,1)S(1)}, f32[2,4,8,256]{3,2,1,0:T(8,128)S(1)}) custom-call(s32[1,1]{1,0:T(1,128)} %bitcast.refs_0_, f32[4,8,1280]{2,1,0:T(8,128)S(1)} %maximum_maximum_fusion.refs_1_, s32[2,1,256]{2,1,0:T(1,128)S(1)} %broadcast_in_dim.14.refs_2_.refs_0_, s32[2,1024,1]{2,1,0:T(8,128)S(1)} %copy.97.refs_3_, ...), custom_call_target="tpu_custom_call" | custom-call | flops 2147483648 | bytes 5242880 | tf_op jit(solution)/shard_map/attend_forward/pallas_call | solution.py:230
  110.4 17.1 %all-gather.7.cloned.1.call-done = bf16[1024,2560]{1,0:T(8,128)(2,1)} async-done(((bf16[64,2560]{1,0:T(8,128)(2,1)}), bf16[1024,2560]{1,0:T(8,128)(2,1)}) %all-gather.7.cloned.1.call-update) | async-done | bytes 5242896 | tf_op jit(solution)/shard_map/all_gather | solution.py:388
  138.3 17.7 %collective-permute-done.2 = bf16[2,256,1024]{2,1,0:T(8,128)(2,1)} collective-permute-done((bf16[2,256,1024]{2,1,0:T(8,128)(2,1)}, bf16[2,256,1024]{2,1,0:T(8,128)(2,1)}, u32[]{:S(2)}, u32[]{:S(2)}) %collective-permute-start.2) | collective-permute-done | bytes 1048608 | tf_op jit(solution)/shard_map/ppermute | solution.py:401
  159.7 9.0 %attend_forward.3 = (bf16[2,256,512]{2,1,0:T(8,128)(2,1)S(1)}, f32[2,4,8,256]{3,2,1,0:T(8,128)S(1)}) custom-call(s32[2,1,256]{2,1,0:T(1,128)S(1)} %broadcast_in_dim.14.refs_2_.refs_0_, s32[2,512,1]{2,1,0:T(8,128)S(1)} %copy-done.4, bf16[2,256,512]{2,1,0:T(8,128)(2,1)S(1)} %convolution_convert_fusion.7.refs_2_, ...), custom_call_target="tpu_custom_call" | custom-call | flops 1073741824 | bytes 3145728 | tf_op jit(solution)/shard_map/attend_forward/pallas_call | solution.py:230
  171.0 23.1 %collective-permute-done.5 = bf16[2,256,1024]{2,1,0:T(8,128)(2,1)S(1)} collective-permute-done((bf16[2,256,1024]{2,1,0:T(8,128)(2,1)S(1)}, bf16[2,256,1024]{2,1,0:T(8,128)(2,1)S(1)}, u32[]{:S(2)}, u32[]{:S(2)}) %collective-permute-start.5) | collective-permute-done | bytes 1048608 | tf_op jit(solution)/shard_map/ppermute | solution.py:401
  195.8 9.9 %all-gather.9.cloned.1.call-done = bf16[1024,4224]{1,0:T(8,128)(2,1)} async-done(((bf16[64,4224]{1,0:T(8,128)(2,1)}), bf16[1024,4224]{1,0:T(8,128)(2,1)}) %all-gather.9.cloned.1.call-update) | async-done | bytes 8650768 | tf_op jit(solution)/shard_map/all_gather | solution.py:388
  205.7 6.6 %fusion.3 = f32[2,256,2816]{2,1,0:T(8,128)S(1)} fusion(bf16[1024,4224]{1,0:T(8,128)(2,1)} %all-gather.9.cloned.1.call-done, f32[2,256,1024]{2,1,0:T(8,128)} %get-tuple-element.101, f32[1024]{0:T(1024)S(1)} %bitcast.225, f32[2,256]{1,0:T(2,128)S(1)} %add_rsqrt_fusion.1), kind=kOutput, calls=%fused_computation.10 | convolution fusion | flops 2954362880 | bytes 13637632 | tf_op jit(solution)/shard_map/dot_general | solution.py:288
  212.3 4.8 fusion.16
  224.3 22.1 %collective-permute-done.7 = bf16[2,256,1024]{2,1,0:T(8,128)(2,1)S(1)} collective-permute-done((bf16[2,256,1024]{2,1,0:T(8,128)(2,1)S(1)}, bf16[2,256,1024]{2,1,0:T(8,128)(2,1)S(1)}, u32[]{:S(2)}, u32[]{:S(2)}) %collective-permute-start.7) | collective-permute-done | bytes 1048608 | tf_op jit(solution)/shard_map/ppermute | solution.py:401
  247.7 20.5 %collective-permute-done.6 = bf16[2,256,1024]{2,1,0:T(8,128)(2,1)S(1)} collective-permute-done((bf16[2,256,1024]{2,1,0:T(8,128)(2,1)S(1)}, bf16[2,256,1024]{2,1,0:T(8,128)(2,1)S(1)}, u32[]{:S(2)}, u32[]{:S(2)}) %collective-permute-start.6) | collective-permute-done | bytes 1048608 | tf_op jit(solution)/shard_map/ppermute | solution.py:401
  272.4 11.2 %attend_backward.2 = (bf16[2,256,512]{2,1,0:T(8,128)(2,1)S(1)}, bf16[2,512,512]{2,1,0:T(8,128)(2,1)S(1)}, bf16[2,512,512]{2,1,0:T(8,128)(2,1)S(1)}) custom-call(s32[2,1,256]{2,1,0:T(1,128)S(1)} %broadcast_in_dim.14.refs_2_.refs_0_, s32[2,512,1]{2,1,0:T(8,128)S(1)} %copy-done.5, bf16[2,256,512]{2,1,0:T(8,128)(2,1)S(1)} %copy-done.21, ...), custom_call_target="tpu_custom_call" | custom-call | flops 2684354560 | bytes 6291456 | tf_op jit(solution)/shard_map/attend_backward/pallas_call | solution.py:270
  285.8 23.1 %collective-permute-done.8 = bf16[2,256,1024]{2,1,0:T(8,128)(2,1)S(1)} collective-permute-done((bf16[2,256,1024]{2,1,0:T(8,128)(2,1)S(1)}, bf16[2,256,1024]{2,1,0:T(8,128)(2,1)S(1)}, u32[]{:S(2)}, u32[]{:S(2)}) %collective-permute-start.8) | collective-permute-done | bytes 1048608 | tf_op jit(solution)/shard_map/ppermute | solution.py:401
  313.5 27.5 %attend_backward.3 = (bf16[2,256,512]{2,1,0:T(8,128)(2,1)S(1)}, bf16[2,1024,512]{2,1,0:T(8,128)(2,1)S(1)}, bf16[2,1024,512]{2,1,0:T(8,128)(2,1)S(1)}, f32[4,8,1280]{2,1,0:T(8,128)S(1)}) custom-call(s32[1,1]{1,0:T(1,128)} %bitcast.refs_0_, f32[4,8,1280]{2,1,0:T(8,128)S(1)} %maximum_maximum_fusion.refs_1_, s32[2,1,256]{2,1,0:T(1,128)S(1)} %broadcast_in_dim.14.refs_2_.refs_0_, ...), custom_call_target="tpu_custom_call" | custom-call | flops 5368709120 | bytes 10485760 | tf_op jit(solution)/shard_map/attend_backward/pallas_call | solution.py:270
  343.5 4.8 bitcast_convert_fusion.3
  351.2 4.7 copy.149
  366.4 13.7 %pad_maximum_fusion.1 = bf16[1024,2560]{0,1:T(8,128)(2,1)} fusion(bf16[1024,512]{0,1:T(8,128)(2,1)S(1)} %bitcast_convert_fusion.4, bf16[1024,512]{0,1:T(8,128)(2,1)S(1)} %bitcast_convert_fusion.5, bf16[1024,1024]{0,1:T(8,128)(2,1)S(1)} %bitcast_convert_fusion.2, bf16[1024,512]{0,1:T(8,128)(2,1)S(1)} %bitcast_convert_fusion.6), kind=kLoop, calls=%fused_computation.8 | loop fusion | flops 20971520 | bytes 10485760 | tf_op jit(solution)/shard_map/concatenate | solution.py:534
  380.1 7.9 %copy.151 = bf16[1024,2560]{1,0:T(8,128)(2,1)} copy(bf16[1024,2560]{0,1:T(8,128)(2,1)} %pad_maximum_fusion.1) | data formatting | bytes 10485760
  392.1 3.7 bitcast_convert_fusion
  395.8 3.8 pad_maximum_fusion
  399.6 4.0 constant_dynamic-slice_fusion.3
  423.2 20.3 %collective-permute-done.10 = bf16[2,256,1024]{2,1,0:T(8,128)(2,1)} collective-permute-done((bf16[2,256,1024]{2,1,0:T(8,128)(2,1)}, bf16[2,256,1024]{2,1,0:T(8,128)(2,1)}, u32[]{:S(2)}, u32[]{:S(2)}) %collective-permute-start.10) | collective-permute-done | bytes 1048608 | tf_op jit(solution)/shard_map/ppermute | solution.py:339
  448.3 5.6 collective-permute-done.13
  459.1 23.1 %collective-permute-done.14 = bf16[2,128,1024]{2,1,0:T(8,128)(2,1)} collective-permute-done((bf16[2,128,1024]{2,1,0:T(8,128)(2,1)}, bf16[2,128,1024]{2,1,0:T(8,128)(2,1)}, u32[]{:S(2)}, u32[]{:S(2)}) %collective-permute-start.14) | collective-permute-done | bytes 524320 | tf_op jit(solution)/shard_map/ppermute | solution.py:401
  486.8 58.6 %psum.7 = f32[3328]{0:T(1024)} all-reduce(f32[3328]{0:T(1024)S(1)} %pad_maximum_fusion.18), channel_id=1, replica_groups=mesh['fsdp'=4,'ctx'=4,'tp'=2] {'fsdp','ctx'}, use_global_device_ids=true, to_apply=%region_10.11 | all-reduce | flops 3328 | bytes 26624 | tf_op jit(solution)/shard_map/psum | solution.py:561
  545.4 9.0 %collective-permute-done.15 = bf16[64,1536]{1,0:T(8,128)(2,1)S(1)} collective-permute-done((bf16[64,1536]{1,0:T(8,128)(2,1)}, bf16[64,1536]{1,0:T(8,128)(2,1)S(1)}, u32[]{:S(2)}, u32[]{:S(2)}) %collective-permute-start.15) | collective-permute-done | bytes 196640 | tf_op jit(solution)/shard_map/ppermute | solution.py:339
  563.7 12.5 %collective-permute-done.17 = bf16[64,2560]{1,0:T(8,128)(2,1)S(1)} collective-permute-done((bf16[64,2560]{1,0:T(8,128)(2,1)}, bf16[64,2560]{1,0:T(8,128)(2,1)S(1)}, u32[]{:S(2)}, u32[]{:S(2)}) %collective-permute-start.17) | collective-permute-done | bytes 327712 | tf_op jit(solution)/shard_map/ppermute | solution.py:339
  577.8 35.1 %reduce-scatter.8.cloned.1.call-done = bf16[64,4224]{1,0:T(8,128)(2,1)} async-done(((bf16[1024,4224]{1,0:T(8,128)(2,1)}), bf16[64,4224]{1,0:T(8,128)(2,1)}) %reduce-scatter.8.cloned.1.call-update) | async-done | bytes 540688 | tf_op jit(solution)/shard_map/reduce_scatter | solution.py:392
  614.7 12.6 %collective-permute-done.19 = bf16[64,4224]{1,0:T(8,128)(2,1)S(1)} collective-permute-done((bf16[64,4224]{1,0:T(8,128)(2,1)}, bf16[64,4224]{1,0:T(8,128)(2,1)S(1)}, u32[]{:S(2)}, u32[]{:S(2)}) %collective-permute-start.19) | collective-permute-done | bytes 540704 | tf_op jit(solution)/shard_map/ppermute | solution.py:339
  (348 shorter events, 143.9 us)
Async XLA Ops:
  7.2 75.5 %all-gather.5.cloned.1.call-start = ((), (), s32[]{:S(2)}) async-start(), calls=%async_computation.3 | async-start | bytes 3342336 | tf_op jit(solution)/shard_map/all_gather | solution.py:388
  9.8 117.7 %all-gather.7.cloned.1.call-start = ((), (), s32[]{:S(2)}) async-start(), calls=%async_computation.4 | async-start | bytes 5570560 | tf_op jit(solution)/shard_map/all_gather | solution.py:388
  14.5 191.2 %all-gather.9.cloned.1.call-start = ((), (), s32[]{:S(2)}) async-start(), calls=%async_computation.5 | async-start | bytes 9191424 | tf_op jit(solution)/shard_map/all_gather | solution.py:388
  16.8 528.6 %reduce-scatter.10.cloned.1.call-start = ((), (), s32[]{:S(2)}) async-start(), calls=%async_computation.7 | async-start | bytes 3342336 | tf_op jit(solution)/shard_map/reduce_scatter | solution.py:392
  16.9 35.3 %collective-permute-start = (bf16[2,256,1024]{2,1,0:T(8,128)(2,1)S(1)}, bf16[2,256,1024]{2,1,0:T(8,128)(2,1)S(1)}, u32[]{:S(2)}, u32[]{:S(2)}) collective-permute-start(bf16[2,256,1024]{2,1,0:T(8,128)(2,1)S(1)} %copy-done.31), channel_id=1, source_target_pairs={{0,4},{2,6},{1,5},{3,7},{8,12},{10,14},{9,13},{11,15},{16,20},{18,... | collective-permute-start | bytes 3145736 | tf_op jit(solution)/shard_map/ppermute | solution.py:339
  21.8 48.0 %collective-permute-start.3 = (bf16[2,128,1024]{2,1,0:T(8,128)(2,1)}, bf16[2,128,1024]{2,1,0:T(8,128)(2,1)S(1)}, u32[]{:S(2)}, u32[]{:S(2)}) collective-permute-start(bf16[2,128,1024]{2,1,0:T(8,128)(2,1)} %param.22), channel_id=1, source_target_pairs={{0,4},{2,6},{4,0},{6,2},{1,5},{3,7},{5,1},{7,3},{8,12},{10,14},{12... | collective-permute-start | bytes 1572872 | tf_op jit(solution)/shard_map/ppermute | solution.py:339
  54.3 18.0 %collective-permute-start.1 = (bf16[2,2,256,1024]{3,2,1,0:T(8,128)(2,1)}, bf16[2,2,256,1024]{3,2,1,0:T(8,128)(2,1)}, u32[]{:S(2)}, u32[]{:S(2)}) collective-permute-start(bf16[2,2,256,1024]{3,2,1,0:T(8,128)(2,1)} %pad_maximum_fusion.4), channel_id=1, source_target_pairs={{0,2},{2,0},{4,6},{6,4},{1,3},{3,1},{5,7},{7,5},{8,10},{10,8},{12,... | collective-permute-start | bytes 6291464 | tf_op jit(solution)/shard_map/ppermute | solution.py:329
  72.2 60.7 %collective-permute-start.4 = (bf16[2,2,128,1024]{3,2,0,1:T(8,128)(2,1)}, bf16[2,2,128,1024]{3,2,0,1:T(8,128)(2,1)}, u32[]{:S(2)}, u32[]{:S(2)}) collective-permute-start(bf16[2,2,128,1024]{3,2,0,1:T(8,128)(2,1)} %pad_maximum_fusion.12), channel_id=1, source_target_pairs={{0,2},{2,0},{4,6},{6,4},{1,3},{3,1},{5,7},{7,5},{8,10},{10,8},{12,... | collective-permute-start | bytes 3145736 | tf_op jit(solution)/shard_map/ppermute | solution.py:329
  130.4 25.6 %collective-permute-start.2 = (bf16[2,256,1024]{2,1,0:T(8,128)(2,1)}, bf16[2,256,1024]{2,1,0:T(8,128)(2,1)}, u32[]{:S(2)}, u32[]{:S(2)}) collective-permute-start(bf16[2,256,1024]{2,1,0:T(8,128)(2,1)} %convolution_convert_fusion.4), channel_id=1, source_target_pairs={{0,1},{1,0},{2,3},{3,2},{4,5},{5,4},{6,7},{7,6},{8,9},{9,8},{10,11... | collective-permute-start | bytes 3145736 | tf_op jit(solution)/shard_map/ppermute | solution.py:401
  158.2 35.8 %copy-start.24 = (f32[2,256,1024]{2,1,0:T(8,128)}, f32[2,256,1024]{2,1,0:T(8,128)S(1)}, u32[]{:S(2)}) copy-start(f32[2,256,1024]{2,1,0:T(8,128)S(1)} %get-tuple-element.103) | copy-start | bytes 6291460
  158.2 152.0 %copy-start.59 = (f32[2,256]{1,0:T(2,128)}, f32[2,256]{1,0:T(2,128)S(1)}, u32[]{:S(2)}) copy-start(f32[2,256]{1,0:T(2,128)S(1)} %add_rsqrt_fusion.2) | copy-start | bytes 6148
  169.4 24.6 %collective-permute-start.5 = (bf16[2,256,1024]{2,1,0:T(8,128)(2,1)S(1)}, bf16[2,256,1024]{2,1,0:T(8,128)(2,1)S(1)}, u32[]{:S(2)}, u32[]{:S(2)}) collective-permute-start(bf16[2,256,1024]{2,1,0:T(8,128)(2,1)S(1)} %convolution_convert_fusion.3), channel_id=1, source_target_pairs={{0,1},{1,0},{2,3},{3,2},{4,5},{5,4},{6,7},{7,6},{8,9},{9,8},{10,11... | collective-permute-start | bytes 3145736 | tf_op jit(solution)/shard_map/ppermute | solution.py:401
  195.7 72.5 %copy-start.61 = (f32[2,256]{1,0:T(2,128)}, f32[2,256]{1,0:T(2,128)S(1)}, u32[]{:S(2)}) copy-start(f32[2,256]{1,0:T(2,128)S(1)} %add_rsqrt_fusion.1) | copy-start | bytes 6148
  220.3 26.1 %collective-permute-start.7 = (bf16[2,256,1024]{2,1,0:T(8,128)(2,1)S(1)}, bf16[2,256,1024]{2,1,0:T(8,128)(2,1)S(1)}, u32[]{:S(2)}, u32[]{:S(2)}) collective-permute-start(bf16[2,256,1024]{2,1,0:T(8,128)(2,1)S(1)} %fusion.34), channel_id=1, source_target_pairs={{0,1},{1,0},{2,3},{3,2},{4,5},{5,4},{6,7},{7,6},{8,9},{9,8},{10,11... | collective-permute-start | bytes 3145736 | tf_op jit(solution)/shard_map/ppermute | solution.py:401
  223.7 44.5 %collective-permute-start.6 = (bf16[2,256,1024]{2,1,0:T(8,128)(2,1)S(1)}, bf16[2,256,1024]{2,1,0:T(8,128)(2,1)S(1)}, u32[]{:S(2)}, u32[]{:S(2)}) collective-permute-start(bf16[2,256,1024]{2,1,0:T(8,128)(2,1)S(1)} %fusion.33), channel_id=1, source_target_pairs={{0,1},{1,0},{2,3},{3,2},{4,5},{5,4},{6,7},{7,6},{8,9},{9,8},{10,11... | collective-permute-start | bytes 3145736 | tf_op jit(solution)/shard_map/ppermute | solution.py:401
  270.3 40.0 %copy-start.29 = (f32[2,256,1024]{2,1,0:T(8,128)}, f32[2,256,1024]{2,1,0:T(8,128)S(1)}, u32[]{:S(2)}) copy-start(f32[2,256,1024]{2,1,0:T(8,128)S(1)} %get-tuple-element.123) | copy-start | bytes 6291460
  284.4 24.6 %collective-permute-start.8 = (bf16[2,256,1024]{2,1,0:T(8,128)(2,1)S(1)}, bf16[2,256,1024]{2,1,0:T(8,128)(2,1)S(1)}, u32[]{:S(2)}, u32[]{:S(2)}) collective-permute-start(bf16[2,256,1024]{2,1,0:T(8,128)(2,1)S(1)} %convolution_convert_fusion.2), channel_id=1, source_target_pairs={{0,1},{1,0},{2,3},{3,2},{4,5},{5,4},{6,7},{7,6},{8,9},{9,8},{10,11... | collective-permute-start | bytes 3145736 | tf_op jit(solution)/shard_map/ppermute | solution.py:401
  355.9 206.3 %reduce-scatter.12.cloned.1.call-start = ((), (), s32[]{:S(2)}) async-start(), calls=%async_computation.8 | async-start | bytes 5570560 | tf_op jit(solution)/shard_map/reduce_scatter | solution.py:392
  388.0 224.9 %reduce-scatter.8.cloned.1.call-start = ((), (), s32[]{:S(2)}) async-start(), calls=%async_computation.6 | async-start | bytes 9191424 | tf_op jit(solution)/shard_map/reduce_scatter | solution.py:392
  405.2 4.5 collective-permute-start.9
  408.1 8.5 %collective-permute-start.12 = (bf16[2,2,128,1024]{3,2,0,1:T(8,128)(2,1)}, bf16[2,2,128,1024]{3,2,0,1:T(8,128)(2,1)}, u32[]{:S(2)}, u32[]{:S(2)}) collective-permute-start(bf16[2,2,128,1024]{3,2,0,1:T(8,128)(2,1)} %bitcast.205), channel_id=1, source_target_pairs={{0,2},{2,0},{4,6},{6,4},{1,3},{3,1},{5,7},{7,5},{8,10},{10,8},{12,... | collective-permute-start | bytes 3145736 | tf_op jit(solution)/shard_map/ppermute | solution.py:329
  415.3 28.2 %collective-permute-start.10 = (bf16[2,256,1024]{2,1,0:T(8,128)(2,1)}, bf16[2,256,1024]{2,1,0:T(8,128)(2,1)}, u32[]{:S(2)}, u32[]{:S(2)}) collective-permute-start(bf16[2,256,1024]{2,1,0:T(8,128)(2,1)} %dynamic-slice_bitcast_fusion), channel_id=1, source_target_pairs={{4,0},{6,2},{5,1},{7,3},{12,8},{14,10},{13,9},{15,11},{20,16},{22,... | collective-permute-start | bytes 3145736 | tf_op jit(solution)/shard_map/ppermute | solution.py:339
  418.8 35.0 %collective-permute-start.13 = (bf16[2,128,1024]{2,1,0:T(8,128)(2,1)S(1)}, bf16[2,128,1024]{2,1,0:T(8,128)(2,1)S(1)}, u32[]{:S(2)}, u32[]{:S(2)}) collective-permute-start(bf16[2,128,1024]{2,1,0:T(8,128)(2,1)S(1)} %dynamic-slice_bitcast_fusion.1), channel_id=1, source_target_pairs={{0,4},{2,6},{4,0},{6,2},{1,5},{3,7},{5,1},{7,3},{8,12},{10,14},{12... | collective-permute-start | bytes 1572872 | tf_op jit(solution)/shard_map/ppermute | solution.py:339
  447.1 37.4 %collective-permute-start.11 = (bf16[2,256,1024]{2,1,0:T(8,128)(2,1)}, bf16[2,256,1024]{2,1,0:T(8,128)(2,1)}, u32[]{:S(2)}, u32[]{:S(2)}) collective-permute-start(bf16[2,256,1024]{2,1,0:T(8,128)(2,1)} %add_convert_fusion), channel_id=1, source_target_pairs={{0,1},{1,0},{2,3},{3,2},{4,5},{5,4},{6,7},{7,6},{8,9},{9,8},{10,11... | collective-permute-start | bytes 3145736 | tf_op jit(solution)/shard_map/ppermute | solution.py:401
  457.1 25.2 %collective-permute-start.14 = (bf16[2,128,1024]{2,1,0:T(8,128)(2,1)}, bf16[2,128,1024]{2,1,0:T(8,128)(2,1)}, u32[]{:S(2)}, u32[]{:S(2)}) collective-permute-start(bf16[2,128,1024]{2,1,0:T(8,128)(2,1)} %fusion.35), channel_id=1, source_target_pairs={{0,1},{1,0},{2,3},{3,2},{4,5},{5,4},{6,7},{7,6},{8,9},{9,8},{10,11... | collective-permute-start | bytes 1572872 | tf_op jit(solution)/shard_map/ppermute | solution.py:401
  459.1 27.7 %copy-start.65 = (f32[1024]{0:T(1024)S(1)}, f32[1024]{0:T(1024)}, u32[]{:S(2)}) copy-start(f32[1024]{0:T(1024)} %get-tuple-element.96) | copy-start | bytes 12292
  545.4 9.0 %collective-permute-start.15 = (bf16[64,1536]{1,0:T(8,128)(2,1)}, bf16[64,1536]{1,0:T(8,128)(2,1)S(1)}, u32[]{:S(2)}, u32[]{:S(2)}) collective-permute-start(bf16[64,1536]{1,0:T(8,128)(2,1)} %reduce-scatter.10.cloned.1.call-done), channel_id=1, source_target_pairs={{0,4},{2,6},{4,0},{6,2},{1,5},{3,7},{5,1},{7,3},{8,12},{10,14},{12... | collective-permute-start | bytes 589832 | tf_op jit(solution)/shard_map/ppermute | solution.py:339
  556.2 6.4 collective-permute-start.16
  562.2 14.0 %collective-permute-start.17 = (bf16[64,2560]{1,0:T(8,128)(2,1)}, bf16[64,2560]{1,0:T(8,128)(2,1)S(1)}, u32[]{:S(2)}, u32[]{:S(2)}) collective-permute-start(bf16[64,2560]{1,0:T(8,128)(2,1)} %reduce-scatter.12.cloned.1.call-done), channel_id=1, source_target_pairs={{0,4},{2,6},{4,0},{6,2},{1,5},{3,7},{5,1},{7,3},{8,12},{10,14},{12... | collective-permute-start | bytes 983048 | tf_op jit(solution)/shard_map/ppermute | solution.py:339
  576.4 38.1 %collective-permute-start.18 = (bf16[2,64,2560]{2,1,0:T(8,128)(2,1)S(1)}, bf16[2,64,2560]{2,1,0:T(8,128)(2,1)S(1)}, u32[]{:S(2)}, u32[]{:S(2)}) collective-permute-start(bf16[2,64,2560]{2,1,0:T(8,128)(2,1)S(1)} %pad_maximum_fusion.14), channel_id=1, source_target_pairs={{0,2},{2,0},{4,6},{6,4},{1,3},{3,1},{5,7},{7,5},{8,10},{10,8},{12,... | collective-permute-start | bytes 1966088 | tf_op jit(solution)/shard_map/ppermute | solution.py:329
  613.0 14.3 %collective-permute-start.19 = (bf16[64,4224]{1,0:T(8,128)(2,1)}, bf16[64,4224]{1,0:T(8,128)(2,1)S(1)}, u32[]{:S(2)}, u32[]{:S(2)}) collective-permute-start(bf16[64,4224]{1,0:T(8,128)(2,1)} %reduce-scatter.8.cloned.1.call-done), channel_id=1, source_target_pairs={{0,4},{2,6},{4,0},{6,2},{1,5},{3,7},{5,1},{7,3},{8,12},{10,14},{12... | collective-permute-start | bytes 1622024 | tf_op jit(solution)/shard_map/ppermute | solution.py:339
  627.5 3.6 collective-permute-start.20
  (81 other events, 641.6 us)
Sparse Core Ops, SparseCore 0:
  10.9 49.4 all-gather.4
  63.3 64.2 all-gather.6
  130.4 75.2 all-gather.8
  356.0 64.5 reduce-scatter.9
  424.3 77.3 reduce-scatter.11
  505.6 107.3 reduce-scatter.7

commit v2 on v1

--- a/solution.py
+++ b/solution.py
@@ -8,6 +8,8 @@
 
 EPSILON = 1e-06
 NEGATIVE = -1e30
+EXTRA = 16
+TINY = pl.CostEstimate(flops=1, bytes_accessed=1, transcendentals=0)
 LANES = 128
 CHUNK = 256
 NT = (((1,), (1,)), ((), ()))
@@ -238,11 +240,7 @@
         ],
         scratch_shapes=scratch,
         compiler_params=pltpu.CompilerParams(vmem_limit_bytes=40 * 1024 * 1024),
-        cost_estimate=pl.CostEstimate(
-            flops=seqs * pairs * 4 * 2 * rows * keys * 128,
-            bytes_accessed=4 * seqs * (rows + keys) * width,
-            transcendentals=seqs * pairs * 2 * rows * keys,
-        ),
+        cost_estimate=TINY,
         name="attend_forward",
     )(*args)
 
@@ -275,28 +273,106 @@
         out_shape=out_shape,
         scratch_shapes=scratch,
         compiler_params=pltpu.CompilerParams(vmem_limit_bytes=40 * 1024 * 1024),
-        cost_estimate=pl.CostEstimate(
-            flops=seqs * pairs * 10 * 2 * rows * keys * 128,
-            bytes_accessed=8 * seqs * (rows + keys) * width,
-            transcendentals=seqs * pairs * 2 * rows * keys,
-        ),
+        cost_estimate=TINY,
         name="attend_backward",
     )(*args)
 
 
+def gradient_kernel(spans, tokens, split, *refs):
+    if split:
+        place_ref, refs = refs[0], refs[1:]
+    lhs_count = len(tokens)
+    lhs_refs = refs[:lhs_count]
+    seqs = (len(refs) - lhs_count - (3 if split else 2)) // len(spans)
+    rhs_refs = refs[lhs_count : lhs_count + seqs * len(spans)]
+    outs = refs[lhs_count + seqs * len(spans) : -1]
+    turned_ref = refs[-1]
+    step = pl.program_id(0)
+    for index, (first, last, group) in enumerate(spans):
+
+        @pl.when(step == first)
+        def _():
+            if index == 0 or spans[index - 1][2] != group:
+                for s in range(seqs):
+                    lhs = lhs_refs[group * seqs + s]
+                    size = lhs.shape[0]
+                    turned_ref[:, s * size : (s + 1) * size] = lhs[...].T
+
+        @pl.when((step >= first) & (step < last))
+        def _():
+            total = None
+            for s in range(seqs):
+                size = lhs_refs[group * seqs + s].shape[0]
+                part = dot(turned_ref[:, s * size : (s + 1) * size], rhs_refs[index * seqs + s][...])
+                total = part if total is None else total + part
+            if split:
+                low = place_ref[0, 0]
+                rows = split
+                for block in range(total.shape[0] // (2 * rows)):
+                    even = total[2 * block * rows : (2 * block + 1) * rows]
+                    odd = total[(2 * block + 1) * rows : (2 * block + 2) * rows]
+                    at = pl.ds(block * rows, rows)
+                    outs[0][at, :] = jnp.where(low == 0, odd, even).astype(jnp.bfloat16)
+                    outs[1][at, :] = jnp.where(low == 0, even, odd).astype(jnp.bfloat16)
+            else:
+                outs[0][...] = total.astype(jnp.bfloat16)
+
+
+def gradient_blocks(segments, columns, place=None, split=0):
+    width = segments[0][0][0].shape[1]
+    lhs_args, lhs_keys, rhs_args, rhs_specs, spans, specs = [], [], [], [], [], []
+    first = 0
+    flops = 0
+    for lhs, rhs in segments:
+        count = rhs[0].shape[1] // columns
+        key = tuple(id(v) for v in lhs)
+        if key not in lhs_keys:
+            lhs_keys.append(key)
+            lhs_args.extend(lhs)
+        spans.append((first, first + count, lhs_keys.index(key)))
+        for value in rhs:
+            flops += 2 * value.shape[0] * value.shape[1] * width
+
+            def where(i, first=first, count=count):
+                return (0, jnp.clip(i - first, 0, count - 1))
+
+            rhs_args.append(value)
+            rhs_specs.append(pl.BlockSpec((value.shape[0], columns), where))
+        first += count
+    for value in lhs_args:
+        specs.append(pl.BlockSpec(value.shape, lambda i: (0, 0)))
+    tokens = [v.shape[0] for v in lhs_args]
+    longest = max(sum(v.shape[0] for v in lhs) for lhs, rhs in segments)
+    out_width = first * columns
+    args = lhs_args + rhs_args
+    specs = specs + rhs_specs
+    if split:
+        args = [place] + args
+        specs = [pl.BlockSpec((1, 1), lambda i: (0, 0), memory_space=pltpu.SMEM)] + specs
+        shapes = [jax.ShapeDtypeStruct((width // 2, out_width), jnp.bfloat16)] * 2
+        out_specs = [pl.BlockSpec((width // 2, columns), lambda i: (0, i))] * 2
+    else:
+        shapes = jax.ShapeDtypeStruct((width, out_width), jnp.bfloat16)
+        out_specs = pl.BlockSpec((width, columns), lambda i: (0, i))
+    return pl.pallas_call(
+        functools.partial(gradient_kernel, spans, tokens, split),
+        grid=(first,),
+        in_specs=specs,
+        out_specs=out_specs,
+        out_shape=shapes,
+        scratch_shapes=[pltpu.VMEM((width, longest), jnp.bfloat16)],
+        compiler_params=pltpu.CompilerParams(vmem_limit_bytes=48 * 1024 * 1024),
+        cost_estimate=TINY,
+        name="weight_gradients",
+    )(*args)
+
+
 def mm(lhs, rhs):
-    return lax.dot_general(lhs, rhs, (((lhs.ndim - 1,), (0,)), ((), ())),
-                           preferred_element_type=jnp.float32)
+    return dot(lhs, rhs)
 
 
 def mm_back(lhs, rhs):
-    return lax.dot_general(lhs, rhs, (((lhs.ndim - 1,), (1,)), ((), ())),
-                           preferred_element_type=jnp.float32)
-
-
-def weight_grad(rows, grads):
-    return lax.dot_general(rows, grads, (((0, 1), (0, 1)), ((), ())),
-                           preferred_element_type=jnp.float32).astype(jnp.bfloat16)
+    return dot(lhs, rhs, NT)
 
 
 def rms_forward(values, gain_row):
@@ -307,9 +383,17 @@
 
 def rms_backward(grad_normed, unit_rows, inverse_rms, gain_row):
     grad_unit = grad_normed * gain_row
-    grad_gain = jnp.sum(grad_normed * unit_rows, axis=(0, 1))
+    grad_gain = jnp.sum(grad_normed * unit_rows, axis=0)
     inner_sum = jnp.mean(grad_unit * unit_rows, axis=-1, keepdims=True)
     return inverse_rms * (grad_unit - unit_rows * inner_sum), grad_gain
+
+
+def low_cast(value):
+    return value.astype(jnp.bfloat16)
+
+
+def wide_cast(value):
+    return value.astype(jnp.float32)
 
 
 def ctx_shape():
@@ -339,68 +423,323 @@
     return lax.ppermute(value, "ctx", pairs)
 
 
-def ctx_gather(value, axis, causal):
+def shift_fsdp(value, step):
+    count = lax.axis_size("fsdp")
+    return lax.ppermute(value, "fsdp", [(i, (i + step) % count) for i in range(count)])
+
+
+def put(buffer, value, at, axis):
+    return lax.dynamic_update_slice_in_dim(buffer, jnp.expand_dims(value, axis), at, axis)
+
+
+def ctx_gather(value, causal, axis, earlier):
     high, low = ctx_shape()
     at_high, at_low = ctx_place()
-    got = [value] + [shift_high(value, step, not causal) for step in range(1, high)]
-    slots = []
-    for slot in range(high):
-        block = jnp.zeros_like(value) if causal else value
-        for place in range(high):
-            if place >= slot or not causal:
-                block = jnp.where(at_high == place, got[(place - slot) % high], block)
-        slots.append(block)
-    held = jnp.stack(slots, axis)
+    pieces = [value] + [shift_high(value, step, not causal) for step in range(1, high)]
+    pieces = before(pieces, earlier)
+    places = [((at_high - step) % high, at_low) for step in range(high)]
     if low == 2:
-        other = swap_low(held)
-        first = jnp.where(at_low == 0, held, other)
-        second = jnp.where(at_low == 0, other, held)
-        held = jnp.stack([first, second], axis + 1)
+        pieces = pieces + [swap_low(piece) for piece in pieces]
+        places = places + [((at_high - step) % high, 1 - at_low) for step in range(high)]
+    shape = value.shape[:axis] + (high, low) + value.shape[axis:]
+    held = assemble(pieces, places, shape, axis)
     shape = value.shape[:axis] + (high * low * value.shape[axis],) + value.shape[axis + 1 :]
     return held.reshape(shape)
 
 
-def ctx_fold(value, axis, causal):
-    high, low = ctx_shape()
-    at_high, at_low = ctx_place()
-    size = value.shape[axis] // (high * low)
-    view = value.reshape(value.shape[:axis] + (high, low, size) + value.shape[axis + 1 :])
-    if low == 2:
-        mine = lax.dynamic_index_in_dim(view, at_low, axis + 1, False)
-        other = swap_low(lax.dynamic_index_in_dim(view, 1 - at_low, axis + 1, False))
-        held = (mine.astype(jnp.float32) + other.astype(jnp.float32)).astype(jnp.bfloat16)
-    else:
-        held = lax.squeeze(view, (axis + 1,))
-    total = lax.dynamic_index_in_dim(held, at_high, axis, False).astype(jnp.float32)
-    for step in range(1, high):
-        target = at_high - step
-        piece = lax.dynamic_index_in_dim(held, target % high, axis, False)
-        total = total + shift_high(piece, -step, not causal).astype(jnp.float32)
-    return total
-
-
-def gather_rows(shards):
+def gather_rows(shards, earlier):
     count = lax.axis_size("ctx")
     rows = shards[0].shape[0] // count
     start = lax.axis_index("ctx") * rows
+    shards = before(shards, earlier)
     parts = [lax.dynamic_slice_in_dim(s, start, rows, 0) for s in shards]
     part = jnp.concatenate(parts, axis=1) if len(parts) > 1 else parts[0]
     return lax.all_gather(part, ("fsdp", "ctx"), axis=0, tiled=True)
 
 
-def scatter_rows(grads):
-    part = lax.psum_scatter(grads, ("fsdp", "ctx"), scatter_dimension=0, tiled=True)
-    return ctx_gather(part, 0, False).astype(jnp.float32)
-
-
-def pair_total(partial):
-    own = partial.astype(jnp.bfloat16)
+def before(value, *earlier):
+    return lax.optimization_barrier((value, earlier))[0]
+
+
+def assemble_kernel(lead, place_ref, *refs):
+    pieces, out_ref = refs[:-1], refs[-1]
+    step = pl.program_id(0)
+    for index, piece in enumerate(pieces):
+
+        @pl.when(step == index)
+        def _():
+            rows = out_ref.shape[-2]
+            out_ref[...] = piece[..., :rows, :].reshape(out_ref.shape)
+
+
+def assemble(pieces, places, shape, lead):
+    places = jnp.stack([jnp.stack([jnp.asarray(v, jnp.int32) for v in p]) for p in places])
+    block = shape[:lead] + (1, 1) + shape[lead + 2 :]
+    rank = len(pieces[0].shape)
+
+    def where(i, place):
+        return (0,) * lead + (place[i, 0], place[i, 1]) + (0,) * (len(shape) - lead - 2)
+
+    return pl.pallas_call(
+        functools.partial(assemble_kernel, lead),
+        grid_spec=pltpu.PrefetchScalarGridSpec(
+            num_scalar_prefetch=1,
+            grid=(len(pieces),),
+            in_specs=[pl.BlockSpec(p.shape, lambda i, place: (0,) * rank) for p in pieces],
+            out_specs=pl.BlockSpec(block, where),
+        ),
+        out_shape=jax.ShapeDtypeStruct(shape, pieces[0].dtype),
+        compiler_params=pltpu.CompilerParams(vmem_limit_bytes=40 * 1024 * 1024),
+        cost_estimate=TINY,
+        name="assemble",
+    )(places, *pieces)
+
+
+def first_part(shards):
+    high, low = ctx_shape()
+    at_high, at_low = ctx_place()
+    rows = shards[0].shape[0] // low
+    parts = [lax.dynamic_slice_in_dim(s, at_low * rows, rows, 0) for s in shards]
+    return jnp.concatenate(parts, axis=1) if len(parts) > 1 else parts[0]
+
+
+def first_pieces(part):
+    count = lax.axis_size("fsdp")
+    if count > 8:
+        held = lax.all_gather(part, "fsdp", axis=0, tiled=False)
+        index = lax.axis_index("fsdp")
+        return [
+            lax.dynamic_index_in_dim(held, (index - step) % count, 0, False)
+            for step in range(count)
+        ]
+    return [part] + [shift_fsdp(part, step) for step in range(1, count)]
+
+
+def first_whole(pieces, rows):
+    count = lax.axis_size("fsdp")
+    index = lax.axis_index("fsdp")
+    high, low = ctx_shape()
+    at_high, at_low = ctx_place()
+    columns = pieces[0].shape[1]
+    places = [((index - step) % count, at_low) for step in range(count)]
+    if low == 2:
+        pieces = pieces + [swap_low(piece) for piece in pieces]
+        places = places + [((index - step) % count, 1 - at_low) for step in range(count)]
+    whole = assemble(pieces, places, (count, low, rows, columns), 0)
+    return whole.reshape(count * low * rows, columns)
+
+
+def gather_small(value):
+    count = lax.axis_size("fsdp")
+    index = lax.axis_index("fsdp")
+    if count > 8:
+        return lax.all_gather(value, "fsdp", axis=0, tiled=False)
+    held = put(jnp.zeros((count,) + value.shape, value.dtype), value, index, 0)
+    for step in range(1, count):
+        held = put(held, shift_fsdp(value, step), (index - step) % count, 0)
+    return held
+
+
+def fold_start(segments, columns):
+    high, low = ctx_shape()
+    at_high, at_low = ctx_place()
+    count = lax.axis_size("fsdp")
+    width = segments[0][0][0].shape[1]
+    rows = width // (count * high * low)
+    shape = (count, high, rows, -1)
+    if low == 2:
+        place = jnp.full((1, 1), at_low, jnp.int32)
+        away, kept = gradient_blocks(segments, columns, place, rows)
+        return [kept.reshape(shape), swap_low(away).reshape(shape)], away
+    kept = gradient_blocks(segments, columns)
+    return [kept.reshape(shape)], kept
+
+
+def fold_high(halves, earlier=()):
+    high, low = ctx_shape()
+    at_high, at_low = ctx_place()
+    halves = before(halves, earlier)
+
+    def part(at):
+        return low_cast(sum(wide_cast(lax.dynamic_index_in_dim(h, at, 1, False)) for h in halves))
+
+    sent = [part((at_high + step) % high) for step in range(1, high)]
+    mine = part(at_high)
+    moved = [shift_high(piece, step + 1, True) for step, piece in enumerate(sent)]
+    return [mine] + moved, (mine, sent)
+
+
+def fold_fsdp(parts, lines, earlier=()):
+    count = lax.axis_size("fsdp")
+    index = lax.axis_index("fsdp")
+    parts, lines = before((parts, lines), earlier)
+    small = jnp.zeros((count, EXTRA, parts[0].shape[2]), jnp.bfloat16)
+    small = small.at[:, 0, : lines.shape[1]].set(low_cast(lines))
+    if count > 8:
+        whole = low_cast(sum(wide_cast(p) for p in parts))
+        whole = jnp.concatenate([whole, small], axis=1)
+        flat = whole.reshape((-1,) + whole.shape[2:])
+        return [lax.psum_scatter(flat, "fsdp", scatter_dimension=0, tiled=True)], whole
+
+    def part(at):
+        total = sum(wide_cast(lax.dynamic_index_in_dim(p, at, 0, False)) for p in parts)
+        line = lax.dynamic_index_in_dim(small, at, 0, False)
+        return jnp.concatenate([low_cast(total), line], axis=0)
+
+    sent = [part((index + step) % count) for step in range(1, count)]
+    mine = part(index)
+    moved = [shift_fsdp(piece, step + 1) for step, piece in enumerate(sent)]
+    return [mine] + moved, (mine, sent)
+
+
+def fold_fsdp_first(halves, earlier=()):
+    count = lax.axis_size("fsdp")
+    index = lax.axis_index("fsdp")
+    halves = before(halves, earlier)
+    if count > 8:
+        whole = low_cast(sum(wide_cast(h) for h in halves))
+        flat = whole.reshape((-1,) + whole.shape[2:])
+        part = lax.psum_scatter(flat, "fsdp", scatter_dimension=0, tiled=True)
+        return [part.reshape(whole.shape[1:])], whole
+
+    def part(at):
+        return low_cast(sum(wide_cast(lax.dynamic_index_in_dim(h, at, 0, False)) for h in halves))
+
+    sent = [part((index + step) % count) for step in range(1, count)]
+    mine = part(index)
+    moved = [shift_fsdp(piece, step + 1) for step, piece in enumerate(sent)]
+    return [mine] + moved, (mine, sent)
+
+
+def fold_high_last(parts, earlier=()):
+    high, low = ctx_shape()
+    at_high, at_low = ctx_place()
+    parts = before(parts, earlier)
+
+    def part(at):
+        return low_cast(sum(wide_cast(lax.dynamic_index_in_dim(p, at, 0, False)) for p in parts))
+
+    sent = [part((at_high + step) % high) for step in range(1, high)]
+    mine = part(at_high)
+    moved = [shift_high(piece, step + 1, True) for step, piece in enumerate(sent)]
+    return [mine] + moved, (mine, sent)
+
+
+def fold_own(parts, earlier=()):
+    parts = before(parts, earlier)
+    return low_cast(sum(wide_cast(p) for p in parts))
+
+
+def spread_high(part):
+    high, low = ctx_shape()
+    return [part] + [shift_high(part, step, True) for step in range(1, high)]
+
+
+def spread_low(parts, earlier=()):
+    high, low = ctx_shape()
+    held = jnp.stack(before(parts, earlier))
+    return [held, swap_low(held) if low == 2 else held], held
+
+
+def finish_kernel(high, low, cuts, extra, place_ref, mine_ref, other_ref, *outs):
+    rows = mine_ref.shape[1] - extra
+    for (start, stop, turned), out in zip(cuts, outs):
+        blocks = []
+        for at_high in range(high):
+            step = lax.rem(place_ref[0, 0] - at_high + high, high)
+            for at_low in range(low):
+                mine = mine_ref[step, :rows, start:stop]
+                other = other_ref[step, :rows, start:stop]
+                chosen = jnp.where(place_ref[0, 1] == at_low, mine, other)
+                blocks.append(chosen.astype(jnp.float32))
+        whole = jnp.concatenate(blocks, axis=0)
+        out[...] = whole.T if turned else whole
+    if extra:
+        total = None
+        for step in range(high):
+            for ref in (mine_ref, other_ref)[:low]:
+                line = ref[step, rows:, :].astype(jnp.float32)
+                total = line if total is None else total + line
+        outs[-1][...] = total
+
+
+def spread_end(pair, cuts, extra=0, earlier=()):
+    high, low = ctx_shape()
+    at_high, at_low = ctx_place()
+    mine, other = before(pair, earlier)
+    rows = mine.shape[1] - extra
+    shapes = []
+    for start, stop, turned in cuts:
+        shape = (high * low * rows, stop - start)
+        shapes.append(jax.ShapeDtypeStruct(shape[::-1] if turned else shape, jnp.float32))
+    if extra:
+        shapes.append(jax.ShapeDtypeStruct((extra, mine.shape[2]), jnp.float32))
+    place = jnp.stack([at_high, at_low]).astype(jnp.int32).reshape(1, 2)
+    whole = pl.BlockSpec(memory_space=pltpu.VMEM)
+    return pl.pallas_call(
+        functools.partial(finish_kernel, high, low, cuts, extra),
+        in_specs=[pl.BlockSpec(memory_space=pltpu.SMEM), whole, whole],
+        out_specs=[whole] * len(shapes),
+        out_shape=shapes,
+        compiler_params=pltpu.CompilerParams(vmem_limit_bytes=48 * 1024 * 1024),
+        cost_estimate=TINY,
+        name="finish",
+    )(place, mine, other)
+
+
+def block_fold_start(lefts, rights):
+    high, low = ctx_shape()
+    at_high, at_low = ctx_place()
+    size = lefts[0].shape[0] // (high * low)
+
+    def part(at):
+        views = [v.reshape(high, low, size, -1) for v in lefts + rights]
+        views = [lax.dynamic_index_in_dim(v, at, 1, False) for v in views]
+        views = [
+            jnp.concatenate([views[i], views[len(lefts) + i]], axis=-1) for i in range(len(lefts))
+        ]
+        return jnp.concatenate(views, axis=1) if len(views) > 1 else views[0]
+
+    if low == 1:
+        whole = part(0)
+        return [whole], whole
+    away = part(1 - at_low)
+    kept = part(at_low)
+    return [kept, swap_low(away)], (kept, away)
+
+
+def block_fold_high(halves, causal, earlier=()):
+    high, low = ctx_shape()
+    at_high, at_low = ctx_place()
+    halves = before(halves, earlier)
+
+    def part(at):
+        return low_cast(sum(wide_cast(lax.dynamic_index_in_dim(h, at, 0, False)) for h in halves))
+
+    sent = [part((at_high - step) % high) for step in range(1, high)]
+    mine = part(at_high)
+    moved = [shift_high(piece, -step - 1, not causal) for step, piece in enumerate(sent)]
+    return [mine] + moved, (mine, sent)
+
+
+def block_fold_end(parts, earlier=()):
+    parts = before(parts, earlier)
+    return low_cast(sum(wide_cast(p) for p in parts))
+
+
+def pair_start(partial):
+    own = low_cast(partial)
     count = lax.axis_size("tp")
-    total = own.astype(jnp.float32)
-    for step in range(1, count):
-        moved = lax.ppermute(own, "tp", [(i, (i + step) % count) for i in range(count)])
-        total = total + moved.astype(jnp.float32)
-    return total
+    moved = [
+        lax.ppermute(own, "tp", [(i, (i + step) % count) for i in range(count)])
+        for step in range(1, count)
+    ]
+    return [own] + moved, own
+
+
+def pair_end(parts, earlier=()):
+    parts = before(parts, earlier)
+    return sum(wide_cast(p) for p in parts)
 
 
 def body(
@@ -427,166 +766,283 @@
     ffn_down,
 ):
     shards = lax.axis_size("fsdp")
-    seq_count, row_count, width = hidden_in.shape
+    seqs, row_count, width = hidden_in.shape
     length = dec_segments.shape[1]
-    heads_width = self_query.shape[1]
+    hw = self_query.shape[1]
     units = ffn_gate.shape[1]
     bucket_rows, head_count = position_bias.shape
     bucket_count = bucket_rows * shards
     gain_rows = self_gain.shape[0]
     offset = lax.axis_index("ctx") * row_count
+    every = range(seqs)
 
     small = jnp.concatenate([self_gain, cross_gain, ffn_gain, position_bias.reshape(-1)])
-    small = lax.all_gather(small, "fsdp", axis=0, tiled=False)
+    line = jnp.zeros((EXTRA, 3 * hw), jnp.bfloat16).at[0, : small.shape[0]].set(small)
+    qkv_part = first_part([self_query, self_key, self_value])
+    first_rows = qkv_part.shape[0]
+    qkv_part = jnp.concatenate([qkv_part, line], axis=0)
+    first_arrived = first_pieces(qkv_part)
+    shard = lax.axis_index("fsdp")
+    small = jnp.stack([piece[first_rows, : small.shape[0]] for piece in first_arrived])
+    small = jnp.stack(
+        [lax.dynamic_index_in_dim(small, (shard - i) % shards, 0, False) for i in range(shards)]
+    )
     gain_self, gain_cross, gain_ffn = [
-        small[:, gain_rows * i : gain_rows * (i + 1)].reshape(width).astype(jnp.float32)
-        for i in range(3)
+        wide_cast(small[:, gain_rows * i : gain_rows * (i + 1)].reshape(width)) for i in range(3)
     ]
-    bias_table = small[:, 3 * gain_rows :].reshape(bucket_count, head_count).astype(jnp.float32)
-    hidden_all = ctx_gather(hidden_in, 1, True)
-    encoder_all = ctx_gather(encoder_states, 1, False)
-    self_weights = gather_rows([self_query, self_key, self_value])
+    bias_table = wide_cast(small[:, 3 * gain_rows :].reshape(bucket_count, head_count))
+    first_weights = first_whole(first_arrived, first_rows)
+    hidden_all = ctx_gather(before(hidden_in, qkv_part), True, 1, first_arrived[-1])
+    source = [wide_cast(hidden_in[s]) for s in every]
+    norm_one = [rms_forward(source[s], gain_self) for s in every]
+    norm_all = [rms_forward(wide_cast(hidden_all[s]), gain_self)[2] for s in every]
     middle_weights = gather_rows(
-        [cross_query, cross_key, cross_value, self_output.T, cross_output.T]
-    )
-    ffn_weights = gather_rows([ffn_gate, ffn_up, ffn_down.T])
-    query_self = self_weights[:, :heads_width]
-    pair_self = self_weights[:, heads_width:]
-    query_cross = middle_weights[:, :heads_width]
-    pair_cross = middle_weights[:, heads_width : 3 * heads_width]
-    output_self = middle_weights[:, 3 * heads_width : 4 * heads_width]
-    output_cross = middle_weights[:, 4 * heads_width :]
-    gate_up = ffn_weights[:, : 2 * units]
-    down = ffn_weights[:, 2 * units :]
+        [self_output.T, cross_query, cross_key, cross_value, cross_output.T], qkv_part
+    )
+    gate_up = gather_rows([ffn_gate, ffn_up], qkv_part)
+    ffn_down, encoder_states = before((ffn_down, encoder_states), first_weights, norm_all[0])
+    down_pieces = first_pieces(first_part([ffn_down.T]))
+    query_self = first_weights[:, :hw]
+    pair_self = first_weights[:, hw:]
+    output_self = middle_weights[:, :hw]
+    query_cross = middle_weights[:, hw : 2 * hw]
+    pair_cross = middle_weights[:, 2 * hw : 4 * hw]
+    output_cross = middle_weights[:, 4 * hw :]
 
     query_docs = lax.dynamic_slice_in_dim(dec_segments, offset, row_count, 1)[:, None, :]
     dec_docs = dec_segments[:, :, None]
     enc_docs = enc_segments[:, :, None]
-    bucket_onehot = (
+    bucket_onehot = wide_cast(
         bucket_table[:, None] == jnp.arange(bucket_count, dtype=jnp.int32)[None, :]
-    ).astype(jnp.float32)
+    )
     distance_bias = jnp.dot(bucket_onehot, bias_table, precision=lax.Precision.HIGHEST).T
     padded = jnp.concatenate([jnp.zeros_like(distance_bias), distance_bias], axis=1)
     lines = lax.dynamic_slice_in_dim(padded, offset, row_count + length, 1)
     lines = lines.reshape(head_count // 2, 2, row_count + length)
-    lines = jnp.concatenate([lines, jnp.zeros_like(lines), jnp.zeros_like(lines),
-                             jnp.zeros_like(lines)], axis=1)
+    lines = jnp.concatenate(
+        [lines, jnp.zeros((head_count // 2, 6, row_count + length), jnp.float32)], axis=1
+    )
     place = jnp.full((1, 1), offset, jnp.int32)
 
-    source = hidden_in.astype(jnp.float32)
-    unit_one, inverse_one, normed_one = rms_forward(source, gain_self)
-    unused_unit, unused_inverse, normed_all = rms_forward(
-        hidden_all.astype(jnp.float32), gain_self
-    )
-    queries_one = mm(normed_one, query_self).astype(jnp.bfloat16)
-    pair_one = mm(normed_all, pair_self).astype(jnp.bfloat16)
-    attended_one, logs_one = attend_forward(
-        queries_one, pair_one, query_docs, dec_docs, place, lines
-    )
-    after_one = source + pair_total(mm_back(attended_one, output_self))
-
-    pair_two = mm(encoder_all, pair_cross).astype(jnp.bfloat16)
-    unit_two, inverse_two, normed_two = rms_forward(after_one, gain_cross)
-    queries_two = mm(normed_two, query_cross).astype(jnp.bfloat16)
-    attended_two, logs_two = attend_forward(queries_two, pair_two, query_docs, enc_docs)
-    after_two = after_one + pair_total(mm_back(attended_two, output_cross))
-
-    grad_units = mm(out_cotangent, down)
-    unit_three, inverse_three, normed_three = rms_forward(after_two, gain_ffn)
-    both_rows = mm(normed_three, gate_up)
-    gate_rows = both_rows[..., :units]
-    up_rows = both_rows[..., units:]
-    activated, gelu_pull = jax.vjp(lambda v: jax.nn.gelu(v, approximate=True), gate_rows)
-    hidden_units = (activated * up_rows).astype(jnp.bfloat16)
-    grad_gate_rows = gelu_pull(grad_units * up_rows)[0].astype(jnp.bfloat16)
-    grad_up_rows = (grad_units * activated).astype(jnp.bfloat16)
-    grad_both = jnp.concatenate([grad_gate_rows, grad_up_rows], axis=-1)
-    grad_normed = pair_total(mm_back(grad_both, gate_up))
-    layer_output = after_two + pair_total(mm_back(hidden_units, down))
-    grads_ffn = scatter_rows(
-        jnp.concatenate(
-            [weight_grad(normed_three, grad_both), weight_grad(out_cotangent, hidden_units)],
-            axis=1,
+    def one(value, s):
+        return value[s : s + 1]
+
+    q_one, kv_one, att_one, log_one, pair_one, done = [], [], [], [], [], ()
+    for s in every:
+        rows_all, rows_own = before((norm_all[s], norm_one[s][2]), done)
+        kv_one.append(low_cast(mm(rows_all, pair_self)))
+        q_one.append(low_cast(mm(rows_own, query_self)))
+        out, logs = attend_forward(
+            q_one[s][None], kv_one[s][None], one(query_docs, s), one(dec_docs, s), place, lines
         )
-    )
-    grad_from, grad_gain_ffn = rms_backward(grad_normed, unit_three, inverse_three, gain_ffn)
-    grad_res = out_cotangent.astype(jnp.float32) + grad_from
-
-    grad_low = grad_res.astype(jnp.bfloat16)
-    grad_attended = mm(grad_low, output_cross).astype(jnp.bfloat16)
-    grad_out_cross = weight_grad(grad_low, attended_two)
-    grad_q_two, grad_k_two, grad_v_two = attend_backward(
-        queries_two, pair_two, query_docs, enc_docs, attended_two, logs_two, grad_attended
-    )
-    grad_normed = pair_total(mm_back(grad_q_two, query_cross))
-    grad_pair_two = jnp.concatenate([grad_k_two, grad_v_two], axis=-1)
-    grad_query_cross = weight_grad(normed_two, grad_q_two)
-    grad_pair_cross = weight_grad(encoder_all, grad_pair_two)
-    folded_two = ctx_fold(grad_pair_two, 1, False).astype(jnp.bfloat16)
-    grad_states = pair_total(mm_back(folded_two, pair_cross))
-    grad_from, grad_gain_cross = rms_backward(grad_normed, unit_two, inverse_two, gain_cross)
-    grad_res = grad_res + grad_from
-
-    grad_low = grad_res.astype(jnp.bfloat16)
-    grad_attended = mm(grad_low, output_self).astype(jnp.bfloat16)
-    grad_out_self = weight_grad(grad_low, attended_one)
-    grads_middle = scatter_rows(
-        jnp.concatenate([grad_query_cross, grad_pair_cross, grad_out_self, grad_out_cross], axis=1)
-    )
-    grad_q_one, grad_k_one, grad_v_one, line_grads = attend_backward(
-        queries_one, pair_one, query_docs, dec_docs, attended_one, logs_one, grad_attended,
-        place, lines,
-    )
-    grad_pair_one = jnp.concatenate([grad_k_one, grad_v_one], axis=-1)
-    folded_one = ctx_fold(grad_pair_one, 1, True).astype(jnp.bfloat16)
-    grads_self = scatter_rows(
-        jnp.concatenate(
-            [weight_grad(normed_one, grad_q_one), weight_grad(normed_all, grad_pair_one)], axis=1
+        att_one.append(out)
+        log_one.append(logs)
+        rows = before(out[0], pair_one[-1]) if s else out[0]
+        parts, done = pair_start(mm_back(rows, output_self))
+        pair_one.append(parts)
+
+    encoder_all = ctx_gather(encoder_states, False, 1, done)
+    down = first_whole(before(down_pieces, done), down_pieces[0].shape[0])
+    kv_two = [low_cast(mm(before(encoder_all[s], down), pair_cross)) for s in every]
+    after_one, norm_two, q_two, att_two, log_two, pair_two = [], [], [], [], [], []
+    done = (done, kv_two)
+    for s in every:
+        after_one.append(source[s] + pair_end(pair_one[s], done))
+        norm_two.append(rms_forward(after_one[s], gain_cross))
+        q_two.append(low_cast(mm(norm_two[s][2], query_cross)))
+        out, logs = attend_forward(
+            q_two[s][None], kv_two[s][None], one(query_docs, s), one(enc_docs, s)
         )
-    )
-    grad_normed = pair_total(
-        mm_back(grad_q_one, query_self) + mm_back(folded_one, pair_self)
-    )
-    grad_from, grad_gain_self = rms_backward(grad_normed, unit_one, inverse_one, gain_self)
-    grad_input = (grad_res + grad_from).astype(jnp.bfloat16)
-
-    line_grads = line_grads[:, :2].reshape(head_count, row_count + length)
+        att_two.append(out)
+        log_two.append(logs)
+        rows = out[0] if s else before(out[0], pair_one[-1])
+        parts, done = pair_start(mm_back(rows, output_cross))
+        pair_two.append(parts)
+
+    grad_units = [mm(before(out_cotangent[s], done), down) for s in every]
+    after_two, norm_three, units_out, grads_gate, grads_up, pair_three = [], [], [], [], [], []
+    done = (done, grad_units)
+    for s in every:
+        after_two.append(after_one[s] + pair_end(pair_two[s], done))
+        norm_three.append(rms_forward(after_two[s], gain_ffn))
+        both_rows = mm(norm_three[s][2], gate_up)
+        up_rows = both_rows[:, units:]
+        activated, gelu_pull = jax.vjp(
+            lambda v: jax.nn.gelu(v, approximate=True), both_rows[:, :units]
+        )
+        units_out.append(low_cast(activated * up_rows))
+        grads_gate.append(low_cast(gelu_pull(grad_units[s] * up_rows)[0]))
+        grads_up.append(low_cast(grad_units[s] * activated))
+        parts, done = pair_start(
+            mm_back(grads_gate[s], gate_up[:, :units]) + mm_back(grads_up[s], gate_up[:, units:])
+        )
+        pair_three.append(parts)
+    cotangent = [out_cotangent[s] for s in every]
+    low_three = [n[2] for n in norm_three]
+    ffn_blocks = gradient_blocks(
+        [(low_three, grads_gate), (low_three, grads_up), (cotangent, units_out)], units
+    )
+    ffn_part = lax.psum_scatter(ffn_blocks, ("fsdp", "ctx"), scatter_dimension=0, tiled=True)
+
+    res_two, low_two, dq_two, dk_two, dv_two, gain_three, pair_four = [], [], [], [], [], [], []
+    done = (done, ffn_blocks)
+    for s in every:
+        grad_from, gain = rms_backward(
+            pair_end(pair_three[s], done), norm_three[s][0], norm_three[s][1], gain_ffn
+        )
+        gain_three.append(gain)
+        res_two.append(wide_cast(out_cotangent[s]) + grad_from)
+        low_two.append(low_cast(res_two[s]))
+        grad_attended = low_cast(mm(low_two[s], output_cross))
+        dq, dk, dv = attend_backward(
+            q_two[s][None], kv_two[s][None], one(query_docs, s), one(enc_docs, s),
+            att_two[s], log_two[s], grad_attended[None],
+        )
+        dq_two.append(dq[0])
+        dk_two.append(dk[0])
+        dv_two.append(dv[0])
+        rows = before(dq[0], pair_four[-1]) if s else dq[0]
+        parts, done = pair_start(mm_back(rows, query_cross))
+        pair_four.append(parts)
+    encoder_rows = [encoder_all[s] for s in every]
+    middle, middle_blocks = fold_start(
+        [
+            (before([n[2] for n in norm_two], done), dq_two),
+            (encoder_rows, dk_two),
+            (encoder_rows, dv_two),
+            (low_two, [a[0] for a in att_two]),
+        ],
+        hw,
+    )
+
+    res_one, low_one, dq_one, dk_one, dv_one, gain_two, line_grads, folds = (
+        [], [], [], [], [], [], [], [],
+    )
+    encoder_fold, encoder_done = block_fold_start(before(dk_two, middle_blocks), dv_two)
+    done = (done, middle_blocks, encoder_done)
+    pair_states, pair_out, pair_six = None, None, []
+    for s in every:
+        grad_from, gain = rms_backward(
+            pair_end(pair_four[s], done), norm_two[s][0], norm_two[s][1], gain_cross
+        )
+        gain_two.append(gain)
+        res_one.append(res_two[s] + grad_from)
+        low_one.append(low_cast(res_one[s]))
+        grad_attended = low_cast(mm(low_one[s], output_self))
+        if s == 0:
+            middle, done = fold_fsdp_first(middle, grad_attended)
+            encoder_fold, encoder_done = block_fold_high(encoder_fold, False, done)
+            done = (done, encoder_done)
+        else:
+            folds[s - 1], done = block_fold_high(folds[s - 1], True, grad_attended)
+            if s == 1:
+                rows = jnp.concatenate(before(units_out, done), axis=0)
+                pair_out, own = pair_start(mm_back(rows, down))
+                done = (done, own)
+        dq, dk, dv, line = attend_backward(
+            q_one[s][None], kv_one[s][None], one(query_docs, s), one(dec_docs, s),
+            att_one[s], log_one[s], before(grad_attended, done)[None], place, lines,
+        )
+        dq_one.append(dq[0])
+        dk_one.append(dk[0])
+        dv_one.append(dv[0])
+        line_grads.append(line)
+        if s == 0:
+            folded = block_fold_end(encoder_fold, dk)
+            pair_states, own = pair_start(mm_back(folded, pair_cross))
+            fold, done = block_fold_start(before([dk[0]], own), [dv[0]])
+            folds.append(fold)
+        elif s < seqs - 1:
+            fold, done = block_fold_start([dk[0]], [dv[0]])
+            folds.append(fold)
+
+    last = seqs - 1
+    for s in range(last):
+        folded = block_fold_end(folds[s], dk_one[last])
+        parts, done = pair_start(mm_back(dq_one[s], query_self) + mm_back(folded, pair_self))
+        pair_six.append(parts)
+    first, done = fold_start(
+        [(before(low_one, done), [a[0] for a in att_one]), ([n[2] for n in norm_one], dq_one)], hw
+    )
+    fold, done = block_fold_start(before([dk_one[last]], done), [dv_one[last]])
+    states = pair_end(pair_states, done)
+    grad_states = low_cast(states).reshape(seqs, -1, width)
+    first, done = fold_fsdp_first(first, (done, grad_states))
+    fold, done = block_fold_high(fold, True, done)
+    second, second_blocks = fold_start([(before(norm_all, done), dk_one), (norm_all, dv_one)], hw)
+    folded = block_fold_end(fold, second_blocks)
+    parts, done = pair_start(mm_back(dq_one[last], query_self) + mm_back(folded, pair_self))
+    pair_six.append(parts)
+    second, done = fold_high(second, done)
+    middle, done = fold_high_last(middle, done)
+    out_rows = pair_end(pair_out, done)
+    layer_output = [
+        low_cast(after_two[s] + out_rows[s * row_count : (s + 1) * row_count]) for s in every
+    ]
+    first, done = fold_high_last(first, layer_output)
+    grad_input, gain_one = [], []
+    for s in every:
+        grad_from, gain = rms_backward(
+            pair_end(pair_six[s], done), norm_one[s][0], norm_one[s][1], gain_self
+        )
+        gain_one.append(gain)
+        grad_input.append(low_cast(res_one[s] + grad_from))
+    line_total = sum(line_grads)[:, :2].reshape(head_count, row_count + length)
     spread = lax.dynamic_update_slice_in_dim(
-        jnp.zeros((head_count, 2 * length), jnp.float32), line_grads, offset, 1
+        jnp.zeros((head_count, 2 * length), jnp.float32), line_total, offset, 1
     )[:, length:]
     grad_bias = jnp.dot(spread, bucket_onehot, precision=lax.Precision.HIGHEST).T
-    totals = jnp.concatenate(
-        [grad_gain_self, grad_gain_cross, grad_gain_ffn, grad_bias.reshape(-1)]
-    )
-    totals = lax.psum(totals, ("fsdp", "ctx"))
-    shard = lax.axis_index("fsdp")
-    gain_grads = [
-        lax.dynamic_slice_in_dim(totals, width * i + shard * gain_rows, gain_rows, 0)
-        for i in range(3)
-    ]
-    bias_grad = lax.dynamic_slice_in_dim(
-        totals, 3 * width + shard * bucket_rows * head_count, bucket_rows * head_count, 0
-    ).reshape(bucket_rows, head_count)
-    hw = heads_width
+    totals = [sum(g).reshape(shards, gain_rows) for g in (gain_one, gain_two, gain_three)]
+    totals = jnp.concatenate(totals + [grad_bias.reshape(shards, -1)], axis=1)
+    second, done = fold_fsdp(second, totals, grad_input)
+    middle_part = fold_own(middle, done)
+    outer = spread_high(jnp.concatenate([before(ffn_part, done), middle_part], axis=1))
+    first_part_sum = fold_own(first, outer[0])
+    second_part = fold_own(second, first_part_sum)
+    inner = jnp.concatenate(
+        [jnp.pad(first_part_sum, ((0, EXTRA), (0, 0))),
+         second_part],
+        axis=1,
+    )
+    outer, done = spread_low(outer, inner)
+    inner = spread_high(inner)
+    edge = 3 * units
+    ffn_gate_grad, ffn_up_grad, ffn_down_grad, cross_q, cross_k, cross_v, cross_o = spread_end(
+        outer,
+        [
+            (0, units, False), (units, 2 * units, False), (2 * units, edge, True),
+            (edge, edge + hw, False), (edge + hw, edge + 2 * hw, False),
+            (edge + 2 * hw, edge + 3 * hw, False), (edge + 3 * hw, edge + 4 * hw, True),
+        ],
+    )
+    inner, done = spread_low(inner, ffn_gate_grad)
+    self_o, self_q, self_k, self_v, sums = spread_end(
+        inner,
+        [(0, hw, True), (hw, 2 * hw, False), (2 * hw, 3 * hw, False), (3 * hw, 4 * hw, False)],
+        EXTRA,
+    )
+    sums = sums[0, 2 * hw :]
+    gain_grads = [sums[gain_rows * i : gain_rows * (i + 1)] for i in range(3)]
+    bias_grad = sums[3 * gain_rows : 3 * gain_rows + bucket_rows * head_count]
     return (
-        layer_output.astype(jnp.bfloat16),
-        grad_input,
-        grad_states.astype(jnp.bfloat16),
+        jnp.stack(layer_output),
+        jnp.stack(grad_input),
+        grad_states,
         gain_grads[0],
-        grads_self[:, :hw],
-        grads_self[:, hw : 2 * hw],
-        grads_self[:, 2 * hw :],
-        grads_middle[:, 3 * hw : 4 * hw].T,
-        bias_grad,
+        self_q,
+        self_k,
+        self_v,
+        self_o,
+        bias_grad.reshape(bucket_rows, head_count),
         gain_grads[1],
-        grads_middle[:, :hw],
-        grads_middle[:, hw : 2 * hw],
-        grads_middle[:, 2 * hw : 3 * hw],
-        grads_middle[:, 4 * hw :].T,
+        cross_q,
+        cross_k,
+        cross_v,
+        cross_o,
         gain_grads[2],
-        grads_ffn[:, :units],
-        grads_ffn[:, units : 2 * units],
-        grads_ffn[:, 2 * units :].T,
+        ffn_gate_grad,
+        ffn_up_grad,
+        ffn_down_grad,
     )
 
 

time: 648 us -> 464 us (0.72)
  waiting for transfers between devices: 283 us -> 104 us
  blocking collectives: 70.8 us -> 0 us
  Pallas kernels: 64.3 us -> 112 us
  starting transfers between devices: 21.7 us -> 56.8 us
  local copies, waits for them, and re-layouts: 60.7 us -> 43 us
    ppermute x7 -> x10, waiting for transfers between devices: 90.1 us -> 9.47 us  [shift_high(): return lax.ppermute(value, 'ctx', pairs)]
    psum x1 -> x0, blocking collectives: 58.6 us -> none  [body(): totals = lax.psum(totals, ('fsdp', 'ctx'))]
    pallas_call x0 -> x10, Pallas kernels: none -> 50.8 us  [the longest x4 32.8 us: gradient_blocks(): pl.pallas_call(functools.partial(gradient_kernel, spans, tokens, split),...]
    ppermute x7 -> x27, waiting for transfers between devices: 130 us -> 89.1 us  [the longest x15 55.7 us: shift_fsdp(): lax.ppermute(value, 'fsdp', [(i, (i + step) % count) for i in range(count)])]
    reduce_scatter x3 -> x1, waiting for transfers between devices: 35.1 us -> 0.02 us  [body(): lax.psum_scatter(ffn_blocks, ('fsdp', 'ctx'), scatter_dimension=0, tiled=...]
    all_gather x3 -> x2, waiting for transfers between devices: 27 us -> 0.02 us  [gather_rows(): return lax.all_gather(part, ('fsdp', 'ctx'), axis=0, tiled=True)]
    ppermute x7 -> x27, starting transfers between devices: 9.1 us -> 30.8 us  [the longest x15 19.1 us: shift_fsdp(): lax.ppermute(value, 'fsdp', [(i, (i + step) % count) for i in range(count)])]
    convert_element_type x8 -> x20, other arithmetic: 14.5 us -> 34.7 us  [the longest x19 33.9 us: low_cast(): return value.astype(jnp.bfloat16)]
  transfers between devices with their start and end apart: 27 -> 60, of which waited for: 16 -> 20; matrix products, arithmetic and copies ran while one was open for 20% -> 30% of each run, Pallas kernels for 4% -> 24%
where the time goes in v2:
time: 464 us; the launch traced here: 455 us
  Pallas kernels  112 us (24%)
  waiting for transfers between devices  104 us (22%)
  matrix products  62.2 us (13%)
  other arithmetic  60.8 us (13%)
  starting transfers between devices  56.8 us (12%)
  local copies, waits for them, and re-layouts  43 us (9%)
  between operations  16.6 us (4%)
    dot_general x32, matrix products, dot(): return lax.dot_general(lhs, rhs, dims, preferred_element_type=jnp.float32)  61.2 us
    ppermute x15, waiting for transfers between devices, shift_fsdp(): lax.ppermute(value, 'fsdp', [(i, (i + step) % count) for i in range(count)])  55.7 us
    pallas_call x4, Pallas kernels, attend_backward(): pl.pallas_call(functools.partial(backward_kernel, causal), grid=(pairs, s...  36.9 us
    convert_element_type x19, other arithmetic, low_cast(): return value.astype(jnp.bfloat16)  33.9 us
    ppermute x12, waiting for transfers between devices, pair_start(): lax.ppermute(own, 'tp', [(i, (i + step) % count) for i in range(count)])  33.4 us
    pallas_call x4, Pallas kernels, gradient_blocks(): pl.pallas_call(functools.partial(gradient_kernel, spans, tokens, split),...  32.8 us
    unnamed x271, local copies, waits for them, and re-layouts  24.8 us
    pallas_call x4, Pallas kernels, attend_forward(): pl.pallas_call(functools.partial(forward_kernel, causal), grid=(pairs, se...  24 us
  transfers between devices with their start and end apart: 60, of which 20 were waited for; matrix products, arithmetic and copies ran while one was open for 30% of the time, Pallas kernels for 24%

profile of v2, /device:TPU:0, one launch (start us, length us, event | category | flops | bytes accessed | tf_op | source)
XLA Modules:
  0.0 455.1 jit_solution(14384672580478255054)
XLA Ops:
  16.9 4.7 %collective-permute-start.2 = (bf16[144,1536]{1,0:T(8,128)(2,1)S(1)}, bf16[144,1536]{1,0:T(8,128)(2,1)}, u32[]{:S(2)}, u32[]{:S(2)}) collective-permute-start(bf16[144,1536]{1,0:T(8,128)(2,1)S(1)} %fusion.134.refs_0_), channel_id=1, source_target_pairs={{0,24},{8,0},{16,8},{24,16},{1,25},{9,1},{17,9},{25,17},{2,26},{10... | collective-permute-start | bytes 1327112 | tf_op jit(solution)/shard_map/ppermute | solution.py:428
  22.6 4.4 collective-permute-start.3
  30.3 6.0 %collective-permute-done.2.refs_3_ = bf16[144,1536]{1,0:T(8,128)(2,1)} collective-permute-done((bf16[144,1536]{1,0:T(8,128)(2,1)S(1)}, bf16[144,1536]{1,0:T(8,128)(2,1)}, u32[]{:S(2)}, u32[]{:S(2)}) %collective-permute-start.2) | collective-permute-done | bytes 442400 | tf_op jit(solution)/shard_map/ppermute | solution.py:428
  37.0 33.6 %collective-permute-done.1.refs_2_ = bf16[144,1536]{1,0:T(8,128)(2,1)} collective-permute-done((bf16[144,1536]{1,0:T(8,128)(2,1)S(1)}, bf16[144,1536]{1,0:T(8,128)(2,1)}, u32[]{:S(2)}, u32[]{:S(2)}) %collective-permute-start.1) | collective-permute-done | bytes 442400 | tf_op jit(solution)/shard_map/ppermute | solution.py:428
  102.2 4.0 convert_bitcast_fusion.1.refs_5_.refs_6_
  106.2 7.5 %attend_forward.4 = (bf16[1,256,512]{2,1,0:T(8,128)(2,1)S(1)}, f32[1,4,8,256]{3,2,1,0:T(8,128)S(1)}) custom-call(s32[1,1]{1,0:T(1,128)} %bitcast.1.refs_0_, f32[4,8,1280]{2,1,0:T(8,128)S(1)} %concatenate.83.refs_1_, s32[1,1,256]{2,1,0:T(1,128)S(1)} %get-tuple-element.444.refs_2_.refs_0_, s32[1,1024,1]{2,1,0:T(8,128)S(1)} %copy.103.refs_3_, ...), custom_call_target="tpu_custom_call" | custom-call | flops 1 | bytes 1 | tf_op jit(solution)/shard_map/attend_forward/pallas_call | solution.py:232
  118.5 4.6 %convert_bitcast_fusion.refs_5_.refs_6_ = bf16[1,1024,1024]{2,1,0:T(8,128)(2,1)S(1)} fusion(bf16[1024,1024]{1,0:T(8,128)(2,1)} %get-tuple-element.293.refs_2_.refs_4_, bf16[1024,1536]{1,0:T(8,128)(2,1)} %bitcast.329), kind=kOutput, calls=%fused_computation.19 | convolution fusion | flops 2148532224 | bytes 6291456 | tf_op jit(solution)/shard_map/dot_general | solution.py:20
  125.6 7.4 %attend_forward.5 = (bf16[1,256,512]{2,1,0:T(8,128)(2,1)S(1)}, f32[1,4,8,256]{3,2,1,0:T(8,128)S(1)}) custom-call(s32[1,1]{1,0:T(1,128)} %bitcast.1.refs_0_, f32[4,8,1280]{2,1,0:T(8,128)S(1)} %concatenate.83.refs_1_, s32[1,1,256]{2,1,0:T(1,128)S(1)} %get-tuple-element.445.refs_2_.refs_0_, s32[1,1024,1]{2,1,0:T(8,128)S(1)} %copy.106.refs_3_, ...), custom_call_target="tpu_custom_call" | custom-call | flops 1 | bytes 1 | tf_op jit(solution)/shard_map/attend_forward/pallas_call | solution.py:232
  135.8 4.9 %collective-permute-done.15.refs_2_ = bf16[128,1408]{1,0:T(8,128)(2,1)} collective-permute-done((bf16[128,1408]{1,0:T(8,128)(2,1)S(1)}, bf16[128,1408]{1,0:T(8,128)(2,1)}, u32[]{:S(2)}, u32[]{:S(2)}) %collective-permute-start.15) | collective-permute-done | bytes 360480 | tf_op jit(solution)/shard_map/ppermute | solution.py:428
  158.8 4.5 attend_forward.6
  166.1 4.6 %attend_forward.7 = (bf16[1,256,512]{2,1,0:T(8,128)(2,1)S(1)}, f32[1,4,8,256]{3,2,1,0:T(8,128)S(1)}) custom-call(s32[1,1,256]{2,1,0:T(1,128)S(1)} %get-tuple-element.445.refs_2_.refs_0_, s32[1,512,1]{2,1,0:T(8,128)S(1)} %copy-done.26, bf16[1,256,512]{2,1,0:T(8,128)(2,1)S(1)} %fusion.75.refs_2_, bf16[1,512,1024]{2,1,0:T(8,128)(2,1)S(1)} %bitcast.319, ...), custom_call_target="tpu_custom_call" | custom-call | flops 1 | bytes 1 | tf_op jit(solution)/shard_map/attend_forward/pallas_call | solution.py:232
  180.1 4.4 fusion.168
  201.4 9.2 %weight_gradients.4 = bf16[1024,4224]{1,0:T(8,128)(2,1)} custom-call(bf16[256,1024]{1,0:T(8,128)(2,1)S(1)} %copy-done.35, bf16[256,1024]{1,0:T(8,128)(2,1)S(1)} %multiply_convert_fusion.4.refs_1_, bf16[256,1024]{1,0:T(8,128)(2,1)S(1)} %copy-done.18, bf16[256,1024]{1,0:T(8,128)(2,1)S(1)} %copy-done.16, bf16[256,1408]{1,0:T(8,128)(2,1)S(1)} %get-tuple-element.380.refs_4_, ...), custom_call_target="tpu_custom_call" | custom-call | flops 1 | bytes 1 | tf_op jit(solution)/shard_map/weight_gradients/pallas_call | solution.py:357
  216.1 5.6 %attend_backward.4 = (bf16[1,256,512]{2,1,0:T(8,128)(2,1)S(1)}, bf16[1,512,512]{2,1,0:T(8,128)(2,1)S(1)}, bf16[1,512,512]{2,1,0:T(8,128)(2,1)S(1)}) custom-call(s32[1,1,256]{2,1,0:T(1,128)S(1)} %get-tuple-element.444.refs_2_.refs_0_, s32[1,512,1]{2,1,0:T(8,128)S(1)} %copy-done.29, bf16[1,256,512]{2,1,0:T(8,128)(2,1)S(1)} %copy-done.52, ...), custom_call_target="tpu_custom_call" | custom-call | flops 1 | bytes 1 | tf_op jit(solution)/shard_map/attend_backward/pallas_call | solution.py:268
  229.8 5.6 %attend_backward.5 = (bf16[1,256,512]{2,1,0:T(8,128)(2,1)S(1)}, bf16[1,512,512]{2,1,0:T(8,128)(2,1)S(1)}, bf16[1,512,512]{2,1,0:T(8,128)(2,1)S(1)}) custom-call(s32[1,1,256]{2,1,0:T(1,128)S(1)} %get-tuple-element.445.refs_2_.refs_0_, s32[1,512,1]{2,1,0:T(8,128)S(1)} %copy-done.27, bf16[1,256,512]{2,1,0:T(8,128)(2,1)S(1)} %copy-done.50, ...), custom_call_target="tpu_custom_call" | custom-call | flops 1 | bytes 1 | tf_op jit(solution)/shard_map/attend_backward/pallas_call | solution.py:268
  239.1 8.5 %weight_gradients.5 = (bf16[512,2048]{1,0:T(8,128)(2,1)}, bf16[512,2048]{1,0:T(8,128)(2,1)}) custom-call(s32[1,1]{1,0:T(1,128)} %bitcast.58.refs_0_, bf16[256,1024]{1,0:T(8,128)(2,1)S(1)} %copy-done.42, bf16[256,1024]{1,0:T(8,128)(2,1)S(1)} %copy-done.44, bf16[512,1024]{1,0:T(8,128)(2,1)} %bitcast.369, bf16[512,1024]{1,0:T(8,128)(2,1)} %bitcast.367, ...), custom_call_target="tpu_custom_call" | custom-call | flops 1 | bytes 1 | tf_op jit(solution)/shard_map/weight_gradients/pallas_call | solution.py:357
  256.2 3.5 fusion.123
  262.3 13.0 %attend_backward.6 = (bf16[1,256,512]{2,1,0:T(8,128)(2,1)S(1)}, bf16[1,1024,512]{2,1,0:T(8,128)(2,1)S(1)}, bf16[1,1024,512]{2,1,0:T(8,128)(2,1)S(1)}, f32[4,8,1280]{2,1,0:T(8,128)S(1)}) custom-call(s32[1,1]{1,0:T(1,128)} %bitcast.1.refs_0_, f32[4,8,1280]{2,1,0:T(8,128)S(1)} %concatenate.83.refs_1_, s32[1,1,256]{2,1,0:T(1,128)S(1)} %get-tuple-element.444.refs_2_.refs_0_, ...), custom_call_target="tpu_custom_call" | custom-call | flops 1 | bytes 1 | tf_op jit(solution)/shard_map/attend_backward/pallas_call | solution.py:268
  290.2 12.7 %attend_backward.7 = (bf16[1,256,512]{2,1,0:T(8,128)(2,1)S(1)}, bf16[1,1024,512]{2,1,0:T(8,128)(2,1)S(1)}, bf16[1,1024,512]{2,1,0:T(8,128)(2,1)S(1)}, f32[4,8,1280]{2,1,0:T(8,128)S(1)}) custom-call(s32[1,1]{1,0:T(1,128)} %bitcast.1.refs_0_, f32[4,8,1280]{2,1,0:T(8,128)S(1)} %concatenate.83.refs_1_, s32[1,1,256]{2,1,0:T(1,128)S(1)} %get-tuple-element.445.refs_2_.refs_0_, ...), custom_call_target="tpu_custom_call" | custom-call | flops 1 | bytes 1 | tf_op jit(solution)/shard_map/attend_backward/pallas_call | solution.py:268
  303.9 3.5 collective-permute-done.36
  316.7 12.4 %collective-permute-done.39 = bf16[256,1024]{1,0:T(8,128)(2,1)} collective-permute-done((bf16[256,1024]{1,0:T(8,128)(2,1)}, bf16[256,1024]{1,0:T(8,128)(2,1)}, u32[]{:S(2)}, u32[]{:S(2)}) %collective-permute-start.39) | collective-permute-done | bytes 524320 | tf_op jit(solution)/shard_map/ppermute | solution.py:734
  339.9 12.1 %weight_gradients.7 = (bf16[512,1024]{1,0:T(8,128)(2,1)}, bf16[512,1024]{1,0:T(8,128)(2,1)S(1)}) custom-call(s32[1,1]{1,0:T(1,128)} %bitcast.58.refs_0_, bf16[1024,1024]{1,0:T(8,128)(2,1)} %get-tuple-element.292.refs_1_.refs_3_, bf16[1024,1024]{1,0:T(8,128)(2,1)} %get-tuple-element.293.refs_2_.refs_4_, ...), custom_call_target="tpu_custom_call" | custom-call | flops 1 | bytes 1 | tf_op jit(solution)/shard_map/weight_gradients/pallas_call | solution.py:357
  362.9 3.9 collective-permute-start.45
  369.9 10.0 %collective-permute-done.32 = bf16[512,1024]{1,0:T(8,128)(2,1)S(1)} collective-permute-done((bf16[512,1024]{1,0:T(8,128)(2,1)}, bf16[512,1024]{1,0:T(8,128)(2,1)S(1)}, u32[]{:S(2)}, u32[]{:S(2)}) %collective-permute-start.32) | collective-permute-done | bytes 1048608 | tf_op jit(solution)/shard_map/ppermute | solution.py:734
  383.0 3.4 collective-permute-start.49
  387.8 3.4 collective-permute-start.48
  392.1 9.9 %collective-permute-done.46 = bf16[256,1024]{1,0:T(8,128)(2,1)S(1)} collective-permute-done((bf16[256,1024]{1,0:T(8,128)(2,1)S(1)}, bf16[256,1024]{1,0:T(8,128)(2,1)S(1)}, u32[]{:S(2)}, u32[]{:S(2)}) %collective-permute-start.46) | collective-permute-done | bytes 524320 | tf_op jit(solution)/shard_map/ppermute | solution.py:734
  403.7 3.3 fusion.83
  410.8 3.5 collective-permute-start.54
  414.3 4.4 collective-permute-start.50
  419.7 9.6 %collective-permute-done.51 = bf16[80,1024]{1,0:T(8,128)(2,1)S(1)} collective-permute-done((bf16[80,1024]{1,0:T(8,128)(2,1)S(1)}, bf16[80,1024]{1,0:T(8,128)(2,1)S(1)}, u32[]{:S(2)}, u32[]{:S(2)}) %collective-permute-start.51) | collective-permute-done | bytes 163872 | tf_op jit(solution)/shard_map/ppermute | solution.py:428
  435.9 3.7 finish.2
  (549 shorter events, 206.7 us)
Async XLA Ops:
  7.2 107.9 %all-gather.3.cloned.1.call-start = ((), (), s32[]{:S(2)}) async-start(), calls=%async_computation.1 | async-start | bytes 5570560 | tf_op jit(solution)/shard_map/all_gather | solution.py:457
  16.4 163.7 %all-gather.5.cloned.1.call-start = ((), (), s32[]{:S(2)}) async-start(), calls=%async_computation.2 | async-start | bytes 6127616 | tf_op jit(solution)/shard_map/all_gather | solution.py:457
  16.4 57.3 %collective-permute-start.6 = (bf16[144,1536]{1,0:T(8,128)(2,1)S(1)}, bf16[144,1536]{1,0:T(8,128)(2,1)S(1)}, u32[]{:S(2)}, u32[]{:S(2)}) collective-permute-start(bf16[144,1536]{1,0:T(8,128)(2,1)S(1)} %fusion.134.refs_0_), channel_id=1, source_target_pairs={{0,2},{2,0},{4,6},{6,4},{1,3},{3,1},{5,7},{7,5},{8,10},{10,8},{12,... | collective-permute-start | bytes 1327112 | tf_op jit(solution)/shard_map/ppermute | solution.py:413
  16.9 19.4 %collective-permute-start.2 = (bf16[144,1536]{1,0:T(8,128)(2,1)S(1)}, bf16[144,1536]{1,0:T(8,128)(2,1)}, u32[]{:S(2)}, u32[]{:S(2)}) collective-permute-start(bf16[144,1536]{1,0:T(8,128)(2,1)S(1)} %fusion.134.refs_0_), channel_id=1, source_target_pairs={{0,24},{8,0},{16,8},{24,16},{1,25},{9,1},{17,9},{25,17},{2,26},{10... | collective-permute-start | bytes 1327112 | tf_op jit(solution)/shard_map/ppermute | solution.py:428
  21.6 49.1 %collective-permute-start.1 = (bf16[144,1536]{1,0:T(8,128)(2,1)S(1)}, bf16[144,1536]{1,0:T(8,128)(2,1)}, u32[]{:S(2)}, u32[]{:S(2)}) collective-permute-start(bf16[144,1536]{1,0:T(8,128)(2,1)S(1)} %fusion.134.refs_0_), channel_id=1, source_target_pairs={{0,16},{8,24},{16,0},{24,8},{1,17},{9,25},{17,1},{25,9},{2,18},{10... | collective-permute-start | bytes 1327112 | tf_op jit(solution)/shard_map/ppermute | solution.py:428
  21.6 49.8 %collective-permute-start = (bf16[144,1536]{1,0:T(8,128)(2,1)S(1)}, bf16[144,1536]{1,0:T(8,128)(2,1)}, u32[]{:S(2)}, u32[]{:S(2)}) collective-permute-start(bf16[144,1536]{1,0:T(8,128)(2,1)S(1)} %fusion.134.refs_0_), channel_id=1, source_target_pairs={{0,8},{8,16},{16,24},{24,0},{1,9},{9,17},{17,25},{25,1},{2,10},{10... | collective-permute-start | bytes 1327112 | tf_op jit(solution)/shard_map/ppermute | solution.py:428
  22.6 49.5 %collective-permute-start.3 = (bf16[2,256,1024]{2,1,0:T(8,128)(2,1)S(1)}, bf16[2,256,1024]{2,1,0:T(8,128)(2,1)}, u32[]{:S(2)}, u32[]{:S(2)}) collective-permute-start(bf16[2,256,1024]{2,1,0:T(8,128)(2,1)S(1)} %copy-done.2), channel_id=1, source_target_pairs={{0,4},{2,6},{1,5},{3,7},{8,12},{10,14},{9,13},{11,15},{16,20},{18,... | collective-permute-start | bytes 3145736 | tf_op jit(solution)/shard_map/ppermute | solution.py:423
  28.8 380.9 %reduce-scatter.2.cloned.1.call-start = ((), (), s32[]{:S(2)}) async-start(), calls=%async_computation.3 | async-start | bytes 9191424 | tf_op jit(solution)/shard_map/reduce_scatter | solution.py:885
  94.9 40.9 %collective-permute-start.16 = (bf16[128,1408]{1,0:T(8,128)(2,1)S(1)}, bf16[128,1408]{1,0:T(8,128)(2,1)}, u32[]{:S(2)}, u32[]{:S(2)}) collective-permute-start(bf16[128,1408]{1,0:T(8,128)(2,1)S(1)} %dynamic-slice_bitcast_fusion.8.refs_0_), channel_id=1, source_target_pairs={{0,24},{8,0},{16,8},{24,16},{1,25},{9,1},{17,9},{25,17},{2,26},{10... | collective-permute-start | bytes 1081352 | tf_op jit(solution)/shard_map/ppermute | solution.py:428
  95.0 45.7 %collective-permute-start.15 = (bf16[128,1408]{1,0:T(8,128)(2,1)S(1)}, bf16[128,1408]{1,0:T(8,128)(2,1)}, u32[]{:S(2)}, u32[]{:S(2)}) collective-permute-start(bf16[128,1408]{1,0:T(8,128)(2,1)S(1)} %dynamic-slice_bitcast_fusion.8.refs_0_), channel_id=1, source_target_pairs={{0,16},{8,24},{16,0},{24,8},{1,17},{9,25},{17,1},{25,9},{2,18},{10... | collective-permute-start | bytes 1081352 | tf_op jit(solution)/shard_map/ppermute | solution.py:428
  97.1 43.6 %collective-permute-start.14 = (bf16[128,1408]{1,0:T(8,128)(2,1)S(1)}, bf16[128,1408]{1,0:T(8,128)(2,1)}, u32[]{:S(2)}, u32[]{:S(2)}) collective-permute-start(bf16[128,1408]{1,0:T(8,128)(2,1)S(1)} %dynamic-slice_bitcast_fusion.8.refs_0_), channel_id=1, source_target_pairs={{0,8},{8,16},{16,24},{24,0},{1,9},{9,17},{17,25},{25,1},{2,10},{10... | collective-permute-start | bytes 1081352 | tf_op jit(solution)/shard_map/ppermute | solution.py:428
  99.0 41.7 %collective-permute-start.11 = (bf16[2,128,1024]{2,1,0:T(8,128)(2,1)}, bf16[2,128,1024]{2,1,0:T(8,128)(2,1)}, u32[]{:S(2)}, u32[]{:S(2)}) collective-permute-start(bf16[2,128,1024]{2,1,0:T(8,128)(2,1)} %refs_0_.1), channel_id=1, source_target_pairs={{0,4},{2,6},{4,0},{6,2},{1,5},{3,7},{5,1},{7,3},{8,12},{10,14},{12... | collective-permute-start | bytes 1572872 | tf_op jit(solution)/shard_map/ppermute | solution.py:423
  172.0 18.8 %collective-permute-start.23 = (bf16[256,1024]{1,0:T(8,128)(2,1)}, bf16[256,1024]{1,0:T(8,128)(2,1)}, u32[]{:S(2)}, u32[]{:S(2)}) collective-permute-start(bf16[256,1024]{1,0:T(8,128)(2,1)} %convolution_convert_fusion.3), channel_id=1, source_target_pairs={{0,1},{1,0},{2,3},{3,2},{4,5},{5,4},{6,7},{7,6},{8,9},{9,8},{10,11... | collective-permute-start | bytes 1572872 | tf_op jit(solution)/shard_map/ppermute | solution.py:734
  190.2 20.5 %collective-permute-start.24 = (bf16[256,1024]{1,0:T(8,128)(2,1)S(1)}, bf16[256,1024]{1,0:T(8,128)(2,1)}, u32[]{:S(2)}, u32[]{:S(2)}) collective-permute-start(bf16[256,1024]{1,0:T(8,128)(2,1)S(1)} %fusion.64), channel_id=1, source_target_pairs={{0,1},{1,0},{2,3},{3,2},{4,5},{5,4},{6,7},{7,6},{8,9},{9,8},{10,11... | collective-permute-start | bytes 1572872 | tf_op jit(solution)/shard_map/ppermute | solution.py:734
  199.9 24.6 %collective-permute-start.26 = (bf16[256,1024]{1,0:T(8,128)(2,1)}, bf16[256,1024]{1,0:T(8,128)(2,1)}, u32[]{:S(2)}, u32[]{:S(2)}) collective-permute-start(bf16[256,1024]{1,0:T(8,128)(2,1)} %fusion.61), channel_id=1, source_target_pairs={{0,1},{1,0},{2,3},{3,2},{4,5},{5,4},{6,7},{7,6},{8,9},{9,8},{10,11... | collective-permute-start | bytes 1572872 | tf_op jit(solution)/shard_map/ppermute | solution.py:734
  261.1 18.3 %collective-permute-start.31 = (bf16[256,1024]{1,0:T(8,128)(2,1)S(1)}, bf16[256,1024]{1,0:T(8,128)(2,1)S(1)}, u32[]{:S(2)}, u32[]{:S(2)}) collective-permute-start(bf16[256,1024]{1,0:T(8,128)(2,1)S(1)} %copy-done.104), channel_id=1, source_target_pairs={{0,1},{1,0},{2,3},{3,2},{4,5},{5,4},{6,7},{7,6},{8,9},{9,8},{10,11... | collective-permute-start | bytes 1572872 | tf_op jit(solution)/shard_map/ppermute | solution.py:734
  285.9 21.5 %collective-permute-start.36 = (bf16[256,1024]{1,0:T(8,128)(2,1)S(1)}, bf16[256,1024]{1,0:T(8,128)(2,1)S(1)}, u32[]{:S(2)}, u32[]{:S(2)}) collective-permute-start(bf16[256,1024]{1,0:T(8,128)(2,1)S(1)} %get-tuple-element.402), channel_id=1, source_target_pairs={{4,0},{6,2},{5,1},{7,3},{12,8},{14,10},{13,9},{15,11},{20,16},{22,... | collective-permute-start | bytes 1572872 | tf_op jit(solution)/shard_map/ppermute | solution.py:423
  312.4 18.9 %collective-permute-start.38 = (bf16[512,1024]{1,0:T(8,128)(2,1)}, bf16[512,1024]{1,0:T(8,128)(2,1)}, u32[]{:S(2)}, u32[]{:S(2)}) collective-permute-start(bf16[512,1024]{1,0:T(8,128)(2,1)} %get-tuple-element.282), channel_id=1, source_target_pairs={{0,2},{2,0},{4,6},{6,4},{1,3},{3,1},{5,7},{7,5},{8,10},{10,8},{12,... | collective-permute-start | bytes 3145736 | tf_op jit(solution)/shard_map/ppermute | solution.py:413
  314.4 19.3 %collective-permute-start.37 = (bf16[2,256,1024]{2,1,0:T(8,128)(2,1)}, bf16[2,256,1024]{2,1,0:T(8,128)(2,1)}, u32[]{:S(2)}, u32[]{:S(2)}) collective-permute-start(bf16[2,256,1024]{2,1,0:T(8,128)(2,1)} %pad_maximum_fusion.4), channel_id=1, source_target_pairs={{0,2},{2,0},{4,6},{6,4},{1,3},{3,1},{5,7},{7,5},{8,10},{10,8},{12,... | collective-permute-start | bytes 3145736 | tf_op jit(solution)/shard_map/ppermute | solution.py:413
  315.0 47.9 %collective-permute-start.35 = (bf16[2,64,2048]{2,1,0:T(8,128)(2,1)}, bf16[2,64,2048]{2,1,0:T(8,128)(2,1)}, u32[]{:S(2)}, u32[]{:S(2)}) collective-permute-start(bf16[2,64,2048]{2,1,0:T(8,128)(2,1)} %get-tuple-element.382), channel_id=1, source_target_pairs={{0,24},{8,0},{16,8},{24,16},{1,25},{9,1},{17,9},{25,17},{2,26},{10... | collective-permute-start | bytes 1572872 | tf_op jit(solution)/shard_map/ppermute | solution.py:428
  315.1 51.7 %collective-permute-start.34 = (bf16[2,64,2048]{2,1,0:T(8,128)(2,1)}, bf16[2,64,2048]{2,1,0:T(8,128)(2,1)}, u32[]{:S(2)}, u32[]{:S(2)}) collective-permute-start(bf16[2,64,2048]{2,1,0:T(8,128)(2,1)} %get-tuple-element.383), channel_id=1, source_target_pairs={{0,16},{8,24},{16,0},{24,8},{1,17},{9,25},{17,1},{25,9},{2,18},{10... | collective-permute-start | bytes 1572872 | tf_op jit(solution)/shard_map/ppermute | solution.py:428
  329.1 37.7 %collective-permute-start.33 = (bf16[2,64,2048]{2,1,0:T(8,128)(2,1)}, bf16[2,64,2048]{2,1,0:T(8,128)(2,1)}, u32[]{:S(2)}, u32[]{:S(2)}) collective-permute-start(bf16[2,64,2048]{2,1,0:T(8,128)(2,1)} %get-tuple-element.384), channel_id=1, source_target_pairs={{0,8},{8,16},{16,24},{24,0},{1,9},{9,17},{17,25},{25,1},{2,10},{10... | collective-permute-start | bytes 1572872 | tf_op jit(solution)/shard_map/ppermute | solution.py:428
  353.7 26.2 %collective-permute-start.32 = (bf16[512,1024]{1,0:T(8,128)(2,1)}, bf16[512,1024]{1,0:T(8,128)(2,1)S(1)}, u32[]{:S(2)}, u32[]{:S(2)}) collective-permute-start(bf16[512,1024]{1,0:T(8,128)(2,1)} %convolution_convert_fusion), channel_id=1, source_target_pairs={{0,1},{1,0},{2,3},{3,2},{4,5},{5,4},{6,7},{7,6},{8,9},{9,8},{10,11... | collective-permute-start | bytes 3145736 | tf_op jit(solution)/shard_map/ppermute | solution.py:734
  358.5 43.5 %collective-permute-start.42 = (bf16[256,1024]{1,0:T(8,128)(2,1)S(1)}, bf16[256,1024]{1,0:T(8,128)(2,1)S(1)}, u32[]{:S(2)}, u32[]{:S(2)}) collective-permute-start(bf16[256,1024]{1,0:T(8,128)(2,1)S(1)} %copy-done.88), channel_id=1, source_target_pairs={{0,1},{1,0},{2,3},{3,2},{4,5},{5,4},{6,7},{7,6},{8,9},{9,8},{10,11... | collective-permute-start | bytes 1572872 | tf_op jit(solution)/shard_map/ppermute | solution.py:734
  362.9 20.1 %collective-permute-start.45 = (bf16[2,64,1024]{2,1,0:T(8,128)(2,1)S(1)}, bf16[2,64,1024]{2,1,0:T(8,128)(2,1)S(1)}, u32[]{:S(2)}, u32[]{:S(2)}) collective-permute-start(bf16[2,64,1024]{2,1,0:T(8,128)(2,1)S(1)} %copy-done.121), channel_id=1, source_target_pairs={{0,24},{8,0},{16,8},{24,16},{1,25},{9,1},{17,9},{25,17},{2,26},{10... | collective-permute-start | bytes 786440 | tf_op jit(solution)/shard_map/ppermute | solution.py:428
  366.8 21.0 %collective-permute-start.44 = (bf16[2,64,1024]{2,1,0:T(8,128)(2,1)S(1)}, bf16[2,64,1024]{2,1,0:T(8,128)(2,1)S(1)}, u32[]{:S(2)}, u32[]{:S(2)}) collective-permute-start(bf16[2,64,1024]{2,1,0:T(8,128)(2,1)S(1)} %copy-done.120), channel_id=1, source_target_pairs={{0,16},{8,24},{16,0},{24,8},{1,17},{9,25},{17,1},{25,9},{2,18},{10... | collective-permute-start | bytes 786440 | tf_op jit(solution)/shard_map/ppermute | solution.py:428
  366.8 24.4 %collective-permute-start.43 = (bf16[2,64,1024]{2,1,0:T(8,128)(2,1)S(1)}, bf16[2,64,1024]{2,1,0:T(8,128)(2,1)S(1)}, u32[]{:S(2)}, u32[]{:S(2)}) collective-permute-start(bf16[2,64,1024]{2,1,0:T(8,128)(2,1)S(1)} %copy-done.119), channel_id=1, source_target_pairs={{0,8},{8,16},{16,24},{24,0},{1,9},{9,17},{17,25},{25,1},{2,10},{10... | collective-permute-start | bytes 786440 | tf_op jit(solution)/shard_map/ppermute | solution.py:428
  379.9 22.1 %collective-permute-start.46 = (bf16[256,1024]{1,0:T(8,128)(2,1)S(1)}, bf16[256,1024]{1,0:T(8,128)(2,1)S(1)}, u32[]{:S(2)}, u32[]{:S(2)}) collective-permute-start(bf16[256,1024]{1,0:T(8,128)(2,1)S(1)} %fusion.68), channel_id=1, source_target_pairs={{0,1},{1,0},{2,3},{3,2},{4,5},{5,4},{6,7},{7,6},{8,9},{9,8},{10,11... | collective-permute-start | bytes 1572872 | tf_op jit(solution)/shard_map/ppermute | solution.py:734
  383.0 25.6 %collective-permute-start.49 = (bf16[64,2048]{1,0:T(8,128)(2,1)}, bf16[64,2048]{1,0:T(8,128)(2,1)}, u32[]{:S(2)}, u32[]{:S(2)}) collective-permute-start(bf16[64,2048]{1,0:T(8,128)(2,1)} %get-tuple-element.392), channel_id=1, source_target_pairs={{0,4},{2,6},{4,0},{6,2},{1,5},{3,7},{5,1},{7,3},{8,12},{10,14},{12... | collective-permute-start | bytes 786440 | tf_op jit(solution)/shard_map/ppermute | solution.py:423
  387.8 19.3 %collective-permute-start.48 = (bf16[4,64,1024]{2,1,0:T(8,128)(2,1)}, bf16[4,64,1024]{2,1,0:T(8,128)(2,1)}, u32[]{:S(2)}, u32[]{:S(2)}) collective-permute-start(bf16[4,64,1024]{2,1,0:T(8,128)(2,1)} %get-tuple-element.394), channel_id=1, source_target_pairs={{0,4},{2,6},{4,0},{6,2},{1,5},{3,7},{5,1},{7,3},{8,12},{10,14},{12... | collective-permute-start | bytes 1572872 | tf_op jit(solution)/shard_map/ppermute | solution.py:423
  392.0 26.7 %collective-permute-start.47 = (bf16[64,1024]{1,0:T(8,128)(2,1)}, bf16[64,1024]{1,0:T(8,128)(2,1)}, u32[]{:S(2)}, u32[]{:S(2)}) collective-permute-start(bf16[64,1024]{1,0:T(8,128)(2,1)} %get-tuple-element.416), channel_id=1, source_target_pairs={{0,4},{2,6},{4,0},{6,2},{1,5},{3,7},{5,1},{7,3},{8,12},{10,14},{12... | collective-permute-start | bytes 393224 | tf_op jit(solution)/shard_map/ppermute | solution.py:423
  410.8 21.4 %collective-permute-start.54 = (bf16[64,6272]{1,0:T(8,128)(2,1)S(1)}, bf16[64,6272]{1,0:T(8,128)(2,1)S(1)}, u32[]{:S(2)}, u32[]{:S(2)}) collective-permute-start(bf16[64,6272]{1,0:T(8,128)(2,1)S(1)} %pad_maximum_fusion.7), channel_id=1, source_target_pairs={{0,4},{2,6},{4,0},{6,2},{1,5},{3,7},{5,1},{7,3},{8,12},{10,14},{12... | collective-permute-start | bytes 2408456 | tf_op jit(solution)/shard_map/ppermute | solution.py:423
  (156 other events, 1133.8 us)
Sparse Core Ops, SparseCore 0:
  16.5 81.5 all-gather.2
  101.0 73.1 all-gather.4
  210.8 107.3 reduce-scatter.1

commit v3 on v2

--- a/solution.py
+++ b/solution.py
@@ -11,6 +11,7 @@
 EXTRA = 16
 TINY = pl.CostEstimate(flops=1, bytes_accessed=1, transcendentals=0)
 LANES = 128
+STRIP = 64
 CHUNK = 256
 NT = (((1,), (1,)), ((), ()))
 NN = (((1,), (0,)), ((), ()))
@@ -239,7 +240,7 @@
             jax.ShapeDtypeStruct((seqs, pairs, 8, rows), jnp.float32),
         ],
         scratch_shapes=scratch,
-        compiler_params=pltpu.CompilerParams(vmem_limit_bytes=40 * 1024 * 1024),
+        compiler_params=pltpu.CompilerParams(vmem_limit_bytes=16 * 1024 * 1024),
         cost_estimate=TINY,
         name="attend_forward",
     )(*args)
@@ -272,7 +273,7 @@
         out_specs=out_specs,
         out_shape=out_shape,
         scratch_shapes=scratch,
-        compiler_params=pltpu.CompilerParams(vmem_limit_bytes=40 * 1024 * 1024),
+        compiler_params=pltpu.CompilerParams(vmem_limit_bytes=18 * 1024 * 1024),
         cost_estimate=TINY,
         name="attend_backward",
     )(*args)
@@ -361,7 +362,7 @@
         out_specs=out_specs,
         out_shape=shapes,
         scratch_shapes=[pltpu.VMEM((width, longest), jnp.bfloat16)],
-        compiler_params=pltpu.CompilerParams(vmem_limit_bytes=48 * 1024 * 1024),
+        compiler_params=pltpu.CompilerParams(vmem_limit_bytes=36 * 1024 * 1024),
         cost_estimate=TINY,
         name="weight_gradients",
     )(*args)
@@ -489,7 +490,7 @@
             out_specs=pl.BlockSpec(block, where),
         ),
         out_shape=jax.ShapeDtypeStruct(shape, pieces[0].dtype),
-        compiler_params=pltpu.CompilerParams(vmem_limit_bytes=40 * 1024 * 1024),
+        compiler_params=pltpu.CompilerParams(vmem_limit_bytes=16 * 1024 * 1024),
         cost_estimate=TINY,
         name="assemble",
     )(places, *pieces)
@@ -540,7 +541,7 @@
     return held
 
 
-def fold_start(segments, columns):
+def fold_start(segments, columns, arrive=None):
     high, low = ctx_shape()
     at_high, at_low = ctx_place()
     count = lax.axis_size("fsdp")
@@ -550,23 +551,26 @@
     if low == 2:
         place = jnp.full((1, 1), at_low, jnp.int32)
         away, kept = gradient_blocks(segments, columns, place, rows)
-        return [kept.reshape(shape), swap_low(away).reshape(shape)], away
+        done = away
+        if arrive is not None:
+            arrive, away = before((arrive, away), away)
+            done = (arrive, done)
+        return [kept.reshape(shape), swap_low(away).reshape(shape)], done
     kept = gradient_blocks(segments, columns)
-    return [kept.reshape(shape)], kept
-
-
-def fold_high(halves, earlier=()):
+    return [kept.reshape(shape)], kept if arrive is None else (before(arrive, kept), kept)
+
+
+def fold_high(parts, earlier=()):
     high, low = ctx_shape()
     at_high, at_low = ctx_place()
-    halves = before(halves, earlier)
-
-    def part(at):
-        return low_cast(sum(wide_cast(lax.dynamic_index_in_dim(h, at, 1, False)) for h in halves))
-
-    sent = [part((at_high + step) % high) for step in range(1, high)]
-    mine = part(at_high)
-    moved = [shift_high(piece, step + 1, True) for step, piece in enumerate(sent)]
-    return [mine] + moved, (mine, sent)
+    parts = before(parts, earlier)
+    found, sent = [], []
+    for step in range(1, high):
+        mine, piece = split_sum(parts, [at_high, (at_high + step) % high])
+        found = found or [mine]
+        sent.append(piece)
+        found.append(shift_high(piece, step, True))
+    return found, (found[0], sent)
 
 
 def fold_fsdp(parts, lines, earlier=()):
@@ -625,9 +629,60 @@
     return [mine] + moved, (mine, sent)
 
 
+def swap_fsdp(value, bit):
+    count = lax.axis_size("fsdp")
+    return lax.ppermute(value, "fsdp", [(i, i ^ bit) for i in range(count)])
+
+
+def doubles(count):
+    return count <= 8 and count & (count - 1) == 0
+
+
+def fold_fsdp_start(parts, lines=None, earlier=()):
+    count = lax.axis_size("fsdp")
+    index = lax.axis_index("fsdp")
+    parts, lines = before((parts, lines), earlier)
+    rest = parts[0].shape[1:]
+    small = None
+    if lines is not None:
+        small = jnp.zeros((count, EXTRA, rest[-1]), jnp.bfloat16)
+        small = small.at[:, 0, : lines.shape[1]].set(low_cast(lines))
+    if not doubles(count):
+        whole = low_cast(sum(wide_cast(p) for p in parts))
+        if small is not None:
+            whole = jnp.concatenate([whole, small], axis=1)
+        flat = whole.reshape((-1,) + whole.shape[2:])
+        part = lax.psum_scatter(flat, "fsdp", scatter_dimension=0, tiled=True)
+        return [part.reshape((1,) + whole.shape[1:])], whole
+    views = [p.reshape((count // 2, 2) + (-1, rest[-1])) for p in parts]
+    if small is not None:
+        small = small.reshape(count // 2, 2, EXTRA, rest[-1])
+    mine, sent = split_sum(views, [index % 2, 1 - index % 2], small)
+    shape = (count // 2,) + (rest if small is None else mine.shape[1:])
+    return [mine.reshape(shape), swap_fsdp(sent, 1).reshape(shape)], (mine, sent)
+
+
+def fold_fsdp_rest(parts, earlier=()):
+    count = lax.axis_size("fsdp")
+    index = lax.axis_index("fsdp")
+    parts = before(parts, earlier)
+    done = parts[0]
+    bit = 2
+    while doubles(count) and bit < count:
+        rest = parts[0].shape[1:]
+        views = [p.reshape((p.shape[0] // 2, 2) + (-1, rest[-1])) for p in parts]
+        at = (index // bit) % 2
+        mine, sent = split_sum(views, [at, 1 - at])
+        done = (mine, sent)
+        parts = [v.reshape((-1,) + rest) for v in (mine, swap_fsdp(sent, bit))]
+        bit *= 2
+    return parts, done
+
+
 def fold_own(parts, earlier=()):
     parts = before(parts, earlier)
-    return low_cast(sum(wide_cast(p) for p in parts))
+    total = add_parts(parts) if len(parts) > 1 else parts[0]
+    return total.reshape(-1, total.shape[-1])
 
 
 def spread_high(part):
@@ -637,54 +692,61 @@
 
 def spread_low(parts, earlier=()):
     high, low = ctx_shape()
-    held = jnp.stack(before(parts, earlier))
-    return [held, swap_low(held) if low == 2 else held], held
-
-
-def finish_kernel(high, low, cuts, extra, place_ref, mine_ref, other_ref, *outs):
-    rows = mine_ref.shape[1] - extra
+    parts = before(parts, earlier)
+    return parts, [swap_low(p) if low == 2 else p for p in parts]
+
+
+def finish_kernel(high, low, cuts, extra, place_ref, *refs):
+    mine_refs, other_refs, outs = refs[:high], refs[high : 2 * high], refs[2 * high :]
+    rows = mine_refs[0].shape[0] - extra
+
+    def chosen(at_high, at_low, start, stop):
+        step = lax.rem(place_ref[0, 0] - at_high + high, high)
+        value = None
+        for index in range(high):
+            mine = mine_refs[index][:rows, start:stop]
+            other = other_refs[index][:rows, start:stop]
+            piece = jnp.where(place_ref[0, 1] == at_low, mine, other)
+            value = piece if value is None else jnp.where(step == index, piece, value)
+        return wide_cast(value)
+
     for (start, stop, turned), out in zip(cuts, outs):
-        blocks = []
-        for at_high in range(high):
-            step = lax.rem(place_ref[0, 0] - at_high + high, high)
-            for at_low in range(low):
-                mine = mine_ref[step, :rows, start:stop]
-                other = other_ref[step, :rows, start:stop]
-                chosen = jnp.where(place_ref[0, 1] == at_low, mine, other)
-                blocks.append(chosen.astype(jnp.float32))
-        whole = jnp.concatenate(blocks, axis=0)
-        out[...] = whole.T if turned else whole
+        blocks = [chosen(h, l, start, stop) for h in range(high) for l in range(low)]
+        if turned:
+            out[...] = jnp.concatenate(blocks, axis=0).T
+        else:
+            for index, block in enumerate(blocks):
+                out[pl.ds(index * rows, rows), :] = block
     if extra:
         total = None
-        for step in range(high):
-            for ref in (mine_ref, other_ref)[:low]:
-                line = ref[step, rows:, :].astype(jnp.float32)
-                total = line if total is None else total + line
+        for ref in mine_refs + (other_refs if low == 2 else ()):
+            line = wide_cast(ref[rows:, :])
+            total = line if total is None else total + line
         outs[-1][...] = total
 
 
-def spread_end(pair, cuts, extra=0, earlier=()):
+def spread_end(pair, cuts, extra=0):
     high, low = ctx_shape()
     at_high, at_low = ctx_place()
-    mine, other = before(pair, earlier)
-    rows = mine.shape[1] - extra
+    mine, other = pair
+    rows = mine[0].shape[0] - extra
     shapes = []
     for start, stop, turned in cuts:
         shape = (high * low * rows, stop - start)
         shapes.append(jax.ShapeDtypeStruct(shape[::-1] if turned else shape, jnp.float32))
     if extra:
-        shapes.append(jax.ShapeDtypeStruct((extra, mine.shape[2]), jnp.float32))
+        shapes.append(jax.ShapeDtypeStruct((extra, mine[0].shape[1]), jnp.float32))
     place = jnp.stack([at_high, at_low]).astype(jnp.int32).reshape(1, 2)
-    whole = pl.BlockSpec(memory_space=pltpu.VMEM)
+    vmem = pl.BlockSpec(memory_space=pltpu.VMEM)
     return pl.pallas_call(
         functools.partial(finish_kernel, high, low, cuts, extra),
-        in_specs=[pl.BlockSpec(memory_space=pltpu.SMEM), whole, whole],
-        out_specs=[whole] * len(shapes),
+        in_specs=[pl.BlockSpec(memory_space=pltpu.SMEM)] + [vmem] * (2 * high),
+        out_specs=[vmem] * len(shapes),
         out_shape=shapes,
-        compiler_params=pltpu.CompilerParams(vmem_limit_bytes=48 * 1024 * 1024),
+        compiler_params=pltpu.CompilerParams(vmem_limit_bytes=20 * 1024 * 1024),
         cost_estimate=TINY,
         name="finish",
-    )(place, mine, other)
+    )(place, *mine, *other)
 
 
 def block_fold_start(lefts, rights):
@@ -725,6 +787,147 @@
 def block_fold_end(parts, earlier=()):
     parts = before(parts, earlier)
     return low_cast(sum(wide_cast(p) for p in parts))
+
+
+def norm_backward(parts, rest_ref, values_ref, gain_ref, out_ref, low_ref, gain_out_ref):
+    gain = wide_cast(gain_ref[...])
+    total = jnp.zeros((8, gain.shape[1]), jnp.float32)
+    for start in range(0, rest_ref.shape[0], STRIP):
+        at = pl.ds(start, STRIP)
+        unit, inverse, normed = rms_rows(wide_cast(values_ref[at, :]), gain)
+        grad = sum(wide_cast(p[at, :]) for p in parts)
+        product = grad * unit
+        for row in range(0, STRIP, 8):
+            total = total + product[row : row + 8]
+        inner = jnp.mean(product * gain, axis=1, keepdims=True)
+        result = wide_cast(rest_ref[at, :]) + inverse * (grad * gain - unit * inner)
+        if out_ref is not None:
+            out_ref[at, :] = result
+        low_ref[at, :] = low_cast(result)
+    gain_out_ref[...] = total
+
+
+def rms_rows(values, gain):
+    inverse = lax.rsqrt(jnp.mean(values * values, axis=1, keepdims=True) + EPSILON)
+    unit = values * inverse
+    return unit, inverse, low_cast(unit * gain)
+
+
+def project_end_kernel(mine_ref, moved_ref, dq_ref, wide_ref, own_ref):
+    width = dq_ref.shape[1]
+    folded = low_cast(wide_cast(mine_ref[...]) + wide_cast(moved_ref[...]))
+    for start in range(0, own_ref.shape[1], CHUNK):
+        at = pl.ds(start, CHUNK)
+        total = dot(dq_ref[...], wide_ref[at, :width], NT)
+        own_ref[:, at] = low_cast(total + dot(folded, wide_ref[at, width:], NT))
+
+
+def project_end(parts, dq, wide_weights):
+    vmem = pl.BlockSpec(memory_space=pltpu.VMEM)
+    return pl.pallas_call(
+        project_end_kernel,
+        in_specs=[vmem] * 4,
+        out_specs=vmem,
+        out_shape=jax.ShapeDtypeStruct((dq.shape[0], wide_weights.shape[0]), jnp.bfloat16),
+        compiler_params=pltpu.CompilerParams(vmem_limit_bytes=16 * 1024 * 1024),
+        cost_estimate=TINY,
+        name="project_end",
+    )(parts[0], parts[1], dq, wide_weights)
+
+
+def last_norm_kernel(part_ref, moved_ref, rest_ref, values_ref, gain_ref, low_ref, gain_out_ref):
+    norm_backward([part_ref, moved_ref], rest_ref, values_ref, gain_ref, None, low_ref,
+                  gain_out_ref)
+
+
+def last_norm(parts, rest, values, gain):
+    vmem = pl.BlockSpec(memory_space=pltpu.VMEM)
+    return pl.pallas_call(
+        last_norm_kernel,
+        in_specs=[vmem] * 5,
+        out_specs=[vmem] * 2,
+        out_shape=[jax.ShapeDtypeStruct(rest.shape, jnp.bfloat16), jax.ShapeDtypeStruct((8, rest.shape[1]), jnp.float32)],
+        compiler_params=pltpu.CompilerParams(vmem_limit_bytes=16 * 1024 * 1024),
+        cost_estimate=TINY,
+        name="last_norm",
+    )(parts[0], parts[1], rest, values, gain)
+
+
+def add_kernel(count, *refs):
+    total = sum(wide_cast(r[...]) for r in refs[:count])
+    refs[count][...] = low_cast(total)
+
+
+def add_parts(parts):
+    vmem = pl.BlockSpec(memory_space=pltpu.VMEM)
+    return pl.pallas_call(
+        functools.partial(add_kernel, len(parts)),
+        in_specs=[vmem] * len(parts),
+        out_specs=vmem,
+        out_shape=jax.ShapeDtypeStruct(parts[0].shape, jnp.bfloat16),
+        compiler_params=pltpu.CompilerParams(vmem_limit_bytes=16 * 1024 * 1024),
+        cost_estimate=TINY,
+        name="add_parts",
+    )(*parts)
+
+
+def split_sum(parts, places, extra=None):
+    shape = parts[0].shape
+    rest = (0,) * (len(shape) - 2)
+    places = jnp.stack([jnp.asarray(v, jnp.int32) for v in places])
+    specs = []
+    for which in range(2):
+        for part in parts:
+            if len(part.shape) == len(shape):
+                spec = pl.BlockSpec(
+                    (1, 1) + shape[2:], lambda i, place, which=which: (i, place[which]) + rest
+                )
+            else:
+                spec = pl.BlockSpec(
+                    (1, 1, 1) + shape[2:],
+                    lambda i, place, which=which: (i, place[which], place[2]) + rest,
+                )
+            specs.append(spec)
+    args = list(parts) + list(parts)
+    added = 0
+    if extra is not None:
+        added = extra.shape[2]
+        args += [extra, extra]
+        for which in range(2):
+            specs.append(
+                pl.BlockSpec(
+                    (1, 1) + extra.shape[2:],
+                    lambda i, place, which=which: (i, place[which]) + rest,
+                )
+            )
+    out_shape = (shape[2] + added,) + shape[3:]
+    out = jax.ShapeDtypeStruct((shape[0],) + out_shape, jnp.bfloat16)
+    out_spec = pl.BlockSpec((1,) + out_shape, lambda i, place: (i,) + rest)
+
+    def kernel(place_ref, *refs):
+        for which in range(2):
+            total = None
+            for ref in refs[which * len(parts) : (which + 1) * len(parts)]:
+                value = wide_cast(ref[...]).reshape(shape[2:])
+                total = value if total is None else total + value
+            out_ref = refs[len(args) + which]
+            out_ref[0, : shape[2]] = low_cast(total)
+            if added:
+                out_ref[0, shape[2] :] = refs[2 * len(parts) + which][0, 0]
+
+    return pl.pallas_call(
+        kernel,
+        grid_spec=pltpu.PrefetchScalarGridSpec(
+            num_scalar_prefetch=1,
+            grid=(shape[0],),
+            in_specs=specs,
+            out_specs=[out_spec, out_spec],
+        ),
+        out_shape=[out, out],
+        compiler_params=pltpu.CompilerParams(vmem_limit_bytes=16 * 1024 * 1024),
+        cost_estimate=TINY,
+        name="split_sum",
+    )(places, *args)
 
 
 def pair_start(partial):
@@ -775,6 +978,7 @@
     gain_rows = self_gain.shape[0]
     offset = lax.axis_index("ctx") * row_count
     every = range(seqs)
+    last = seqs - 1
 
     small = jnp.concatenate([self_gain, cross_gain, ffn_gain, position_bias.reshape(-1)])
     line = jnp.zeros((EXTRA, 3 * hw), jnp.bfloat16).at[0, : small.shape[0]].set(small)
@@ -880,7 +1084,12 @@
     cotangent = [out_cotangent[s] for s in every]
     low_three = [n[2] for n in norm_three]
     ffn_blocks = gradient_blocks(
-        [(low_three, grads_gate), (low_three, grads_up), (cotangent, units_out)], units
+        [
+            (before(low_three, done, pair_three[0]), grads_gate),
+            (low_three, grads_up),
+            (cotangent, units_out),
+        ],
+        units,
     )
     ffn_part = lax.psum_scatter(ffn_blocks, ("fsdp", "ctx"), scatter_dimension=0, tiled=True)
 
@@ -905,7 +1114,10 @@
         parts, done = pair_start(mm_back(rows, query_cross))
         pair_four.append(parts)
     encoder_rows = [encoder_all[s] for s in every]
-    middle, middle_blocks = fold_start(
+    pair_out = []
+    parts, done = pair_start(mm_back(before(units_out[0], done), down))
+    pair_out.append(parts)
+    middle, done = fold_start(
         [
             (before([n[2] for n in norm_two], done), dq_two),
             (encoder_rows, dk_two),
@@ -918,9 +1130,13 @@
     res_one, low_one, dq_one, dk_one, dv_one, gain_two, line_grads, folds = (
         [], [], [], [], [], [], [], [],
     )
-    encoder_fold, encoder_done = block_fold_start(before(dk_two, middle_blocks), dv_two)
-    done = (done, middle_blocks, encoder_done)
-    pair_states, pair_out, pair_six = None, None, []
+    encoder_fold, done = block_fold_start(before(dk_two, done), dv_two)
+    layer_output = []
+
+    def finish_output(s, earlier):
+        layer_output.append(low_cast(after_two[s] + pair_end(pair_out[s], earlier)))
+        return layer_output[-1]
+
     for s in every:
         grad_from, gain = rms_backward(
             pair_end(pair_four[s], done), norm_two[s][0], norm_two[s][1], gain_cross
@@ -930,15 +1146,12 @@
         low_one.append(low_cast(res_one[s]))
         grad_attended = low_cast(mm(low_one[s], output_self))
         if s == 0:
-            middle, done = fold_fsdp_first(middle, grad_attended)
-            encoder_fold, encoder_done = block_fold_high(encoder_fold, False, done)
-            done = (done, encoder_done)
+            encoder_fold, done = block_fold_high(encoder_fold, False, grad_attended)
+            done = finish_output(0, done)
         else:
             folds[s - 1], done = block_fold_high(folds[s - 1], True, grad_attended)
-            if s == 1:
-                rows = jnp.concatenate(before(units_out, done), axis=0)
-                pair_out, own = pair_start(mm_back(rows, down))
-                done = (done, own)
+            parts, done = pair_start(mm_back(before(units_out[s], done), down))
+            pair_out.append(parts)
         dq, dk, dv, line = attend_backward(
             q_one[s][None], kv_one[s][None], one(query_docs, s), one(dec_docs, s),
             att_one[s], log_one[s], before(grad_attended, done)[None], place, lines,
@@ -950,43 +1163,52 @@
         if s == 0:
             folded = block_fold_end(encoder_fold, dk)
             pair_states, own = pair_start(mm_back(folded, pair_cross))
-            fold, done = block_fold_start(before([dk[0]], own), [dv[0]])
+            done = own
+        if s < last:
+            fold, done = block_fold_start(before([dk[0]], done), [dv[0]])
             folds.append(fold)
-        elif s < seqs - 1:
-            fold, done = block_fold_start([dk[0]], [dv[0]])
-            folds.append(fold)
-
-    last = seqs - 1
+
+    arrived = before((folds, pair_out[1:]), dk_one[last])
+    folds, pair_out[1:] = arrived
+    fold, done = block_fold_start(before([dk_one[last]], arrived), [dv_one[last]])
+    pair_six = []
     for s in range(last):
-        folded = block_fold_end(folds[s], dk_one[last])
-        parts, done = pair_start(mm_back(dq_one[s], query_self) + mm_back(folded, pair_self))
+        parts, done = pair_start(project_end(before(folds[s], done), dq_one[s], first_weights))
         pair_six.append(parts)
+    fold, done = block_fold_high(fold, True, done)
     first, done = fold_start(
         [(before(low_one, done), [a[0] for a in att_one]), ([n[2] for n in norm_one], dq_one)], hw
     )
-    fold, done = block_fold_start(before([dk_one[last]], done), [dv_one[last]])
-    states = pair_end(pair_states, done)
-    grad_states = low_cast(states).reshape(seqs, -1, width)
-    first, done = fold_fsdp_first(first, (done, grad_states))
-    fold, done = block_fold_high(fold, True, done)
-    second, second_blocks = fold_start([(before(norm_all, done), dk_one), (norm_all, dv_one)], hw)
-    folded = block_fold_end(fold, second_blocks)
-    parts, done = pair_start(mm_back(dq_one[last], query_self) + mm_back(folded, pair_self))
+    second, (arrived, done) = fold_start(
+        [(before(norm_all, done), dk_one), (norm_all, dv_one)], hw, (fold, pair_six)
+    )
+    fold, pair_six = arrived
+    parts, done = pair_start(project_end(before(fold, arrived), dq_one[last], first_weights))
     pair_six.append(parts)
+    ffn_spread = spread_high(before(ffn_part, done))
+    middle, done = fold_fsdp_start(middle, None, ffn_spread[0])
     second, done = fold_high(second, done)
-    middle, done = fold_high_last(middle, done)
-    out_rows = pair_end(pair_out, done)
-    layer_output = [
-        low_cast(after_two[s] + out_rows[s * row_count : (s + 1) * row_count]) for s in every
-    ]
-    first, done = fold_high_last(first, layer_output)
+    first, done = fold_fsdp_start(first, None, done)
     grad_input, gain_one = [], []
-    for s in every:
-        grad_from, gain = rms_backward(
-            pair_end(pair_six[s], done), norm_one[s][0], norm_one[s][1], gain_self
+
+    gain_row = gain_self.reshape(1, -1)
+
+    def finish_sequence(s, earlier):
+        rows, gain = last_norm(
+            before(pair_six[s], earlier), res_one[s], hidden_in[s], gain_row
         )
-        gain_one.append(gain)
-        grad_input.append(low_cast(res_one[s] + grad_from))
+        gain_one.append(jnp.sum(gain, axis=0))
+        grad_input.append(rows)
+        return rows
+
+    for s in range(last):
+        done = finish_sequence(s, done)
+    line_grads = before(line_grads, done)
+    for s in range(1, seqs):
+        done = finish_output(s, done)
+    ffn_spread = spread_low(ffn_spread, done)
+    second = before(second, done)
+    done = finish_sequence(last, second)
     line_total = sum(line_grads)[:, :2].reshape(head_count, row_count + length)
     spread = lax.dynamic_update_slice_in_dim(
         jnp.zeros((head_count, 2 * length), jnp.float32), line_total, offset, 1
@@ -994,28 +1216,30 @@
     grad_bias = jnp.dot(spread, bucket_onehot, precision=lax.Precision.HIGHEST).T
     totals = [sum(g).reshape(shards, gain_rows) for g in (gain_one, gain_two, gain_three)]
     totals = jnp.concatenate(totals + [grad_bias.reshape(shards, -1)], axis=1)
-    second, done = fold_fsdp(second, totals, grad_input)
-    middle_part = fold_own(middle, done)
-    outer = spread_high(jnp.concatenate([before(ffn_part, done), middle_part], axis=1))
-    first_part_sum = fold_own(first, outer[0])
-    second_part = fold_own(second, first_part_sum)
-    inner = jnp.concatenate(
-        [jnp.pad(first_part_sum, ((0, EXTRA), (0, 0))),
-         second_part],
-        axis=1,
-    )
-    outer, done = spread_low(outer, inner)
+    second, done = fold_fsdp_start(second, totals, grad_input)
+    middle, done = fold_fsdp_rest(middle, done)
+    first, done = fold_fsdp_rest(first, done)
+    second, done = fold_fsdp_rest(second, done)
+    middle, done = fold_high(middle, done)
+    first, done = fold_high(first, done)
+    middle_sum = fold_own(middle, done)
+    middle_spread = spread_high(middle_sum)
+    second_sum = fold_own(second, middle_sum)
+    done = second_sum
+    ffn_gate_grad, ffn_up_grad, ffn_down_grad = spread_end(
+        before(ffn_spread, done),
+        [(0, units, False), (units, 2 * units, False), (2 * units, 3 * units, True)],
+    )
+    middle_spread = spread_low(middle_spread, ffn_gate_grad)
+    first_sum = fold_own(first, middle_spread[0])
+    inner = jnp.concatenate([jnp.pad(first_sum, ((0, EXTRA), (0, 0))), second_sum], axis=1)
     inner = spread_high(inner)
-    edge = 3 * units
-    ffn_gate_grad, ffn_up_grad, ffn_down_grad, cross_q, cross_k, cross_v, cross_o = spread_end(
-        outer,
-        [
-            (0, units, False), (units, 2 * units, False), (2 * units, edge, True),
-            (edge, edge + hw, False), (edge + hw, edge + 2 * hw, False),
-            (edge + 2 * hw, edge + 3 * hw, False), (edge + 3 * hw, edge + 4 * hw, True),
-        ],
-    )
-    inner, done = spread_low(inner, ffn_gate_grad)
+    cross_q, cross_k, cross_v, cross_o = spread_end(
+        before(middle_spread, inner[0]),
+        [(0, hw, False), (hw, 2 * hw, False), (2 * hw, 3 * hw, False), (3 * hw, 4 * hw, True)],
+    )
+    inner = spread_low(inner, cross_q)
+    grad_states = low_cast(pair_end(pair_states, inner[0])).reshape(seqs, -1, width)
     self_o, self_q, self_k, self_v, sums = spread_end(
         inner,
         [(0, hw, True), (hw, 2 * hw, False), (2 * hw, 3 * hw, False), (3 * hw, 4 * hw, False)],

time: 464 us -> 452 us (0.974)
  other arithmetic: 60.8 us -> 35 us
  Pallas kernels: 112 us -> 127 us
  local copies, waits for them, and re-layouts: 43 us -> 58 us
  matrix products: 62.2 us -> 49.2 us
  starting transfers between devices: 56.8 us -> 51.9 us
    ppermute x0 -> x6, waiting for transfers between devices: none -> 34.4 us  [swap_fsdp(): return lax.ppermute(value, 'fsdp', [(i, i ^ bit) for i in range(count)])]
    ppermute x12 -> x13, waiting for transfers between devices: 33.4 us -> 8.62 us  [pair_start(): lax.ppermute(own, 'tp', [(i, (i + step) % count) for i in range(count)])]
    pallas_call x0 -> x16, Pallas kernels: none -> 20.3 us  [the longest x9 14.9 us: split_sum(): pl.pallas_call(kernel, grid_spec=pltpu.PrefetchScalarGridSpec(num_scalar_...]
    convert_element_type x19 -> x12, other arithmetic: 33.9 us -> 14.5 us  [low_cast(): return value.astype(jnp.bfloat16)]
    ppermute x15 -> x6, waiting for transfers between devices: 55.7 us -> 36.7 us  [shift_fsdp(): lax.ppermute(value, 'fsdp', [(i, (i + step) % count) for i in range(count)])]
    ppermute x10 -> x11, waiting for transfers between devices: 9.47 us -> 24.6 us  [shift_high(): return lax.ppermute(value, 'ctx', pairs)]
    unnamed x271 -> x281, local copies, waits for them, and re-layouts: 24.8 us -> 39 us
    dot_general x32 -> x29, matrix products: 61.2 us -> 47.6 us  [dot(): return lax.dot_general(lhs, rhs, dims, preferred_element_type=jnp.float32)]
  transfers between devices with their start and end apart: 60 -> 63, of which waited for: 20 -> 20; matrix products, arithmetic and copies ran while one was open for 30% -> 22% of each run, Pallas kernels for 24% -> 26%
where the time goes in v3:
time: 452 us; the launch traced here: 444 us
  Pallas kernels  127 us (28%)
  waiting for transfers between devices  106 us (23%)
  local copies, waits for them, and re-layouts  58 us (13%)
  starting transfers between devices  51.9 us (11%)
  matrix products  49.2 us (11%)
  other arithmetic  35 us (8%)
  between operations  16.7 us (4%)
    dot_general x29, matrix products, dot(): return lax.dot_general(lhs, rhs, dims, preferred_element_type=jnp.float32)  47.6 us
    unnamed x281, local copies, waits for them, and re-layouts  39 us
    pallas_call x4, Pallas kernels, attend_backward(): pl.pallas_call(functools.partial(backward_kernel, causal), grid=(pairs, s...  37.1 us
    ppermute x6, waiting for transfers between devices, shift_fsdp(): lax.ppermute(value, 'fsdp', [(i, (i + step) % count) for i in range(count)])  36.7 us
    ppermute x6, waiting for transfers between devices, swap_fsdp(): return lax.ppermute(value, 'fsdp', [(i, i ^ bit) for i in range(count)])  34.4 us
    pallas_call x4, Pallas kernels, gradient_blocks(): pl.pallas_call(functools.partial(gradient_kernel, spans, tokens, split),...  25.2 us
    ppermute x11, waiting for transfers between devices, shift_high(): return lax.ppermute(value, 'ctx', pairs)  24.6 us
    pallas_call x4, Pallas kernels, attend_forward(): pl.pallas_call(functools.partial(forward_kernel, causal), grid=(pairs, se...  24.1 us
  transfers between devices with their start and end apart: 63, of which 20 were waited for; matrix products, arithmetic and copies ran while one was open for 22% of the time, Pallas kernels for 26%

profile of v3, /device:TPU:0, one launch (start us, length us, event | category | flops | bytes accessed | tf_op | source)
XLA Modules:
  0.0 443.7 jit_solution(12334931334487176742)
XLA Ops:
  16.4 5.1 %collective-permute-start.2 = (bf16[144,1536]{1,0:T(8,128)(2,1)S(1)}, bf16[144,1536]{1,0:T(8,128)(2,1)S(1)}, u32[]{:S(2)}, u32[]{:S(2)}) collective-permute-start(bf16[144,1536]{1,0:T(8,128)(2,1)S(1)} %fusion.95.refs_0_), channel_id=1, source_target_pairs={{0,24},{8,0},{16,8},{24,16},{1,25},{9,1},{17,9},{25,17},{2,26},{10... | collective-permute-start | bytes 1327112 | tf_op jit(solution)/shard_map/ppermute | solution.py:429
  22.5 4.4 collective-permute-start.3
  33.1 19.8 %collective-permute-done.refs_1_ = bf16[144,1536]{1,0:T(8,128)(2,1)S(1)} collective-permute-done((bf16[144,1536]{1,0:T(8,128)(2,1)S(1)}, bf16[144,1536]{1,0:T(8,128)(2,1)S(1)}, u32[]{:S(2)}, u32[]{:S(2)}) %collective-permute-start) | collective-permute-done | bytes 442400 | tf_op jit(solution)/shard_map/ppermute | solution.py:429
  52.9 16.9 %collective-permute-done.1.refs_2_ = bf16[144,1536]{1,0:T(8,128)(2,1)S(1)} collective-permute-done((bf16[144,1536]{1,0:T(8,128)(2,1)S(1)}, bf16[144,1536]{1,0:T(8,128)(2,1)S(1)}, u32[]{:S(2)}, u32[]{:S(2)}) %collective-permute-start.1) | collective-permute-done | bytes 442400 | tf_op jit(solution)/shard_map/ppermute | solution.py:429
  101.2 4.0 convert_bitcast_fusion.1.refs_5_.refs_6_
  105.2 7.5 %attend_forward.4 = (bf16[1,256,512]{2,1,0:T(8,128)(2,1)S(1)}, f32[1,4,8,256]{3,2,1,0:T(8,128)S(1)}) custom-call(s32[1,1]{1,0:T(1,128)} %bitcast.1.refs_0_, f32[4,8,1280]{2,1,0:T(8,128)S(1)} %concatenate.65.refs_1_, s32[1,1,256]{2,1,0:T(1,128)S(1)} %get-tuple-element.511.refs_2_.refs_0_, s32[1,1024,1]{2,1,0:T(8,128)S(1)} %copy-done.22, ...), custom_call_target="tpu_custom_call" | custom-call | flops 1 | bytes 1 | tf_op jit(solution)/shard_map/attend_forward/pallas_call | solution.py:233
  117.5 4.6 %convert_bitcast_fusion.refs_5_.refs_6_ = bf16[1,1024,1024]{2,1,0:T(8,128)(2,1)S(1)} fusion(bf16[1024,1024]{1,0:T(8,128)(2,1)} %get-tuple-element.338.refs_2_.refs_4_, bf16[1024,1536]{1,0:T(8,128)(2,1)} %bitcast.310), kind=kOutput, calls=%fused_computation.18 | convolution fusion | flops 2148532224 | bytes 6291456 | tf_op jit(solution)/shard_map/dot_general | solution.py:21
  123.9 7.4 %attend_forward.5 = (bf16[1,256,512]{2,1,0:T(8,128)(2,1)S(1)}, f32[1,4,8,256]{3,2,1,0:T(8,128)S(1)}) custom-call(s32[1,1]{1,0:T(1,128)} %bitcast.1.refs_0_, f32[4,8,1280]{2,1,0:T(8,128)S(1)} %concatenate.65.refs_1_, s32[1,1,256]{2,1,0:T(1,128)S(1)} %get-tuple-element.512.refs_2_.refs_0_, s32[1,1024,1]{2,1,0:T(8,128)S(1)} %copy.101.refs_3_, ...), custom_call_target="tpu_custom_call" | custom-call | flops 1 | bytes 1 | tf_op jit(solution)/shard_map/attend_forward/pallas_call | solution.py:233
  141.3 3.4 assemble.7
  153.2 4.5 %attend_forward.6 = (bf16[1,256,512]{2,1,0:T(8,128)(2,1)S(1)}, f32[1,4,8,256]{3,2,1,0:T(8,128)S(1)}) custom-call(s32[1,1,256]{2,1,0:T(1,128)S(1)} %get-tuple-element.511.refs_2_.refs_0_, s32[1,512,1]{2,1,0:T(8,128)S(1)} %copy-done.48, bf16[1,256,512]{2,1,0:T(8,128)(2,1)S(1)} %fusion.57.refs_2_, bf16[1,512,1024]{2,1,0:T(8,128)(2,1)S(1)} %bitcast.322, ...), custom_call_target="tpu_custom_call" | custom-call | flops 1 | bytes 1 | tf_op jit(solution)/shard_map/attend_forward/pallas_call | solution.py:233
  160.9 4.7 %attend_forward.7 = (bf16[1,256,512]{2,1,0:T(8,128)(2,1)S(1)}, f32[1,4,8,256]{3,2,1,0:T(8,128)S(1)}) custom-call(s32[1,1,256]{2,1,0:T(1,128)S(1)} %get-tuple-element.512.refs_2_.refs_0_, s32[1,512,1]{2,1,0:T(8,128)S(1)} %copy-done.46, bf16[1,256,512]{2,1,0:T(8,128)(2,1)S(1)} %fusion.58.refs_2_, bf16[1,512,1024]{2,1,0:T(8,128)(2,1)S(1)} %bitcast.318, ...), custom_call_target="tpu_custom_call" | custom-call | flops 1 | bytes 1 | tf_op jit(solution)/shard_map/attend_forward/pallas_call | solution.py:233
  174.5 4.5 %fusion.114 = f32[256,2816]{1,0:T(8,128)S(1)} fusion(bf16[256,1024]{1,0:T(8,128)(2,1)S(1)} %multiply_convert_fusion.5.refs_0_.refs_2_, bf16[1024,2816]{1,0:T(8,128)(2,1)} %all-gather.5.cloned.1.call-done), kind=kOutput, calls=%fused_computation.274 | convolution fusion | flops 1476395008 | bytes 9175040 | tf_op jit(solution)/shard_map/dot_general | solution.py:21
  193.0 4.4 collective-permute-done.25
  198.2 7.5 %weight_gradients.4 = bf16[1024,4224]{1,0:T(8,128)(2,1)S(1)} custom-call(bf16[256,1024]{1,0:T(8,128)(2,1)S(1)} %copy-done.29, bf16[256,1024]{1,0:T(8,128)(2,1)S(1)} %multiply_convert_fusion.4.refs_1_.refs_3_, bf16[256,1024]{1,0:T(8,128)(2,1)S(1)} %copy-done.29, bf16[256,1024]{1,0:T(8,128)(2,1)S(1)} %multiply_convert_fusion.4.refs_1_.refs_3_, ...), custom_call_target="tpu_custom_call" | custom-call | flops 1 | bytes 1 | tf_op jit(solution)/shard_map/weight_gradients/pallas_call | solution.py:358
  205.8 3.3 copy-done.2
  216.2 5.6 %attend_backward.4 = (bf16[1,256,512]{2,1,0:T(8,128)(2,1)S(1)}, bf16[1,512,512]{2,1,0:T(8,128)(2,1)S(1)}, bf16[1,512,512]{2,1,0:T(8,128)(2,1)S(1)}) custom-call(s32[1,1,256]{2,1,0:T(1,128)S(1)} %get-tuple-element.511.refs_2_.refs_0_, s32[1,512,1]{2,1,0:T(8,128)S(1)} %copy-done.49, bf16[1,256,512]{2,1,0:T(8,128)(2,1)S(1)} %copy-done.74, ...), custom_call_target="tpu_custom_call" | custom-call | flops 1 | bytes 1 | tf_op jit(solution)/shard_map/attend_backward/pallas_call | solution.py:269
  227.2 5.8 %attend_backward.5 = (bf16[1,256,512]{2,1,0:T(8,128)(2,1)S(1)}, bf16[1,512,512]{2,1,0:T(8,128)(2,1)S(1)}, bf16[1,512,512]{2,1,0:T(8,128)(2,1)S(1)}) custom-call(s32[1,1,256]{2,1,0:T(1,128)S(1)} %get-tuple-element.512.refs_2_.refs_0_, s32[1,512,1]{2,1,0:T(8,128)S(1)} %copy-done.47, bf16[1,256,512]{2,1,0:T(8,128)(2,1)S(1)} %copy-done.72, ...), custom_call_target="tpu_custom_call" | custom-call | flops 1 | bytes 1 | tf_op jit(solution)/shard_map/attend_backward/pallas_call | solution.py:269
  239.7 6.4 %weight_gradients.5 = (bf16[512,2048]{1,0:T(8,128)(2,1)}, bf16[512,2048]{1,0:T(8,128)(2,1)S(1)}) custom-call(s32[1,1]{1,0:T(1,128)} %bitcast.58.refs_0_, bf16[256,1024]{1,0:T(8,128)(2,1)S(1)} %copy-done.64, bf16[256,1024]{1,0:T(8,128)(2,1)S(1)} %copy-done.66, bf16[512,1024]{1,0:T(8,128)(2,1)S(1)} %bitcast.347, bf16[512,1024]{1,0:T(8,128)(2,1)S(1)} %bitcast.345, ...), custom_call_target="tpu_custom_call" | custom-call | flops 1 | bytes 1 | tf_op jit(solution)/shard_map/weight_gradients/pallas_call | solution.py:358
  254.6 13.0 %attend_backward.6 = (bf16[1,256,512]{2,1,0:T(8,128)(2,1)S(1)}, bf16[1,1024,512]{2,1,0:T(8,128)(2,1)S(1)}, bf16[1,1024,512]{2,1,0:T(8,128)(2,1)S(1)}, f32[4,8,1280]{2,1,0:T(8,128)S(1)}) custom-call(s32[1,1]{1,0:T(1,128)} %bitcast.1.refs_0_, f32[4,8,1280]{2,1,0:T(8,128)S(1)} %concatenate.65.refs_1_, s32[1,1,256]{2,1,0:T(1,128)S(1)} %get-tuple-element.511.refs_2_.refs_0_, ...), custom_call_target="tpu_custom_call" | custom-call | flops 1 | bytes 1 | tf_op jit(solution)/shard_map/attend_backward/pallas_call | solution.py:269
  280.1 12.7 %attend_backward.7 = (bf16[1,256,512]{2,1,0:T(8,128)(2,1)S(1)}, bf16[1,1024,512]{2,1,0:T(8,128)(2,1)S(1)}, bf16[1,1024,512]{2,1,0:T(8,128)(2,1)S(1)}, f32[4,8,1280]{2,1,0:T(8,128)S(1)}) custom-call(s32[1,1]{1,0:T(1,128)} %bitcast.1.refs_0_, f32[4,8,1280]{2,1,0:T(8,128)S(1)} %concatenate.65.refs_1_, s32[1,1,256]{2,1,0:T(1,128)S(1)} %get-tuple-element.512.refs_2_.refs_0_, ...), custom_call_target="tpu_custom_call" | custom-call | flops 1 | bytes 1 | tf_op jit(solution)/shard_map/attend_backward/pallas_call | solution.py:269
  293.0 7.1 %collective-permute-done.32.moved_ref = bf16[256,1024]{1,0:T(8,128)(2,1)S(1)} collective-permute-done((bf16[256,1024]{1,0:T(8,128)(2,1)S(1)}, bf16[256,1024]{1,0:T(8,128)(2,1)S(1)}, u32[]{:S(2)}, u32[]{:S(2)}) %collective-permute-start.32) | collective-permute-done | bytes 524320 | tf_op jit(solution)/shard_map/ppermute | solution.py:424
  307.4 3.2 weight_gradients.6
  310.6 8.0 %weight_gradients.7 = (bf16[512,1024]{1,0:T(8,128)(2,1)}, bf16[512,1024]{1,0:T(8,128)(2,1)S(1)}) custom-call(s32[1,1]{1,0:T(1,128)} %bitcast.58.refs_0_, bf16[1024,1024]{1,0:T(8,128)(2,1)S(1)} %copy-done.14, bf16[1024,1024]{1,0:T(8,128)(2,1)S(1)} %copy-done.15, bf16[1024,1024]{1,0:T(8,128)(2,1)S(1)} %copy-done.14, bf16[1024,1024]{1,0:T(8,128)(2,1)S(1)} %copy-done.15, ...), custom_call_target="tpu_custom_call" | custom-call | flops 1 | bytes 1 | tf_op jit(solution)/shard_map/weight_gradients/pallas_call | solution.py:358
  320.5 4.7 %collective-permute-done.35.moved_ref = bf16[256,1024]{1,0:T(8,128)(2,1)S(1)} collective-permute-done((bf16[256,1024]{1,0:T(8,128)(2,1)S(1)}, bf16[256,1024]{1,0:T(8,128)(2,1)S(1)}, u32[]{:S(2)}, u32[]{:S(2)}) %collective-permute-start.35) | collective-permute-done | bytes 524320 | tf_op jit(solution)/shard_map/ppermute | solution.py:424
  340.5 3.9 split_sum.10
  356.1 4.2 collective-permute-done.41
  373.5 8.8 %collective-permute-done.43 = bf16[2,128,1024]{2,1,0:T(8,128)(2,1)} collective-permute-done((bf16[2,128,1024]{2,1,0:T(8,128)(2,1)}, bf16[2,128,1024]{2,1,0:T(8,128)(2,1)}, u32[]{:S(2)}, u32[]{:S(2)}) %collective-permute-start.43) | collective-permute-done | bytes 524320 | tf_op jit(solution)/shard_map/ppermute | solution.py:634
  384.1 9.8 %collective-permute-done.47 = bf16[2,80,1024]{2,1,0:T(8,128)(2,1)S(1)} collective-permute-done((bf16[2,80,1024]{2,1,0:T(8,128)(2,1)S(1)}, bf16[2,80,1024]{2,1,0:T(8,128)(2,1)S(1)}, u32[]{:S(2)}, u32[]{:S(2)}) %collective-permute-start.47) | collective-permute-done | bytes 327712 | tf_op jit(solution)/shard_map/ppermute | solution.py:634
  394.5 7.2 %collective-permute-done.46 = bf16[1,128,2048]{2,1,0:T(8,128)(2,1)S(1)} collective-permute-done((bf16[1,128,2048]{2,1,0:T(8,128)(2,1)S(1)}, bf16[1,128,2048]{2,1,0:T(8,128)(2,1)S(1)}, u32[]{:S(2)}, u32[]{:S(2)}) %collective-permute-start.46) | collective-permute-done | bytes 524320 | tf_op jit(solution)/shard_map/ppermute | solution.py:634
  405.8 5.4 %collective-permute-done.49.refs_1_ = bf16[1,64,2048]{2,1,0:T(8,128)(2,1)S(1)} collective-permute-done((bf16[1,64,2048]{2,1,0:T(8,128)(2,1)S(1)}, bf16[1,64,2048]{2,1,0:T(8,128)(2,1)S(1)}, u32[]{:S(2)}, u32[]{:S(2)}) %collective-permute-start.49) | collective-permute-done | bytes 262176 | tf_op jit(solution)/shard_map/ppermute | solution.py:424
  413.4 5.9 %collective-permute-done.54.refs_1_ = bf16[1,80,1024]{2,1,0:T(8,128)(2,1)S(1)} collective-permute-done((bf16[1,80,1024]{2,1,0:T(8,128)(2,1)S(1)}, bf16[1,80,1024]{2,1,0:T(8,128)(2,1)S(1)}, u32[]{:S(2)}, u32[]{:S(2)}) %collective-permute-start.54) | collective-permute-done | bytes 163872 | tf_op jit(solution)/shard_map/ppermute | solution.py:634
  420.1 3.5 finish.3
  (566 shorter events, 209.8 us)
Async XLA Ops:
  7.2 106.9 %all-gather.3.cloned.1.call-start = ((), (), s32[]{:S(2)}) async-start(), calls=%async_computation.1 | async-start | bytes 5570560 | tf_op jit(solution)/shard_map/all_gather | solution.py:458
  16.4 158.1 %all-gather.5.cloned.1.call-start = ((), (), s32[]{:S(2)}) async-start(), calls=%async_computation.2 | async-start | bytes 6127616 | tf_op jit(solution)/shard_map/all_gather | solution.py:458
  16.4 53.4 %collective-permute-start.2 = (bf16[144,1536]{1,0:T(8,128)(2,1)S(1)}, bf16[144,1536]{1,0:T(8,128)(2,1)S(1)}, u32[]{:S(2)}, u32[]{:S(2)}) collective-permute-start(bf16[144,1536]{1,0:T(8,128)(2,1)S(1)} %fusion.95.refs_0_), channel_id=1, source_target_pairs={{0,24},{8,0},{16,8},{24,16},{1,25},{9,1},{17,9},{25,17},{2,26},{10... | collective-permute-start | bytes 1327112 | tf_op jit(solution)/shard_map/ppermute | solution.py:429
  21.5 31.4 %collective-permute-start = (bf16[144,1536]{1,0:T(8,128)(2,1)S(1)}, bf16[144,1536]{1,0:T(8,128)(2,1)S(1)}, u32[]{:S(2)}, u32[]{:S(2)}) collective-permute-start(bf16[144,1536]{1,0:T(8,128)(2,1)S(1)} %fusion.95.refs_0_), channel_id=1, source_target_pairs={{0,8},{8,16},{16,24},{24,0},{1,9},{9,17},{17,25},{25,1},{2,10},{10... | collective-permute-start | bytes 1327112 | tf_op jit(solution)/shard_map/ppermute | solution.py:429
  21.5 48.3 %collective-permute-start.1 = (bf16[144,1536]{1,0:T(8,128)(2,1)S(1)}, bf16[144,1536]{1,0:T(8,128)(2,1)S(1)}, u32[]{:S(2)}, u32[]{:S(2)}) collective-permute-start(bf16[144,1536]{1,0:T(8,128)(2,1)S(1)} %fusion.95.refs_0_), channel_id=1, source_target_pairs={{0,16},{8,24},{16,0},{24,8},{1,17},{9,25},{17,1},{25,9},{2,18},{10... | collective-permute-start | bytes 1327112 | tf_op jit(solution)/shard_map/ppermute | solution.py:429
  22.5 50.2 %collective-permute-start.6 = (bf16[144,1536]{1,0:T(8,128)(2,1)S(1)}, bf16[144,1536]{1,0:T(8,128)(2,1)}, u32[]{:S(2)}, u32[]{:S(2)}) collective-permute-start(bf16[144,1536]{1,0:T(8,128)(2,1)S(1)} %fusion.95.refs_0_), channel_id=1, source_target_pairs={{0,2},{2,0},{4,6},{6,4},{1,3},{3,1},{5,7},{7,5},{8,10},{10,8},{12,... | collective-permute-start | bytes 1327112 | tf_op jit(solution)/shard_map/ppermute | solution.py:414
  22.5 48.0 %collective-permute-start.3 = (bf16[2,256,1024]{2,1,0:T(8,128)(2,1)S(1)}, bf16[2,256,1024]{2,1,0:T(8,128)(2,1)}, u32[]{:S(2)}, u32[]{:S(2)}) collective-permute-start(bf16[2,256,1024]{2,1,0:T(8,128)(2,1)S(1)} %copy-done.8), channel_id=1, source_target_pairs={{0,4},{2,6},{1,5},{3,7},{8,12},{10,14},{9,13},{11,15},{16,20},{18,... | collective-permute-start | bytes 3145736 | tf_op jit(solution)/shard_map/ppermute | solution.py:424
  28.6 306.3 %reduce-scatter.2.cloned.1.call-start = ((), (), s32[]{:S(2)}) async-start(), calls=%async_computation.3 | async-start | bytes 9191424 | tf_op jit(solution)/shard_map/reduce_scatter | solution.py:1094
  93.7 41.0 %collective-permute-start.14 = (bf16[128,1408]{1,0:T(8,128)(2,1)}, bf16[128,1408]{1,0:T(8,128)(2,1)}, u32[]{:S(2)}, u32[]{:S(2)}) collective-permute-start(bf16[128,1408]{1,0:T(8,128)(2,1)} %dynamic-slice_bitcast_fusion.8.refs_0_), channel_id=1, source_target_pairs={{0,8},{8,16},{16,24},{24,0},{1,9},{9,17},{17,25},{25,1},{2,10},{10... | collective-permute-start | bytes 1081352 | tf_op jit(solution)/shard_map/ppermute | solution.py:429
  94.8 39.9 %collective-permute-start.15 = (bf16[128,1408]{1,0:T(8,128)(2,1)}, bf16[128,1408]{1,0:T(8,128)(2,1)}, u32[]{:S(2)}, u32[]{:S(2)}) collective-permute-start(bf16[128,1408]{1,0:T(8,128)(2,1)} %dynamic-slice_bitcast_fusion.8.refs_0_), channel_id=1, source_target_pairs={{0,16},{8,24},{16,0},{24,8},{1,17},{9,25},{17,1},{25,9},{2,18},{10... | collective-permute-start | bytes 1081352 | tf_op jit(solution)/shard_map/ppermute | solution.py:429
  97.9 36.8 %collective-permute-start.16 = (bf16[128,1408]{1,0:T(8,128)(2,1)}, bf16[128,1408]{1,0:T(8,128)(2,1)}, u32[]{:S(2)}, u32[]{:S(2)}) collective-permute-start(bf16[128,1408]{1,0:T(8,128)(2,1)} %dynamic-slice_bitcast_fusion.8.refs_0_), channel_id=1, source_target_pairs={{0,24},{8,0},{16,8},{24,16},{1,25},{9,1},{17,9},{25,17},{2,26},{10... | collective-permute-start | bytes 1081352 | tf_op jit(solution)/shard_map/ppermute | solution.py:429
  97.9 36.9 %collective-permute-start.11 = (bf16[2,128,1024]{2,1,0:T(8,128)(2,1)}, bf16[2,128,1024]{2,1,0:T(8,128)(2,1)}, u32[]{:S(2)}, u32[]{:S(2)}) collective-permute-start(bf16[2,128,1024]{2,1,0:T(8,128)(2,1)} %refs_0_.1), channel_id=1, source_target_pairs={{0,4},{2,6},{4,0},{6,2},{1,5},{3,7},{5,1},{7,3},{8,12},{10,14},{12... | collective-permute-start | bytes 1572872 | tf_op jit(solution)/shard_map/ppermute | solution.py:424
  115.9 15.3 %collective-permute-start.10 = (bf16[256,1024]{1,0:T(8,128)(2,1)S(1)}, bf16[256,1024]{1,0:T(8,128)(2,1)S(1)}, u32[]{:S(2)}, u32[]{:S(2)}) collective-permute-start(bf16[256,1024]{1,0:T(8,128)(2,1)S(1)} %convolution_convert_fusion.5), channel_id=1, source_target_pairs={{0,1},{1,0},{2,3},{3,2},{4,5},{5,4},{6,7},{7,6},{8,9},{9,8},{10,11... | collective-permute-start | bytes 1572872 | tf_op jit(solution)/shard_map/ppermute | solution.py:937
  140.7 17.0 %collective-permute-start.21 = (bf16[256,1024]{1,0:T(8,128)(2,1)S(1)}, bf16[256,1024]{1,0:T(8,128)(2,1)S(1)}, u32[]{:S(2)}, u32[]{:S(2)}) collective-permute-start(bf16[256,1024]{1,0:T(8,128)(2,1)S(1)} %copy-done.119), channel_id=1, source_target_pairs={{0,1},{1,0},{2,3},{3,2},{4,5},{5,4},{6,7},{7,6},{8,9},{9,8},{10,11... | collective-permute-start | bytes 1572872 | tf_op jit(solution)/shard_map/ppermute | solution.py:937
  166.9 18.4 %collective-permute-start.23 = (bf16[256,1024]{1,0:T(8,128)(2,1)}, bf16[256,1024]{1,0:T(8,128)(2,1)}, u32[]{:S(2)}, u32[]{:S(2)}) collective-permute-start(bf16[256,1024]{1,0:T(8,128)(2,1)} %convolution_convert_fusion.2), channel_id=1, source_target_pairs={{0,1},{1,0},{2,3},{3,2},{4,5},{5,4},{6,7},{7,6},{8,9},{9,8},{10,11... | collective-permute-start | bytes 1572872 | tf_op jit(solution)/shard_map/ppermute | solution.py:937
  251.4 18.3 %collective-permute-start.29 = (bf16[256,1024]{1,0:T(8,128)(2,1)S(1)}, bf16[256,1024]{1,0:T(8,128)(2,1)S(1)}, u32[]{:S(2)}, u32[]{:S(2)}) collective-permute-start(bf16[256,1024]{1,0:T(8,128)(2,1)S(1)} %get-tuple-element.476), channel_id=1, source_target_pairs={{0,4},{2,6},{4,0},{6,2},{1,5},{3,7},{5,1},{7,3},{8,12},{10,14},{12... | collective-permute-start | bytes 1572872 | tf_op jit(solution)/shard_map/ppermute | solution.py:424
  252.2 19.5 %collective-permute-start.31 = (bf16[256,1024]{1,0:T(8,128)(2,1)S(1)}, bf16[256,1024]{1,0:T(8,128)(2,1)S(1)}, u32[]{:S(2)}, u32[]{:S(2)}) collective-permute-start(bf16[256,1024]{1,0:T(8,128)(2,1)S(1)} %convolution_convert_fusion), channel_id=1, source_target_pairs={{0,1},{1,0},{2,3},{3,2},{4,5},{5,4},{6,7},{7,6},{8,9},{9,8},{10,11... | collective-permute-start | bytes 1572872 | tf_op jit(solution)/shard_map/ppermute | solution.py:937
  277.2 15.7 %collective-permute-start.33 = (bf16[256,1024]{1,0:T(8,128)(2,1)S(1)}, bf16[256,1024]{1,0:T(8,128)(2,1)S(1)}, u32[]{:S(2)}, u32[]{:S(2)}) collective-permute-start(bf16[256,1024]{1,0:T(8,128)(2,1)S(1)} %convolution_convert_fusion.6), channel_id=1, source_target_pairs={{0,1},{1,0},{2,3},{3,2},{4,5},{5,4},{6,7},{7,6},{8,9},{9,8},{10,11... | collective-permute-start | bytes 1572872 | tf_op jit(solution)/shard_map/ppermute | solution.py:937
  278.8 21.3 %collective-permute-start.32 = (bf16[256,1024]{1,0:T(8,128)(2,1)S(1)}, bf16[256,1024]{1,0:T(8,128)(2,1)S(1)}, u32[]{:S(2)}, u32[]{:S(2)}) collective-permute-start(bf16[256,1024]{1,0:T(8,128)(2,1)S(1)} %get-tuple-element.474), channel_id=1, source_target_pairs={{4,0},{6,2},{5,1},{7,3},{12,8},{14,10},{13,9},{15,11},{20,16},{22,... | collective-permute-start | bytes 1572872 | tf_op jit(solution)/shard_map/ppermute | solution.py:424
  300.3 34.6 %collective-permute-start.39 = (bf16[512,2048]{1,0:T(8,128)(2,1)}, bf16[512,2048]{1,0:T(8,128)(2,1)}, u32[]{:S(2)}, u32[]{:S(2)}) collective-permute-start(bf16[512,2048]{1,0:T(8,128)(2,1)} %get-tuple-element.298), channel_id=1, source_target_pairs={{0,2},{2,0},{4,6},{6,4},{1,3},{3,1},{5,7},{7,5},{8,10},{10,8},{12,... | collective-permute-start | bytes 6291464 | tf_op jit(solution)/shard_map/ppermute | solution.py:414
  303.1 16.7 %collective-permute-start.36 = (bf16[256,1024]{1,0:T(8,128)(2,1)S(1)}, bf16[256,1024]{1,0:T(8,128)(2,1)S(1)}, u32[]{:S(2)}, u32[]{:S(2)}) collective-permute-start(bf16[256,1024]{1,0:T(8,128)(2,1)S(1)} %project_end.2.part_ref), channel_id=1, source_target_pairs={{0,1},{1,0},{2,3},{3,2},{4,5},{5,4},{6,7},{7,6},{8,9},{9,8},{10,11... | collective-permute-start | bytes 1572872 | tf_op jit(solution)/shard_map/ppermute | solution.py:937
  305.9 19.3 %collective-permute-start.35 = (bf16[256,1024]{1,0:T(8,128)(2,1)S(1)}, bf16[256,1024]{1,0:T(8,128)(2,1)S(1)}, u32[]{:S(2)}, u32[]{:S(2)}) collective-permute-start(bf16[256,1024]{1,0:T(8,128)(2,1)S(1)} %get-tuple-element.472), channel_id=1, source_target_pairs={{4,0},{6,2},{5,1},{7,3},{12,8},{14,10},{13,9},{15,11},{20,16},{22,... | collective-permute-start | bytes 1572872 | tf_op jit(solution)/shard_map/ppermute | solution.py:424
  326.0 21.2 %collective-permute-start.37 = (bf16[512,1024]{1,0:T(8,128)(2,1)}, bf16[512,1024]{1,0:T(8,128)(2,1)}, u32[]{:S(2)}, u32[]{:S(2)}) collective-permute-start(bf16[512,1024]{1,0:T(8,128)(2,1)} %get-tuple-element.336), channel_id=1, source_target_pairs={{0,2},{2,0},{4,6},{6,4},{1,3},{3,1},{5,7},{7,5},{8,10},{10,8},{12,... | collective-permute-start | bytes 3145736 | tf_op jit(solution)/shard_map/ppermute | solution.py:414
  333.5 27.6 %collective-permute-start.40 = (bf16[256,1024]{1,0:T(8,128)(2,1)}, bf16[256,1024]{1,0:T(8,128)(2,1)}, u32[]{:S(2)}, u32[]{:S(2)}) collective-permute-start(bf16[256,1024]{1,0:T(8,128)(2,1)} %project_end.3.part_ref), channel_id=1, source_target_pairs={{0,1},{1,0},{2,3},{3,2},{4,5},{5,4},{6,7},{7,6},{8,9},{9,8},{10,11... | collective-permute-start | bytes 1572872 | tf_op jit(solution)/shard_map/ppermute | solution.py:937
  335.0 38.1 %collective-permute-start.51 = (bf16[64,4224]{1,0:T(8,128)(2,1)}, bf16[64,4224]{1,0:T(8,128)(2,1)}, u32[]{:S(2)}, u32[]{:S(2)}) collective-permute-start(bf16[64,4224]{1,0:T(8,128)(2,1)} %reduce-scatter.2.cloned.1.call-done.refs_0_), channel_id=1, source_target_pairs={{0,4},{2,6},{4,0},{6,2},{1,5},{3,7},{5,1},{7,3},{8,12},{10,14},{12... | collective-permute-start | bytes 1622024 | tf_op jit(solution)/shard_map/ppermute | solution.py:424
  339.0 29.2 %collective-permute-start.44 = (bf16[2,128,2048]{2,1,0:T(8,128)(2,1)}, bf16[2,128,2048]{2,1,0:T(8,128)(2,1)S(1)}, u32[]{:S(2)}, u32[]{:S(2)}) collective-permute-start(bf16[2,128,2048]{2,1,0:T(8,128)(2,1)} %get-tuple-element.354), channel_id=1, source_target_pairs={{0,8},{8,0},{16,24},{24,16},{1,9},{9,1},{17,25},{25,17},{2,10},{10... | collective-permute-start | bytes 3145736 | tf_op jit(solution)/shard_map/ppermute | solution.py:634
  349.8 32.5 %collective-permute-start.43 = (bf16[2,128,1024]{2,1,0:T(8,128)(2,1)}, bf16[2,128,1024]{2,1,0:T(8,128)(2,1)}, u32[]{:S(2)}, u32[]{:S(2)}) collective-permute-start(bf16[2,128,1024]{2,1,0:T(8,128)(2,1)} %get-tuple-element.362), channel_id=1, source_target_pairs={{0,8},{8,0},{16,24},{24,16},{1,9},{9,1},{17,25},{25,17},{2,10},{10... | collective-permute-start | bytes 1572872 | tf_op jit(solution)/shard_map/ppermute | solution.py:634
  369.1 32.7 %collective-permute-start.46 = (bf16[1,128,2048]{2,1,0:T(8,128)(2,1)S(1)}, bf16[1,128,2048]{2,1,0:T(8,128)(2,1)S(1)}, u32[]{:S(2)}, u32[]{:S(2)}) collective-permute-start(bf16[1,128,2048]{2,1,0:T(8,128)(2,1)S(1)} %get-tuple-element.387), channel_id=1, source_target_pairs={{0,16},{8,24},{16,0},{24,8},{1,17},{9,25},{17,1},{25,9},{2,18},{10... | collective-permute-start | bytes 1572872 | tf_op jit(solution)/shard_map/ppermute | solution.py:634
  371.5 22.4 %collective-permute-start.47 = (bf16[2,80,1024]{2,1,0:T(8,128)(2,1)S(1)}, bf16[2,80,1024]{2,1,0:T(8,128)(2,1)S(1)}, u32[]{:S(2)}, u32[]{:S(2)}) collective-permute-start(bf16[2,80,1024]{2,1,0:T(8,128)(2,1)S(1)} %get-tuple-element.383), channel_id=1, source_target_pairs={{0,8},{8,0},{16,24},{24,16},{1,9},{9,1},{17,25},{25,17},{2,10},{10... | collective-permute-start | bytes 983048 | tf_op jit(solution)/shard_map/ppermute | solution.py:634
  373.0 47.0 %collective-permute-start.52 = (bf16[64,4224]{1,0:T(8,128)(2,1)S(1)}, bf16[64,4224]{1,0:T(8,128)(2,1)S(1)}, u32[]{:S(2)}, u32[]{:S(2)}) collective-permute-start(bf16[64,4224]{1,0:T(8,128)(2,1)S(1)} %copy-done.85), channel_id=1, source_target_pairs={{0,2},{2,0},{4,6},{6,4},{1,3},{3,1},{5,7},{7,5},{8,10},{10,8},{12,... | collective-permute-start | bytes 1622024 | tf_op jit(solution)/shard_map/ppermute | solution.py:414
  373.0 47.0 %collective-permute-start.53 = (bf16[64,4224]{1,0:T(8,128)(2,1)}, bf16[64,4224]{1,0:T(8,128)(2,1)S(1)}, u32[]{:S(2)}, u32[]{:S(2)}) collective-permute-start(bf16[64,4224]{1,0:T(8,128)(2,1)} %collective-permute-done.51.refs_1_), channel_id=1, source_target_pairs={{0,2},{2,0},{4,6},{6,4},{1,3},{3,1},{5,7},{7,5},{8,10},{10,8},{12,... | collective-permute-start | bytes 1622024 | tf_op jit(solution)/shard_map/ppermute | solution.py:414
  384.0 21.2 %collective-permute-start.45 = (bf16[1,128,1024]{2,1,0:T(8,128)(2,1)S(1)}, bf16[1,128,1024]{2,1,0:T(8,128)(2,1)S(1)}, u32[]{:S(2)}, u32[]{:S(2)}) collective-permute-start(bf16[1,128,1024]{2,1,0:T(8,128)(2,1)S(1)} %get-tuple-element.391), channel_id=1, source_target_pairs={{0,16},{8,24},{16,0},{24,8},{1,17},{9,25},{17,1},{25,9},{2,18},{10... | collective-permute-start | bytes 786440 | tf_op jit(solution)/shard_map/ppermute | solution.py:634
  (165 other events, 979.9 us)
Sparse Core Ops, SparseCore 0:
  16.5 81.8 all-gather.2
  101.3 72.5 all-gather.4
  209.3 120.9 reduce-scatter.1
